TPU v7x, 32 devices: a whole 2x2x4 slice. The times are simulated.
32 devices in a mesh: fsdp: 4 (over x, core), seq: 8 (over z, y).
Axes of the slice: x: 2, y: 2, z: 4, core: 2. Of those that a mesh axis runs over, the one named last changes fastest.
Arguments:
- tokens: bfloat16 [4096, 2048], P(('fsdp', 'seq')), may hold values from -6 to 6
- cotangent: bfloat16 [4096, 2048], P(('fsdp', 'seq')), may hold values from -6 to 6
- expert_ids: int32 [4096, 8], P(('fsdp', 'seq')), may hold values from 0 to 15, all different within a row; in each aligned block of 128 rows (0 to 127, 128 to 255, ...) at most 85 rows name the same one
- attn_gain: bfloat16 [2048], P(('fsdp', 'seq')), may hold values from 0.5 to 1.5
- w_query: bfloat16 [2048, 4096], P(('fsdp', 'seq')), may hold values from -0.125 to 0.125
- w_key: bfloat16 [2048, 512], P(('fsdp', 'seq')), may hold values from -0.125 to 0.125
- w_value: bfloat16 [2048, 512], P(('fsdp', 'seq')), may hold values from -0.125 to 0.125
- query_gain: bfloat16 [128], P(('fsdp', 'seq')), may hold values from 0.5 to 1.5
- key_gain: bfloat16 [128], P(('fsdp', 'seq')), may hold values from 0.5 to 1.5
- w_output: bfloat16 [4096, 2048], P(('fsdp', 'seq')), may hold values from -0.75 to 0.75
- mlp_gain: bfloat16 [2048], P(('fsdp', 'seq')), may hold values from 0.5 to 1.5
- w_router: bfloat16 [2048, 16], P(('fsdp', 'seq')), may hold values from -0.0625 to 0.0625
- w_gate: bfloat16 [16, 2048, 768], P('seq', 'fsdp'), may hold values from -0.125 to 0.125
- w_up: bfloat16 [16, 2048, 768], P('seq', 'fsdp'), may hold values from -0.125 to 0.125
- w_down: bfloat16 [16, 768, 2048], P('seq', None, 'fsdp'), may hold values from -0.875 to 0.875
Outputs:
- layer_out: bfloat16 [4096, 2048], P(('fsdp', 'seq'))
- grad_tokens: bfloat16 [4096, 2048], P(('fsdp', 'seq'))
- grad_attn_gain: float32 [2048], P(('fsdp', 'seq'))
- grad_query: float32 [2048, 4096], P(('fsdp', 'seq'))
- grad_key: float32 [2048, 512], P(('fsdp', 'seq'))
- grad_value: float32 [2048, 512], P(('fsdp', 'seq'))
- grad_query_gain: float32 [128], P(('fsdp', 'seq'))
- grad_key_gain: float32 [128], P(('fsdp', 'seq'))
- grad_output: float32 [4096, 2048], P(('fsdp', 'seq'))
- grad_mlp_gain: float32 [2048], P(('fsdp', 'seq'))
- grad_router: float32 [2048, 16], P(('fsdp', 'seq'))
- grad_gate: float32 [16, 2048, 768], P('seq', 'fsdp')
- grad_up: float32 [16, 2048, 768], P('seq', 'fsdp')
- grad_down: float32 [16, 768, 2048], P('seq', None, 'fsdp')
Inputs may be any that keep to these rules, and one draw needn't show every extreme that they name: `expert_ids`: each row names 8 different experts. In each aligned block of 128 rows (the rows of one device) no expert is named by more than 85 rows, a bound that some block reaches.
All inputs are finite; a program needn't handle non-finite values.
Results may differ from a plain program's by a relative error of at most 0.025.
Values may be sent and summed in bfloat16 or wider, within the bound.
No kernel may reach another device: no remote copies, remote signals or barrier semaphores. Data moves between devices by JAX's collectives and lax.ppermute only.
A program may use at most 320 MiB of HBM per device.

v0:
```python
import math

import jax
import jax.numpy as jnp
from jax import lax
from jax.sharding import PartitionSpec as P

NORM_EPS = 1e-06
ROPE_BASE = 1000000.0
NEG_LARGE = -1e30


def contract_rows(left_mat, right_mat):
    return lax.dot_general(
        left_mat, right_mat, (((0,), (0,)), ((), ())), preferred_element_type=jnp.float32
    )


def against(left_mat, right_mat):
    return lax.dot_general(
        left_mat, right_mat, (((1,), (1,)), ((), ())), preferred_element_type=jnp.float32
    )


def norm_parts(values):
    row_scale = lax.rsqrt(jnp.mean(values * values, axis=-1, keepdims=True) + NORM_EPS)
    return (values * row_scale, row_scale)


def norm_back(grad_normed, normed, row_scale):
    return row_scale * (
        grad_normed - normed * jnp.mean(grad_normed * normed, axis=-1, keepdims=True)
    )


def rotary_tables(positions, head_size):
    half_size = head_size // 2
    frequency = jnp.exp(
        jnp.arange(half_size, dtype=jnp.float32) * (-2.0 * math.log(ROPE_BASE) / head_size)
    )
    angles = positions[:, None] * frequency[None, :]
    return (jnp.cos(angles)[:, None, :], jnp.sin(angles)[:, None, :])


def rotate(values, cos_table, sine_table):
    half_size = values.shape[-1] // 2
    first_half = values[..., :half_size]
    second_half = values[..., half_size:]
    return jnp.concatenate(
        [
            first_half * cos_table - second_half * sine_table,
            second_half * cos_table + first_half * sine_table,
        ],
        axis=-1,
    )


def unrotate(gradient, cos_table, sine_table):
    half_size = gradient.shape[-1] // 2
    first_half = gradient[..., :half_size]
    second_half = gradient[..., half_size:]
    return jnp.concatenate(
        [
            first_half * cos_table + second_half * sine_table,
            second_half * cos_table - first_half * sine_table,
        ],
        axis=-1,
    )


def on_device(
    tokens,
    cotangent,
    expert_ids,
    attn_gain,
    w_query,
    w_key,
    w_value,
    query_gain,
    key_gain,
    w_output,
    mlp_gain,
    w_router,
    w_gate,
    w_up,
    w_down,
):
    groups = lax.axis_size("seq")
    tok_rows, model_width = tokens.shape
    top_k = expert_ids.shape[1]
    gain_attn, query_w, key_w, value_w, gain_query, gain_key, output_w, gain_mlp, router_w = (
        lax.all_gather(attn_gain, ("fsdp", "seq"), axis=0, tiled=True),
        lax.all_gather(w_query, ("fsdp", "seq"), axis=0, tiled=True),
        lax.all_gather(w_key, ("fsdp", "seq"), axis=0, tiled=True),
        lax.all_gather(w_value, ("fsdp", "seq"), axis=0, tiled=True),
        lax.all_gather(query_gain, ("fsdp", "seq"), axis=0, tiled=True),
        lax.all_gather(key_gain, ("fsdp", "seq"), axis=0, tiled=True),
        lax.all_gather(w_output, ("fsdp", "seq"), axis=0, tiled=True),
        lax.all_gather(mlp_gain, ("fsdp", "seq"), axis=0, tiled=True),
        lax.all_gather(w_router, ("fsdp", "seq"), axis=0, tiled=True),
    )
    gate_w, up_w, down_w = (
        lax.all_gather(w_gate, "fsdp", axis=1, tiled=True),
        lax.all_gather(w_up, "fsdp", axis=1, tiled=True),
        lax.all_gather(w_down, "fsdp", axis=2, tiled=True),
    )
    head_size = gain_query.shape[0]
    heads_all = query_w.shape[1] // head_size
    kv_heads = key_w.shape[1] // head_size
    head_local = heads_all // groups
    copies = groups // kv_heads
    experts_all = router_w.shape[1]
    local_experts = gate_w.shape[0]
    capacity = max(2, tok_rows * top_k * 4 // (3 * experts_all))
    route_rows = tok_rows * top_k
    scale_qk = 1.0 / math.sqrt(head_size)
    positions = (lax.axis_index("seq") * tok_rows + jnp.arange(tok_rows, dtype=jnp.int32)).astype(
        jnp.float32
    )
    cos_table, sine_table = rotary_tables(positions, head_size)
    inputs = tokens.astype(jnp.float32)
    normed_a, scale_a = norm_parts(inputs)
    hidden = (normed_a * gain_attn.astype(jnp.float32)).astype(jnp.bfloat16)
    query_pre = jnp.dot(hidden, query_w, preferred_element_type=jnp.float32).reshape(
        tok_rows, heads_all, head_size
    )
    key_pre = jnp.dot(hidden, key_w, preferred_element_type=jnp.float32).reshape(
        tok_rows, kv_heads, head_size
    )
    value_pre = jnp.dot(hidden, value_w, preferred_element_type=jnp.float32).reshape(
        tok_rows, kv_heads, head_size
    )
    query_hat, query_scale = norm_parts(query_pre)
    key_hat, key_scale = norm_parts(key_pre)
    gain_q = gain_query.astype(jnp.float32)
    gain_k = gain_key.astype(jnp.float32)
    query_send = (
        rotate(query_hat * gain_q, cos_table, sine_table)
        .astype(jnp.bfloat16)
        .reshape(tok_rows, groups, head_local * head_size)
    )
    key_send = jnp.repeat(
        rotate(key_hat * gain_k, cos_table, sine_table).astype(jnp.bfloat16), copies, axis=1
    )
    value_send = jnp.repeat(value_pre.astype(jnp.bfloat16), copies, axis=1)
    query_seq, key_seq, value_seq = (
        lax.all_to_all(query_send, "seq", split_axis=1, concat_axis=0, tiled=True),
        lax.all_to_all(key_send, "seq", split_axis=1, concat_axis=0, tiled=True),
        lax.all_to_all(value_send, "seq", split_axis=1, concat_axis=0, tiled=True),
    )
    seq_rows = query_seq.shape[0]
    key_seq = key_seq.reshape(seq_rows, head_size)
    value_seq = value_seq.reshape(seq_rows, head_size)
    block_rows = min(512, seq_rows)
    block_count = seq_rows // block_rows
    query_blocks = query_seq.reshape(block_count, block_rows, head_local, head_size)
    firsts = jnp.arange(block_count, dtype=jnp.int32) * block_rows
    columns = jnp.arange(seq_rows, dtype=jnp.int32)

    def block_scores(query_blk, first_row):
        scores = (
            jnp.einsum("qhd,kd->hqk", query_blk, key_seq, preferred_element_type=jnp.float32)
            * scale_qk
        )
        causal = columns[None, :] <= (first_row + jnp.arange(block_rows, dtype=jnp.int32))[:, None]
        return jnp.where(causal[None], scores, NEG_LARGE)

    def attend(operands):
        query_blk, first_row = operands
        scores = block_scores(query_blk, first_row)
        row_peak = jnp.max(scores, axis=-1, keepdims=True)
        exponent = jnp.exp(scores - row_peak)
        row_total = jnp.sum(exponent, axis=-1, keepdims=True)
        weights_low = (exponent / row_total).astype(jnp.bfloat16)
        output = jnp.einsum(
            "hqk,kd->qhd", weights_low, value_seq, preferred_element_type=jnp.float32
        )
        return (output.astype(jnp.bfloat16), (row_peak + jnp.log(row_total))[..., 0])

    attended, log_sums = lax.map(attend, (query_blocks, firsts))
    attn_tok = lax.all_to_all(
        attended.reshape(seq_rows, 1, head_local * head_size),
        "seq",
        split_axis=0,
        concat_axis=1,
        tiled=True,
    ).reshape(tok_rows, heads_all * head_size)
    middle = inputs + jnp.dot(attn_tok, output_w, preferred_element_type=jnp.float32)
    normed_m, scale_m = norm_parts(middle)
    mixer_in = (normed_m * gain_mlp.astype(jnp.float32)).astype(jnp.bfloat16)
    logits = jnp.dot(mixer_in, router_w, preferred_element_type=jnp.float32)
    chosen = expert_ids[:, :, None] == jnp.arange(experts_all, dtype=jnp.int32)[None, None, :]
    picked_logits = jnp.sum(jnp.where(chosen, logits[:, None, :], 0.0), axis=-1)
    gate_share = jax.nn.softmax(picked_logits, axis=-1)
    flat_ids = expert_ids.reshape(route_rows)
    onehot = (flat_ids[:, None] == jnp.arange(experts_all, dtype=jnp.int32)[None, :]).astype(
        jnp.int32
    )
    slot_index = jnp.sum((jnp.cumsum(onehot, axis=0) - 1) * onehot, axis=-1)
    places = flat_ids * capacity + slot_index
    route_token = jnp.arange(route_rows, dtype=jnp.int32) // top_k
    send_rows = (
        jnp.zeros((experts_all * capacity, model_width), jnp.bfloat16)
        .at[places]
        .set(mixer_in[route_token])
    )
    arrived = lax.all_to_all(
        send_rows.reshape(groups, local_experts, capacity, model_width),
        "seq",
        split_axis=0,
        concat_axis=0,
        tiled=True,
    )
    gate_pre = jnp.einsum("secd,edf->secf", arrived, gate_w, preferred_element_type=jnp.float32)
    up_pre = jnp.einsum("secd,edf->secf", arrived, up_w, preferred_element_type=jnp.float32)
    silu_gate = jax.nn.silu(gate_pre)
    active = (silu_gate * up_pre).astype(jnp.bfloat16)
    produced = jnp.einsum(
        "secf,efd->secd", active, down_w, preferred_element_type=jnp.float32
    ).astype(jnp.bfloat16)
    returned = lax.all_to_all(produced, "seq", split_axis=0, concat_axis=0, tiled=True).reshape(
        experts_all * capacity, model_width
    )
    picked = returned[places].astype(jnp.float32).reshape(tok_rows, top_k, model_width)
    layer_out = (middle + jnp.sum(picked * gate_share[:, :, None], axis=1)).astype(jnp.bfloat16)
    grad_out = cotangent.astype(jnp.float32)
    grad_gates = jnp.sum(grad_out[:, None, :] * picked, axis=-1)
    grad_picked = gate_share * (
        grad_gates - jnp.sum(gate_share * grad_gates, axis=-1, keepdims=True)
    )
    grad_logits = jnp.sum(jnp.where(chosen, grad_picked[:, :, None], 0.0), axis=1).astype(
        jnp.bfloat16
    )
    grad_rows = (
        (gate_share[:, :, None] * grad_out[:, None, :])
        .astype(jnp.bfloat16)
        .reshape(route_rows, model_width)
    )
    grad_send = (
        jnp.zeros((experts_all * capacity, model_width), jnp.bfloat16).at[places].set(grad_rows)
    )
    grad_arrived = lax.all_to_all(
        grad_send.reshape(groups, local_experts, capacity, model_width),
        "seq",
        split_axis=0,
        concat_axis=0,
        tiled=True,
    )
    grad_active = jnp.einsum(
        "secd,efd->secf", grad_arrived, down_w, preferred_element_type=jnp.float32
    )
    grad_down = jnp.einsum(
        "secf,secd->efd", active, grad_arrived, preferred_element_type=jnp.float32
    )
    gate_sigmoid = jax.nn.sigmoid(gate_pre)
    grad_up_pre = (grad_active * silu_gate).astype(jnp.bfloat16)
    grad_gate_pre = (
        grad_active * up_pre * gate_sigmoid * (1.0 + gate_pre * (1.0 - gate_sigmoid))
    ).astype(jnp.bfloat16)
    grad_gate = jnp.einsum(
        "secd,secf->edf", arrived, grad_gate_pre, preferred_element_type=jnp.float32
    )
    grad_up = jnp.einsum("secd,secf->edf", arrived, grad_up_pre, preferred_element_type=jnp.float32)
    grad_entered = (
        jnp.einsum("secf,edf->secd", grad_gate_pre, gate_w, preferred_element_type=jnp.float32)
        + jnp.einsum("secf,edf->secd", grad_up_pre, up_w, preferred_element_type=jnp.float32)
    ).astype(jnp.bfloat16)
    grad_back = lax.all_to_all(
        grad_entered, "seq", split_axis=0, concat_axis=0, tiled=True
    ).reshape(experts_all * capacity, model_width)
    grad_mixer = jnp.sum(
        grad_back[places].astype(jnp.float32).reshape(tok_rows, top_k, model_width), axis=1
    ) + against(grad_logits, router_w)
    grad_router = contract_rows(mixer_in, grad_logits)
    grad_gain_m = jnp.sum(grad_mixer * normed_m, axis=0)
    grad_middle = grad_out + norm_back(grad_mixer * gain_mlp.astype(jnp.float32), normed_m, scale_m)
    grad_branch = grad_middle.astype(jnp.bfloat16)
    grad_output_w = contract_rows(attn_tok, grad_branch)
    grad_attended = (
        against(grad_branch, output_w)
        .astype(jnp.bfloat16)
        .reshape(tok_rows, groups, head_local * head_size)
    )
    grad_seq = lax.all_to_all(
        grad_attended, "seq", split_axis=1, concat_axis=0, tiled=True
    ).reshape(block_count, block_rows, head_local, head_size)

    def attend_back(carried, operands):
        grad_key_acc, grad_value_acc = carried
        query_blk, grad_blk, log_blk, first_row = operands
        scores = block_scores(query_blk, first_row)
        probs_full = jnp.exp(scores - log_blk[:, :, None])
        grad_value_acc = grad_value_acc + jnp.einsum(
            "hqk,qhd->kd",
            probs_full.astype(jnp.bfloat16),
            grad_blk,
            preferred_element_type=jnp.float32,
        )
        grad_probs = jnp.einsum(
            "qhd,kd->hqk", grad_blk, value_seq, preferred_element_type=jnp.float32
        )
        grad_scores = (
            probs_full * (grad_probs - jnp.sum(probs_full * grad_probs, axis=-1, keepdims=True))
        ).astype(jnp.bfloat16)
        grad_query_blk = (
            jnp.einsum("hqk,kd->qhd", grad_scores, key_seq, preferred_element_type=jnp.float32)
            * scale_qk
        )
        grad_key_acc = (
            grad_key_acc
            + jnp.einsum("hqk,qhd->kd", grad_scores, query_blk, preferred_element_type=jnp.float32)
            * scale_qk
        )
        return ((grad_key_acc, grad_value_acc), grad_query_blk.astype(jnp.bfloat16))

    zeros_kv = jnp.zeros((seq_rows, head_size), jnp.float32)
    (grad_key_seq, grad_value_seq), grad_query_seq = lax.scan(
        attend_back, (zeros_kv, zeros_kv), (query_blocks, grad_seq, log_sums, firsts)
    )
    grad_query_tok, grad_key_tok, grad_value_tok = (
        lax.all_to_all(
            grad_query_seq.reshape(seq_rows, 1, head_local * head_size),
            "seq",
            split_axis=0,
            concat_axis=1,
            tiled=True,
        ),
        lax.all_to_all(
            grad_key_seq.astype(jnp.bfloat16).reshape(seq_rows, 1, head_size),
            "seq",
            split_axis=0,
            concat_axis=1,
            tiled=True,
        ),
        lax.all_to_all(
            grad_value_seq.astype(jnp.bfloat16).reshape(seq_rows, 1, head_size),
            "seq",
            split_axis=0,
            concat_axis=1,
            tiled=True,
        ),
    )
    grad_query_rot = grad_query_tok.astype(jnp.float32).reshape(tok_rows, heads_all, head_size)
    grad_key_rot = jnp.sum(
        grad_key_tok.astype(jnp.float32).reshape(tok_rows, kv_heads, copies, head_size), axis=2
    )
    grad_value_sum = jnp.sum(
        grad_value_tok.astype(jnp.float32).reshape(tok_rows, kv_heads, copies, head_size), axis=2
    )
    grad_query_norm = unrotate(grad_query_rot, cos_table, sine_table)
    grad_key_norm = unrotate(grad_key_rot, cos_table, sine_table)
    grad_gain_q = jnp.sum(grad_query_norm * query_hat, axis=(0, 1))
    grad_gain_k = jnp.sum(grad_key_norm * key_hat, axis=(0, 1))
    grad_query_pre = (
        norm_back(grad_query_norm * gain_q, query_hat, query_scale)
        .astype(jnp.bfloat16)
        .reshape(tok_rows, heads_all * head_size)
    )
    grad_key_pre = (
        norm_back(grad_key_norm * gain_k, key_hat, key_scale)
        .astype(jnp.bfloat16)
        .reshape(tok_rows, kv_heads * head_size)
    )
    grad_value_pre = grad_value_sum.astype(jnp.bfloat16).reshape(tok_rows, kv_heads * head_size)
    grad_hidden = (
        against(grad_query_pre, query_w)
        + against(grad_key_pre, key_w)
        + against(grad_value_pre, value_w)
    )
    grad_query_w = contract_rows(hidden, grad_query_pre)
    grad_key_w = contract_rows(hidden, grad_key_pre)
    grad_value_w = contract_rows(hidden, grad_value_pre)
    grad_gain_a = jnp.sum(grad_hidden * normed_a, axis=0)
    grad_tokens = (
        grad_middle + norm_back(grad_hidden * gain_attn.astype(jnp.float32), normed_a, scale_a)
    ).astype(jnp.bfloat16)
    dense_out = (
        lax.psum_scatter(grad_gain_a, ("fsdp", "seq"), scatter_dimension=0, tiled=True),
        lax.psum_scatter(grad_query_w, ("fsdp", "seq"), scatter_dimension=0, tiled=True),
        lax.psum_scatter(grad_key_w, ("fsdp", "seq"), scatter_dimension=0, tiled=True),
        lax.psum_scatter(grad_value_w, ("fsdp", "seq"), scatter_dimension=0, tiled=True),
        lax.psum_scatter(grad_gain_q, ("fsdp", "seq"), scatter_dimension=0, tiled=True),
        lax.psum_scatter(grad_gain_k, ("fsdp", "seq"), scatter_dimension=0, tiled=True),
        lax.psum_scatter(grad_output_w, ("fsdp", "seq"), scatter_dimension=0, tiled=True),
        lax.psum_scatter(grad_gain_m, ("fsdp", "seq"), scatter_dimension=0, tiled=True),
        lax.psum_scatter(grad_router, ("fsdp", "seq"), scatter_dimension=0, tiled=True),
    )
    expert_out = (
        lax.psum_scatter(
            grad_gate.astype(jnp.bfloat16), "fsdp", scatter_dimension=1, tiled=True
        ).astype(jnp.float32),
        lax.psum_scatter(
            grad_up.astype(jnp.bfloat16), "fsdp", scatter_dimension=1, tiled=True
        ).astype(jnp.float32),
        lax.psum_scatter(
            grad_down.astype(jnp.bfloat16), "fsdp", scatter_dimension=2, tiled=True
        ).astype(jnp.float32),
    )
    return (
        layer_out,
        grad_tokens,
        dense_out[0],
        dense_out[1],
        dense_out[2],
        dense_out[3],
        dense_out[4],
        dense_out[5],
        dense_out[6],
        dense_out[7],
        dense_out[8],
        expert_out[0],
        expert_out[1],
        expert_out[2],
    )


def solution(mesh):
    in_specs = (
        P(("fsdp", "seq"), None),
        P(("fsdp", "seq"), None),
        P(("fsdp", "seq"), None),
        P(("fsdp", "seq")),
        P(("fsdp", "seq"), None),
        P(("fsdp", "seq"), None),
        P(("fsdp", "seq"), None),
        P(("fsdp", "seq")),
        P(("fsdp", "seq")),
        P(("fsdp", "seq"), None),
        P(("fsdp", "seq")),
        P(("fsdp", "seq"), None),
        P("seq", "fsdp", None),
        P("seq", "fsdp", None),
        P("seq", None, "fsdp"),
    )
    out_specs = (
        P(("fsdp", "seq"), None),
        P(("fsdp", "seq"), None),
        P(("fsdp", "seq")),
        P(("fsdp", "seq"), None),
        P(("fsdp", "seq"), None),
        P(("fsdp", "seq"), None),
        P(("fsdp", "seq")),
        P(("fsdp", "seq")),
        P(("fsdp", "seq"), None),
        P(("fsdp", "seq")),
        P(("fsdp", "seq"), None),
        P("seq", "fsdp", None),
        P("seq", "fsdp", None),
        P("seq", None, "fsdp"),
    )
    return jax.shard_map(
        on_device, mesh=mesh, in_specs=in_specs, out_specs=out_specs, check_vma=False
    )
```

profile of v0, /device:TPU:0, one launch (start us, length us, event | category | flops | bytes accessed | tf_op | source)
XLA Modules:
  0.0 3075.1 jit_solution(11224609173771714770)
XLA Ops:
  13.4 42.2 %all-reduce.9 = (bf16[2048]{0:T(1024)(128)(2,1)S(1)}, bf16[128]{0:T(256)(128)(2,1)S(1)}, bf16[128]{0:T(256)(128)(2,1)S(1)}, bf16[2048]{0:T(1024)(128)(2,1)S(1)}) all-reduce(bf16[2048]{0:T(1024)(128)(2,1)S(1)} %dynamic-update-slice, bf16[128]{0:T(256)(128)(2,1)S(1)} %dynamic-update-slice.1, ...), channel_id=1, replica_groups=mesh['fsdp'=4,'seq'=8] {'fsdp','seq'}, use_global_device_ids=true, to_apply=%add | all-reduce | flops 4352 | bytes 17408
  57.4 12.9 all-gather.11.cloned.1.call-done
  79.1 110.7 %all-gather.9.cloned.1.call-done = bf16[2048,4096]{1,0:T(8,128)(2,1)} async-done(((bf16[64,4096]{1,0:T(8,128)(2,1)}), bf16[2048,4096]{1,0:T(8,128)(2,1)}) %all-gather.9.cloned.1.call-update) | async-done | bytes 16777232 | tf_op jit(solution)/shard_map/all_gather | solution.py:93
  213.4 41.0 %all-gather.13.cloned.1.call-done = bf16[2048,512]{1,0:T(8,128)(2,1)} async-done(((bf16[64,512]{1,0:T(8,128)(2,1)}), bf16[2048,512]{1,0:T(8,128)(2,1)}) %all-gather.13.cloned.1.call-update) | async-done | bytes 2097168 | tf_op jit(solution)/shard_map/all_gather | solution.py:95
  274.3 19.0 while.28
  317.2 37.6 %all-to-all-done.3 = bf16[8,2,32768]{2,1,0:T(2,128)(2,1)S(1)} async-done(((bf16[8,2,32768]{2,1,0:T(2,128)(2,1)}), bf16[8,2,32768]{2,1,0:T(2,128)(2,1)S(1)}, u32[]{:S(2)}, u32[]{:S(2)}) %all-to-all-start.3) | async-done | bytes 1048608 | tf_op jit(solution)/shard_map/all_to_all | solution.py:181
  360.9 24.9 all-gather.15.cloned.1.call-done
  395.4 32.4 %scatter_custom_fusion = bf16[1360,2048]{1,0:T(8,128)(2,1)} fusion(s32[1024]{0:T(1024)S(1)} %bitcast.436, bf16[128,2048]{1,0:T(8,128)(2,1)S(1)} %multiply_convert_fusion, s32[1024]{0:T(1024)S(1)} %broadcast_clamp_fusion.1, bf16[]{:T(256)} %constant.58.clone.1), kind=kCustom, calls=%fused_computation.109 | custom fusion | bytes 5570562 | tf_op jit(solution)/shard_map/scatter | solution.py:205
  450.0 178.5 %all-gather = bf16[32,64,16]{1,2,0:T(8,128)(2,1)S(1)} all-gather(bf16[1,64,16]{1,2,0:T(8,128)(2,1)S(1)} %bitcast.440), channel_id=1, replica_groups=mesh['fsdp'=4,'seq'=8] {'fsdp','seq'}, dimensions={0}, use_global_device_ids=true | all-gather | bytes 67584 | tf_op jit(solution)/shard_map/all_gather | solution.py:100
  661.9 12.5 fusion.57
  674.5 12.4 fusion.53
  686.9 23.4 all-gather.21.cloned.1.call-done
  710.3 68.8 %all-to-all-done.6 = bf16[8,2,85,2048]{3,1,2,0:T(2,128)(2,1)} async-done(((bf16[8,2,85,2048]{3,1,2,0:T(2,128)(2,1)}), bf16[8,2,85,2048]{3,1,2,0:T(2,128)(2,1)}, u32[]{:S(2)}, u32[]{:S(2)}) %all-to-all-start.6) | async-done | bytes 5570592 | tf_op jit(solution)/shard_map/all_to_all | solution.py:242
  779.1 17.3 fusion.70
  804.5 14.5 copy.410
  824.0 121.6 %all-to-all-done.5 = bf16[8,2,85,2048]{3,1,2,0:T(2,128)(2,1)} async-done(((bf16[8,2,85,2048]{3,1,2,0:T(2,128)(2,1)}), bf16[8,2,85,2048]{3,1,2,0:T(2,128)(2,1)}, u32[]{:S(2)}, u32[]{:S(2)}) %all-to-all-start.5) | async-done | bytes 5570592 | tf_op jit(solution)/shard_map/all_to_all | solution.py:221
  958.5 12.1 gather_fusion
  987.8 12.5 fusion.51
  1000.3 13.9 fusion.63
  1042.5 115.1 %all-to-all-done.7 = bf16[8,2,85,2048]{3,1,2,0:T(2,128)(2,1)} async-done(((bf16[8,2,85,2048]{3,1,2,0:T(2,128)(2,1)}), bf16[8,2,85,2048]{3,1,2,0:T(2,128)(2,1)}, u32[]{:S(2)}, u32[]{:S(2)}) %all-to-all-start.7) | async-done | bytes 5570592 | tf_op jit(solution)/shard_map/all_to_all | solution.py:268
  1170.5 12.3 gather_fusion.1
  1191.3 11.8 convolution_convert_fusion
  1220.2 13.8 all-to-all-done.8
  1237.4 48.8 %while.29 = (s32[]{:T(128)}, f32[1024,128]{1,0:T(8,128)S(1)}, f32[1024,128]{1,0:T(8,128)}, bf16[2,512,4,128]{3,2,1,0:T(4,128)(2,1)}, s32[2]{0:T(128)S(1)}, /*ind...) while((s32[]{:T(128)}, f32[1024,128]{1,0:T(8,128)S(1)}, ...), condition=%wide.region_24.25_spmd.clone, body=%wide.region_22.24_spmd.clone.sunk | while | flops 2717514240 | bytes 127202032 | solution.py:317
  1322.8 13.2 fusion.111
  1359.1 26.3 all-to-all-done.9
  1407.4 13.5 fusion.128
  1449.2 40.2 %all-reduce.8 = (f32[2048]{0:T(1024)S(1)}, f32[128]{0:T(128)S(1)}, f32[128]{0:T(128)S(1)}, f32[2048]{0:T(1024)S(1)}) all-reduce(f32[2048]{0:T(1024)S(1)} %get-tuple-element.329, f32[128]{0:T(128)S(1)} %bitcast_reduce_fusion.1, f32[128]{0:T(128)S(1)} %bitcast_reduce_fusion.2, ...), channel_id=2, replica_groups=mesh['fsdp'=4,'seq'=8] {'fsdp','seq'}, use_global_device_ids=true, to_apply=%region_31.32.clone | all-reduce | flops 4352 | bytes 34816
  1493.0 16.5 reduce-scatter.13.cloned.1.call-done
  1509.5 144.1 %reduce-scatter.15.cloned.1.call-done = f32[64,512]{1,0:T(8,128)} async-done(((f32[2048,512]{1,0:T(8,128)}), f32[64,512]{1,0:T(8,128)}) %reduce-scatter.15.cloned.1.call-update) | async-done | bytes 131088 | tf_op jit(solution)/shard_map/reduce_scatter | solution.py:381
  1653.5 706.0 %reduce-scatter.17.cloned.1.call-done = f32[128,2048]{1,0:T(8,128)} async-done(((f32[4096,2048]{1,0:T(8,128)}), f32[128,2048]{1,0:T(8,128)}) %reduce-scatter.17.cloned.1.call-update) | async-done | bytes 1048592 | tf_op jit(solution)/shard_map/reduce_scatter | solution.py:384
  2359.5 708.6 %reduce-scatter.11.cloned.1.call-done = f32[64,4096]{1,0:T(8,128)} async-done(((f32[2048,4096]{1,0:T(8,128)}), f32[64,4096]{1,0:T(8,128)}) %reduce-scatter.11.cloned.1.call-update) | async-done | bytes 1048592 | tf_op jit(solution)/shard_map/reduce_scatter | solution.py:379
  (388 shorter events, 448.0 us)
Async XLA Ops:
  7.2 182.6 %copy-start.4 = (bf16[128,2048]{1,0:T(8,128)(2,1)S(1)}, bf16[128,2048]{1,0:T(8,128)(2,1)}, u32[]{:S(2)}) copy-start(bf16[128,2048]{1,0:T(8,128)(2,1)} %param.19) | copy-start | bytes 1572868
  7.2 63.1 %all-gather.11.cloned.1.call-start = ((), (), s32[]{:S(2)}) async-start(), calls=%async_computation.21 | async-start | bytes 2162688 | tf_op jit(solution)/shard_map/all_gather | solution.py:94
  7.9 181.8 %all-gather.9.cloned.1.call-start = ((), (), s32[]{:S(2)}) async-start(), calls=%async_computation.20 | async-start | bytes 17301504 | tf_op jit(solution)/shard_map/all_gather | solution.py:93
  8.7 245.7 %all-gather.13.cloned.1.call-start = ((), (), s32[]{:S(2)}) async-start(), calls=%async_computation.22 | async-start | bytes 2162688 | tf_op jit(solution)/shard_map/all_gather | solution.py:95
  9.4 376.4 %all-gather.15.cloned.1.call-start = ((), (), s32[]{:S(2)}) async-start(), calls=%async_computation.23 | async-start | bytes 17301504 | tf_op jit(solution)/shard_map/all_gather | solution.py:98
  55.6 198.8 %copy-start.27 = (f32[2048]{0:T(1024)}, f32[2048]{0:T(1024)S(1)}, u32[]{:S(2)}) copy-start(f32[2048]{0:T(1024)S(1)} %convert_element_type.216) | copy-start | bytes 24580
  55.8 152.5 %copy-start.35 = (f32[128,64]{0,1:T(8,128)}, f32[128,64]{0,1:T(8,128)S(1)}, u32[]{:S(2)}) copy-start(f32[128,64]{0,1:T(8,128)S(1)} %get-tuple-element.398) | copy-start | bytes 98308
  55.8 152.5 %copy-start.37 = (f32[128,64]{0,1:T(8,128)}, f32[128,64]{0,1:T(8,128)S(1)}, u32[]{:S(2)}) copy-start(f32[128,64]{0,1:T(8,128)S(1)} %get-tuple-element.399) | copy-start | bytes 98308
  57.3 197.1 %copy-start.46 = (f32[128]{0:T(128)}, f32[128]{0:T(128)S(1)}, u32[]{:S(2)}) copy-start(f32[128]{0:T(128)S(1)} %add_rsqrt_fusion.3) | copy-start | bytes 1540
  74.7 135.0 %all-to-all-start.1 = ((bf16[128,8,128]{2,0,1:T(8,128)(2,1)}), bf16[128,8,128]{2,0,1:T(8,128)(2,1)S(1)}, u32[]{:S(2)}, u32[]{:S(2)}) async-start(bf16[128,8,128]{2,0,1:T(8,128)(2,1)} %bitcast.3), calls=%async_computation.1 | async-start | bytes 524288 | tf_op jit(solution)/shard_map/all_to_all | solution.py:148
  209.7 46.8 %all-to-all-start = ((bf16[128,8,512]{0,2,1:T(8,128)(2,1)}), bf16[128,8,512]{0,2,1:T(8,128)(2,1)S(1)}, u32[]{:S(2)}, u32[]{:S(2)}) async-start(bf16[128,8,512]{0,2,1:T(8,128)(2,1)} %bitcast), calls=%async_computation | async-start | bytes 2097152 | tf_op jit(solution)/shard_map/all_to_all | solution.py:147
  257.3 16.8 all-to-all-start.2
  261.6 400.3 %all-gather.17.cloned.1.call-start = ((), (), s32[]{:S(2)}) async-start(), calls=%async_computation.24 | async-start | bytes 7864320 | tf_op jit(solution)/shard_map/all_gather | solution.py:103
  306.9 48.0 %all-to-all-start.3 = ((bf16[8,2,32768]{2,1,0:T(2,128)(2,1)}), bf16[8,2,32768]{2,1,0:T(2,128)(2,1)S(1)}, u32[]{:S(2)}, u32[]{:S(2)}) async-start(bf16[8,2,32768]{2,1,0:T(2,128)(2,1)} %reshape.637), calls=%async_computation.3 | async-start | bytes 2097152 | tf_op jit(solution)/shard_map/all_to_all | solution.py:181
  444.6 184.2 %copy-start.25 = (bf16[128,2048]{1,0:T(8,128)(2,1)S(1)}, bf16[128,2048]{1,0:T(8,128)(2,1)}, u32[]{:S(2)}) copy-start(bf16[128,2048]{1,0:T(8,128)(2,1)} %param.20) | copy-start | bytes 1572868
  444.6 211.8 %all-to-all-start.4 = ((bf16[8,2,85,2048]{3,1,2,0:T(2,128)(2,1)}), bf16[8,2,85,2048]{3,1,2,0:T(2,128)(2,1)}, u32[]{:S(2)}, u32[]{:S(2)}) async-start(bf16[8,2,85,2048]{3,1,2,0:T(2,128)(2,1)} %copy.407), calls=%async_computation.4 | async-start | bytes 11141120 | tf_op jit(solution)/shard_map/all_to_all | solution.py:207
  449.4 225.0 %all-gather.19.cloned.1.call-start = ((), (), s32[]{:S(2)}) async-start(), calls=%async_computation.25 | async-start | bytes 7864320 | tf_op jit(solution)/shard_map/all_gather | solution.py:104
  656.4 122.7 %all-to-all-start.6 = ((bf16[8,2,85,2048]{3,1,2,0:T(2,128)(2,1)}), bf16[8,2,85,2048]{3,1,2,0:T(2,128)(2,1)}, u32[]{:S(2)}, u32[]{:S(2)}) async-start(bf16[8,2,85,2048]{3,1,2,0:T(2,128)(2,1)} %copy.415), calls=%async_computation.6 | async-start | bytes 11141120 | tf_op jit(solution)/shard_map/all_to_all | solution.py:242
  661.1 49.2 %all-gather.21.cloned.1.call-start = ((), (), s32[]{:S(2)}) async-start(), calls=%async_computation.26 | async-start | bytes 7864320 | tf_op jit(solution)/shard_map/all_gather | solution.py:105
  819.0 126.6 %all-to-all-start.5 = ((bf16[8,2,85,2048]{3,1,2,0:T(2,128)(2,1)}), bf16[8,2,85,2048]{3,1,2,0:T(2,128)(2,1)}, u32[]{:S(2)}, u32[]{:S(2)}) async-start(bf16[8,2,85,2048]{3,1,2,0:T(2,128)(2,1)} %copy.410), calls=%async_computation.5 | async-start | bytes 11141120 | tf_op jit(solution)/shard_map/all_to_all | solution.py:221
  823.8 597.2 %reduce-scatter.25.cloned.1.call-start = ((), (), s32[]{:S(2)}) async-start(), calls=%async_computation.34 | async-start | bytes 1081344
  977.0 445.5 %reduce-scatter.23.cloned.1.call-start = ((), (), s32[]{:S(2)}) async-start(), calls=%async_computation.33 | async-start | bytes 7864320 | tf_op jit(solution)/shard_map/reduce_scatter | solution.py:395
  1025.9 131.7 %all-to-all-start.7 = ((bf16[8,2,85,2048]{3,1,2,0:T(2,128)(2,1)}), bf16[8,2,85,2048]{3,1,2,0:T(2,128)(2,1)}, u32[]{:S(2)}, u32[]{:S(2)}) async-start(bf16[8,2,85,2048]{3,1,2,0:T(2,128)(2,1)} %copy.417), calls=%async_computation.7 | async-start | bytes 11141120 | tf_op jit(solution)/shard_map/all_to_all | solution.py:268
  1030.6 395.4 %reduce-scatter.19.cloned.1.call-start = ((), (), s32[]{:S(2)}) async-start(), calls=%async_computation.31 | async-start | bytes 7864320 | tf_op jit(solution)/shard_map/reduce_scatter | solution.py:389
  1204.2 29.8 all-to-all-start.8
  1208.4 220.9 %reduce-scatter.21.cloned.1.call-start = ((), (), s32[]{:S(2)}) async-start(), calls=%async_computation.32 | async-start | bytes 7864320 | tf_op jit(solution)/shard_map/reduce_scatter | solution.py:392
  1289.0 12.2 all-to-all-start.10
  1292.5 217.0 %reduce-scatter.13.cloned.1.call-start = ((), (), s32[]{:S(2)}) async-start(), calls=%async_computation.28 | async-start | bytes 4325376 | tf_op jit(solution)/shard_map/reduce_scatter | solution.py:380
  1306.7 346.9 %reduce-scatter.15.cloned.1.call-start = ((), (), s32[]{:S(2)}) async-start(), calls=%async_computation.29 | async-start | bytes 4325376 | tf_op jit(solution)/shard_map/reduce_scatter | solution.py:381
  1322.8 1036.8 %reduce-scatter.17.cloned.1.call-start = ((), (), s32[]{:S(2)}) async-start(), calls=%async_computation.30 | async-start | bytes 34603008 | tf_op jit(solution)/shard_map/reduce_scatter | solution.py:384
  1352.6 32.8 %all-to-all-start.9 = ((bf16[8,2,32768]{2,1,0:T(2,128)(2,1)}), bf16[8,2,32768]{2,1,0:T(2,128)(2,1)}, u32[]{:S(2)}, u32[]{:S(2)}) async-start(bf16[8,2,32768]{2,1,0:T(2,128)(2,1)} %reshape.639), calls=%async_computation.9 | async-start | bytes 2097152 | tf_op jit(solution)/shard_map/all_to_all | solution.py:321
  1356.9 1711.3 %reduce-scatter.11.cloned.1.call-start = ((), (), s32[]{:S(2)}) async-start(), calls=%async_computation.27 | async-start | bytes 34603008 | tf_op jit(solution)/shard_map/reduce_scatter | solution.py:379
  (57 other events, 1526.6 us)
Sparse Core Ops, SparseCore 0:
  11.0 59.2 all-gather.10
  73.4 116.3 all-gather.8
  192.7 61.6 all-gather.12
  257.3 128.3 all-gather.14
  387.2 44.0 all-gather.16
  451.5 46.7 all-gather.18
  663.5 46.7 all-gather.20
  977.1 197.4 reduce-scatter.24
  1177.3 59.3 reduce-scatter.22
  1239.1 58.3 reduce-scatter.18
  1300.2 58.3 reduce-scatter.20
  1361.3 148.1 reduce-scatter.12
  1512.3 141.1 reduce-scatter.14
  1656.3 703.2 reduce-scatter.16
  2362.2 705.8 reduce-scatter.10
where the time goes:
time: 3080 us
  waiting for transfers between devices  2190 us (71%)
  blocking collectives  272 us (9%)
  matrix products  238 us (8%)
  local copies, waits for them, and re-layouts  216 us (7%)
  other arithmetic  90.2 us (3%)
  starting transfers between devices  49.8 us (2%)
    reduce_scatter x1, waiting for transfers between devices, on_device(): lax.psum_scatter(grad_query_w, ('fsdp', 'seq'), scatter_dimension=0, tile...  709 us
    reduce_scatter x1, waiting for transfers between devices, on_device(): lax.psum_scatter(grad_output_w, ('fsdp', 'seq'), scatter_dimension=0, til...  706 us
    all_gather x1, blocking collectives, on_device(): lax.all_gather(w_router, ('fsdp', 'seq'), axis=0, tiled=True)  179 us
    reduce_scatter x1, waiting for transfers between devices, on_device(): lax.psum_scatter(grad_value_w, ('fsdp', 'seq'), scatter_dimension=0, tile...  144 us
    all_to_all x1, waiting for transfers between devices, on_device(): lax.all_to_all(produced, 'seq', split_axis=0, concat_axis=0, tiled=True)  122 us
    all_to_all x1, waiting for transfers between devices, on_device(): lax.all_to_all(grad_entered, 'seq', split_axis=0, concat_axis=0, tiled=True)  115 us
    all_gather x1, waiting for transfers between devices, on_device(): lax.all_gather(w_query, ('fsdp', 'seq'), axis=0, tiled=True)  111 us
    unnamed x2, blocking collectives  82.4 us
  transfers between devices with their start and end apart: 26, of which 17 were waited for; matrix products, arithmetic and copies ran while one was open for 15% of the time, Pallas kernels for 0%

commit v1 on v0

v1 whole, which is shorter than its diff:
```python
import math

import jax
import jax.numpy as jnp
from jax import lax
from jax.sharding import PartitionSpec as P

NORM_EPS = 1e-06
ROPE_BASE = 1000000.0
NEG_LARGE = -1e30
F32 = jnp.float32
BF16 = jnp.bfloat16
ALL = ("fsdp", "seq")


def dot(left, right, left_dim, right_dim):
    return lax.dot_general(
        left, right, (((left_dim,), (right_dim,)), ((), ())), preferred_element_type=F32
    )


def norm_parts(values):
    row_scale = lax.rsqrt(jnp.mean(values * values, axis=-1, keepdims=True) + NORM_EPS)
    return (values * row_scale, row_scale)


def norm_back(grad_normed, normed, row_scale):
    return row_scale * (
        grad_normed - normed * jnp.mean(grad_normed * normed, axis=-1, keepdims=True)
    )


def rotary_tables(positions, head_size):
    half_size = head_size // 2
    frequency = jnp.exp(
        jnp.arange(half_size, dtype=F32) * (-2.0 * math.log(ROPE_BASE) / head_size)
    )
    angles = positions[:, None] * frequency[None, :]
    return (jnp.cos(angles)[:, None, :], jnp.sin(angles)[:, None, :])


def rotate(values, cos_table, sine_table):
    half_size = values.shape[-1] // 2
    first_half = values[..., :half_size]
    second_half = values[..., half_size:]
    return jnp.concatenate(
        [
            first_half * cos_table - second_half * sine_table,
            second_half * cos_table + first_half * sine_table,
        ],
        axis=-1,
    )


def unrotate(gradient, cos_table, sine_table):
    return rotate(gradient, cos_table, -sine_table)


def after(value, *others):
    return lax.optimization_barrier((value, *others))[0]


def ring_order(size):
    if size % 4 or size < 8:
        return list(range(size))
    wide = size // 4
    walk = [(0, y) for y in range(wide)]
    for z in range(1, 4):
        walk += [(z, y) for y in (range(wide - 1, 0, -1) if z % 2 else range(1, wide))]
    walk += [(z, 0) for z in (3, 2, 1)]
    return [z * wide + y for z, y in walk]


class Ring:
    def __init__(self, size):
        self.size = size
        self.order = ring_order(size)
        place = [0] * size
        for i, member in enumerate(self.order):
            place[member] = i
        self.here = jnp.asarray(place, jnp.int32)[lax.axis_index("seq")]
        self.table = jnp.asarray(self.order, jnp.int32)
        self.up = [(self.order[i], self.order[(i + 1) % size]) for i in range(size)]
        self.down = [(self.order[i], self.order[(i - 1) % size]) for i in range(size)]

    def member(self, offset):
        return self.table[lax.rem(self.here + (offset + self.size), self.size)]

    def gather(self, block):
        size, rows = self.size, block.shape[0]
        whole = jnp.zeros((size * rows,) + block.shape[1:], block.dtype)
        tail = (0,) * (block.ndim - 1)

        def put(whole, piece, owner, shift=0):
            return lax.dynamic_update_slice(whole, piece, (owner * rows + shift,) + tail)

        whole = put(whole, block, self.member(0))
        from_left = from_right = block
        for step in range(1, size // 2):
            from_left = lax.ppermute(from_left, "seq", self.up)
            from_right = lax.ppermute(from_right, "seq", self.down)
            whole = put(whole, from_left, self.member(-step))
            whole = put(whole, from_right, self.member(step))
        half = rows // 2
        far = self.member(size // 2)
        whole = put(whole, lax.ppermute(from_left[:half], "seq", self.up), far)
        return put(whole, lax.ppermute(from_right[half:], "seq", self.down), far, half)

    def scatter(self, whole):
        size = self.size
        rows = whole.shape[0] // size
        half = rows // 2

        def piece(offset):
            return lax.dynamic_slice_in_dim(whole, self.member(offset) * rows, rows, 0)

        far = piece(size // 2).astype(BF16)
        left_half = lax.ppermute(far[:half], "seq", self.up)
        right_half = lax.ppermute(far[half:], "seq", self.down)
        blank = jnp.zeros((rows - half,) + whole.shape[1:], BF16)
        from_left = jnp.concatenate([left_half, blank], axis=0)
        from_right = jnp.concatenate([blank, right_half], axis=0)
        for step in range(size // 2 - 1, 0, -1):
            send_up = (piece(step) + from_left.astype(F32)).astype(BF16)
            send_down = (piece(-step) + from_right.astype(F32)).astype(BF16)
            from_left = lax.ppermute(send_up, "seq", self.up)
            from_right = lax.ppermute(send_down, "seq", self.down)
        return piece(0) + from_left.astype(F32) + from_right.astype(F32)


class Fsdp:
    def __init__(self, size):
        self.size = size
        self.across = size // 2
        index = lax.axis_index("fsdp")
        self.x = index // 2
        self.core = index % 2
        self.swap = [(i, i ^ 1) for i in range(size)]

    def shift(self, step):
        return [(x * 2 + c, (x + step) % self.across * 2 + c) for x in range(self.across) for c in (0, 1)]

    def gather(self, block, dim):
        width = block.shape[dim]
        shape = list(block.shape)
        shape[dim] = width * self.size
        whole = jnp.zeros(shape, block.dtype)
        for step in range(self.across):
            mine = lax.ppermute(block, "fsdp", self.shift(step)) if step else block
            owner = lax.rem(self.x - step + self.across, self.across) * 2
            other = lax.ppermute(mine, "fsdp", self.swap)
            whole = lax.dynamic_update_slice_in_dim(whole, mine, (owner + self.core) * width, dim)
            whole = lax.dynamic_update_slice_in_dim(whole, other, (owner + 1 - self.core) * width, dim)
        return whole

    def scatter(self, whole, dim):
        width = whole.shape[dim] // self.size

        def piece(x, core):
            return lax.dynamic_slice_in_dim(whole, (x * 2 + core) * width, width, dim)

        total = None
        for step in range(self.across):
            x = lax.rem(self.x + step, self.across)
            other = lax.ppermute(piece(x, 1 - self.core), "fsdp", self.swap)
            both = piece(x, self.core).astype(F32) + other.astype(F32)
            if step:
                both = lax.ppermute(both.astype(BF16), "fsdp", self.shift(step)).astype(F32)
            total = both if total is None else total + both
        return total


def doubling_gather(block, counts):
    me = lax.axis_index(ALL)
    bit = 1
    while bit < counts:
        other = lax.ppermute(block, ALL, [(i, i ^ bit) for i in range(counts)])
        low = (me & bit) == 0
        block = jnp.concatenate(
            [jnp.where(low, block, other), jnp.where(low, other, block)], axis=0
        )
        bit *= 2
    return block


def halving_scatter(block, counts):
    me = lax.axis_index(ALL)
    bit = counts // 2
    while bit:
        half = block.shape[0] // 2
        low = (me & bit) == 0
        keep = jnp.where(low, block[:half], block[half:])
        send = jnp.where(low, block[half:], block[:half])
        block = keep + lax.ppermute(send, ALL, [(i, i ^ bit) for i in range(counts)])
        bit //= 2
    return block


def on_device(
    tokens,
    cotangent,
    expert_ids,
    attn_gain,
    w_query,
    w_key,
    w_value,
    query_gain,
    key_gain,
    w_output,
    mlp_gain,
    w_router,
    w_gate,
    w_up,
    w_down,
):
    groups = lax.axis_size("seq")
    splits = lax.axis_size("fsdp")
    counts = groups * splits
    ring, fsdp = Ring(groups), Fsdp(splits)
    seat = lax.axis_index("seq")
    tok_rows, model_width = tokens.shape
    own_rows = w_query.shape[0]
    head_size = query_gain.shape[0] * counts
    heads_all = w_query.shape[1] // head_size
    kv_heads = w_key.shape[1] // head_size
    head_local = heads_all // groups
    copies = groups // kv_heads
    query_width = head_local * head_size
    experts_all = w_router.shape[1]
    local_experts, _, ff = w_gate.shape
    seq_rows = tok_rows * groups
    scale_qk = 1.0 / math.sqrt(head_size)

    tokens_all = ring.gather(tokens)

    packed = jnp.concatenate(
        [query_gain, key_gain, mlp_gain, w_router.reshape(-1)], axis=0
    )[None, :]
    packed = doubling_gather(packed, counts)
    cuts = [query_gain.shape[0], key_gain.shape[0], own_rows, own_rows * experts_all]
    ends = [sum(cuts[: i + 1]) for i in range(4)]
    gain_q = packed[:, : ends[0]].reshape(-1).astype(F32)
    gain_k = packed[:, ends[0] : ends[1]].reshape(-1).astype(F32)
    gain_mlp = packed[:, ends[1] : ends[2]].reshape(-1).astype(F32)
    router_w = packed[:, ends[2] :].reshape(model_width, experts_all)
    ids_all = lax.all_gather(expert_ids, "seq", axis=0, tiled=True)

    gain_rows = attn_gain.astype(F32)[:, None, None]
    weights_own = jnp.concatenate(
        [
            w_query.reshape(own_rows, groups, query_width),
            jnp.repeat(w_key.reshape(own_rows, kv_heads, head_size), copies, axis=1),
            jnp.repeat(w_value.reshape(own_rows, kv_heads, head_size), copies, axis=1),
        ],
        axis=2,
    )
    scaled = (weights_own.astype(F32) * gain_rows).astype(BF16)
    qkv_width = query_width + 2 * head_size
    qkv_w = lax.all_to_all(
        scaled.transpose(1, 0, 2), "seq", split_axis=0, concat_axis=0, tiled=True
    ).reshape(groups * own_rows, qkv_width)
    qkv_w = fsdp.gather(qkv_w, 0)

    me = lax.axis_index(ALL)
    out_rows = w_output.shape[0]
    chunk = model_width // splits
    held = jnp.zeros((splits * out_rows, chunk), BF16)
    my_split = lax.axis_index("fsdp")
    for step in range(splits):
        perm = [(b, ((b % splits + step) % splits) * groups + b // splits) for b in range(counts)]
        target = lax.rem(me + step, splits)
        piece = lax.dynamic_slice_in_dim(w_output, target * chunk, chunk, 1)
        piece = lax.ppermute(piece, ALL, perm)
        origin = lax.rem(my_split - step + splits, splits)
        held = lax.dynamic_update_slice_in_dim(held, piece, origin * out_rows, 0)
    output_w = fsdp.gather(held, 1)

    gate_w = fsdp.gather(w_gate, 1)
    up_w = fsdp.gather(w_up, 1)
    down_w = fsdp.gather(w_down, 2)

    positions = jnp.arange(seq_rows, dtype=jnp.int32).astype(F32)
    cos_table, sine_table = rotary_tables(positions, head_size)
    normed_all = norm_parts(tokens_all.astype(F32))[0].astype(BF16)
    qkv = jnp.dot(normed_all, qkv_w, preferred_element_type=F32)
    query_pre = qkv[:, :query_width].reshape(seq_rows, head_local, head_size)
    key_pre = qkv[:, query_width : query_width + head_size].reshape(seq_rows, 1, head_size)
    value_seq = qkv[:, query_width + head_size :].astype(BF16)
    query_hat, query_scale = norm_parts(query_pre)
    key_hat, key_scale = norm_parts(key_pre)
    query_seq = rotate(query_hat * gain_q, cos_table, sine_table).astype(BF16)
    key_seq = rotate(key_hat * gain_k, cos_table, sine_table).astype(BF16)[:, 0]

    block_rows = min(512, seq_rows)
    block_count = seq_rows // block_rows
    blocks = []

    def block_scores(query_blk, first):
        limit = first + block_rows
        scores = (
            jnp.einsum("qhd,kd->hqk", query_blk, key_seq[:limit], preferred_element_type=F32)
            * scale_qk
        )
        rows = first + jnp.arange(block_rows, dtype=jnp.int32)
        causal = jnp.arange(limit, dtype=jnp.int32)[None, :] <= rows[:, None]
        return jnp.where(causal[None], scores, NEG_LARGE)

    attended, log_sums = [], []
    for block in range(block_count):
        first = block * block_rows
        scores = block_scores(query_seq[first : first + block_rows], first)
        row_peak = jnp.max(scores, axis=-1, keepdims=True)
        exponent = jnp.exp(scores - row_peak)
        row_total = jnp.sum(exponent, axis=-1, keepdims=True)
        weights_low = (exponent / row_total).astype(BF16)
        attended.append(
            jnp.einsum(
                "hqk,kd->qhd",
                weights_low,
                value_seq[: first + block_rows],
                preferred_element_type=F32,
            )
            .astype(BF16)
            .reshape(block_rows, query_width)
        )
        log_sums.append(row_peak + jnp.log(row_total))
    attended = jnp.concatenate(attended, axis=0)

    inputs = tokens.astype(F32)
    middle = inputs + ring.scatter(jnp.dot(attended, output_w, preferred_element_type=F32))
    normed_m, scale_m = norm_parts(middle)
    mixer_in = (normed_m * gain_mlp).astype(BF16)

    mixer_all = ring.gather(mixer_in)
    cot_all = ring.gather(after(cotangent, tokens_all))

    def shares(rows_in, ids):
        logits = jnp.dot(rows_in, router_w, preferred_element_type=F32)
        chosen = jnp.sum(
            (ids[:, :, None] == jnp.arange(experts_all, dtype=jnp.int32)).astype(F32), axis=1
        )
        masked = jnp.where(chosen > 0, logits, NEG_LARGE)
        grown = jnp.exp(masked - jnp.max(masked, axis=-1, keepdims=True)) * chosen
        return grown / jnp.sum(grown, axis=-1, keepdims=True)

    share_own = shares(mixer_in, expert_ids)
    share_all = shares(mixer_all, ids_all)
    share = lax.dynamic_slice_in_dim(share_all, seat * local_experts, local_experts, 1).T[
        :, :, None
    ]

    gate_pre = jnp.einsum("td,edf->etf", mixer_all, gate_w, preferred_element_type=F32)
    up_pre = jnp.einsum("td,edf->etf", mixer_all, up_w, preferred_element_type=F32)
    down_back = jnp.einsum("td,efd->etf", cot_all, down_w, preferred_element_type=F32)
    sigmoid = jax.nn.sigmoid(gate_pre)
    silu_gate = gate_pre * sigmoid
    active = silu_gate * up_pre
    grad_share = jnp.sum(active * down_back, axis=-1)
    active_shared = (active * share).astype(BF16)
    grad_active = down_back * share
    grad_up_pre = (grad_active * silu_gate).astype(BF16)
    grad_gate_pre = (
        grad_active * up_pre * sigmoid * (1.0 + gate_pre * (1.0 - sigmoid))
    ).astype(BF16)
    grad_entered = jnp.einsum(
        "etf,edf->td", grad_gate_pre, gate_w, preferred_element_type=F32
    ) + jnp.einsum("etf,edf->td", grad_up_pre, up_w, preferred_element_type=F32)

    grad_share_own = lax.all_to_all(
        grad_share.reshape(local_experts, groups, tok_rows).transpose(1, 0, 2),
        "seq",
        split_axis=0,
        concat_axis=0,
        tiled=True,
    )
    grad_share_own = grad_share_own.reshape(experts_all, tok_rows).T
    grad_logits = (
        share_own
        * (grad_share_own - jnp.sum(share_own * grad_share_own, axis=-1, keepdims=True))
    ).astype(BF16)

    grad_mixer = ring.scatter(grad_entered) + dot(grad_logits, router_w, 1, 1)
    grad_router = dot(mixer_in, grad_logits, 0, 0)
    grad_gain_m = jnp.sum(grad_mixer * normed_m, axis=0)
    grad_out = cotangent.astype(F32)
    grad_middle = grad_out + norm_back(grad_mixer * gain_mlp, normed_m, scale_m)
    grad_branch = grad_middle.astype(BF16)
    branch_all = ring.gather(grad_branch)

    produced = jnp.einsum("etf,efd->td", active_shared, down_w, preferred_element_type=F32)
    layer_out = (middle + ring.scatter(after(produced, branch_all))).astype(BF16)

    grad_gate = jnp.einsum("td,etf->edf", mixer_all, grad_gate_pre, preferred_element_type=F32)
    grad_up = jnp.einsum("td,etf->edf", mixer_all, grad_up_pre, preferred_element_type=F32)
    grad_down = jnp.einsum("etf,td->efd", active_shared, cot_all, preferred_element_type=F32)
    grad_gate = fsdp.scatter(grad_gate.astype(BF16), 1)
    grad_up = fsdp.scatter(grad_up.astype(BF16), 1)
    grad_down = fsdp.scatter(grad_down.astype(BF16), 2)

    grad_attended = (
        dot(branch_all, output_w, 1, 1).astype(BF16).reshape(seq_rows, head_local, head_size)
    )
    grad_output = dot(attended, branch_all, 0, 0).astype(BF16)
    grad_key_seq = jnp.zeros((seq_rows, head_size), F32)
    grad_value_seq = jnp.zeros((seq_rows, head_size), F32)
    grad_query_seq = []
    for block in range(block_count):
        first = block * block_rows
        limit = first + block_rows
        query_blk = query_seq[first:limit]
        grad_blk = grad_attended[first:limit]
        probs = jnp.exp(block_scores(query_blk, first) - log_sums[block])
        value_part = jnp.einsum(
            "hqk,qhd->kd", probs.astype(BF16), grad_blk, preferred_element_type=F32
        )
        grad_probs = jnp.einsum(
            "qhd,kd->hqk", grad_blk, value_seq[:limit], preferred_element_type=F32
        )
        grad_scores = (
            probs * (grad_probs - jnp.sum(probs * grad_probs, axis=-1, keepdims=True))
        ).astype(BF16)
        grad_query_seq.append(
            jnp.einsum("hqk,kd->qhd", grad_scores, key_seq[:limit], preferred_element_type=F32)
            * scale_qk
        )
        key_part = (
            jnp.einsum("hqk,qhd->kd", grad_scores, query_blk, preferred_element_type=F32)
            * scale_qk
        )
        spare = ((0, seq_rows - limit), (0, 0))
        grad_key_seq = grad_key_seq + jnp.pad(key_part, spare)
        grad_value_seq = grad_value_seq + jnp.pad(value_part, spare)
    grad_query_seq = jnp.concatenate(grad_query_seq, axis=0)

    grad_query_norm = unrotate(grad_query_seq, cos_table, sine_table)
    grad_key_norm = unrotate(grad_key_seq[:, None, :], cos_table, sine_table)
    grad_gain_q = jnp.sum(grad_query_norm * query_hat, axis=(0, 1))
    grad_gain_k = jnp.sum(grad_key_norm * key_hat, axis=(0, 1))
    grad_qkv = jnp.concatenate(
        [
            norm_back(grad_query_norm * gain_q, query_hat, query_scale)
            .astype(BF16)
            .reshape(seq_rows, query_width),
            norm_back(grad_key_norm * gain_k, key_hat, key_scale)
            .astype(BF16)
            .reshape(seq_rows, head_size),
            grad_value_seq.astype(BF16),
        ],
        axis=1,
    )
    grad_normed = ring.scatter(dot(grad_qkv, qkv_w, 1, 1))
    normed_a, scale_a = norm_parts(inputs)
    grad_tokens = (grad_middle + norm_back(grad_normed, normed_a, scale_a)).astype(BF16)

    grad_qkv_w = fsdp.scatter(dot(normed_all, grad_qkv, 0, 0).astype(BF16), 0)
    grad_qkv_w = lax.all_to_all(
        grad_qkv_w.astype(BF16).reshape(groups, own_rows, qkv_width),
        "seq",
        split_axis=0,
        concat_axis=0,
        tiled=True,
    ).astype(F32)
    grad_gain_a = jnp.sum(grad_qkv_w * weights_own.transpose(1, 0, 2).astype(F32), axis=(0, 2))
    grad_qkv_w = grad_qkv_w * attn_gain.astype(F32)[None, :, None]
    grad_query_w = (
        grad_qkv_w[:, :, :query_width].transpose(1, 0, 2).reshape(own_rows, heads_all * head_size)
    )

    def merged(part):
        summed = jnp.sum(part.reshape(kv_heads, copies, own_rows, head_size), axis=1)
        return summed.transpose(1, 0, 2).reshape(own_rows, kv_heads * head_size)

    grad_key_w = merged(grad_qkv_w[:, :, query_width : query_width + head_size])
    grad_value_w = merged(grad_qkv_w[:, :, query_width + head_size :])

    grad_output = fsdp.scatter(grad_output, 1).astype(BF16)
    grad_output_w = jnp.zeros((out_rows, model_width), F32)
    for step in range(splits):
        perm = [(((b % splits + step) % splits) * groups + b // splits, b) for b in range(counts)]
        origin = lax.rem(my_split - step + splits, splits)
        piece = lax.dynamic_slice_in_dim(grad_output, origin * out_rows, out_rows, 0)
        piece = lax.ppermute(piece, ALL, perm).astype(F32)
        target = lax.rem(me + step, splits)
        grad_output_w = lax.dynamic_update_slice_in_dim(grad_output_w, piece, target * chunk, 1)

    small = jnp.concatenate(
        [grad_gain_m[:, None], grad_router], axis=1
    ).reshape(counts, own_rows, 1 + experts_all)
    small = halving_scatter(small, counts)[0]
    gains = jnp.concatenate(
        [grad_gain_q.reshape(counts, -1), grad_gain_k.reshape(counts, -1)], axis=1
    )
    gains = halving_scatter(gains, counts)[0]
    cut = query_gain.shape[0]
    return (
        layer_out,
        grad_tokens,
        grad_gain_a,
        grad_query_w,
        grad_key_w,
        grad_value_w,
        gains[:cut],
        gains[cut:],
        grad_output_w,
        small[:, 0],
        small[:, 1:],
        grad_gate,
        grad_up,
        grad_down,
    )


def solution(mesh):
    rows = P(("fsdp", "seq"), None)
    line = P(("fsdp", "seq"))
    wide = P("seq", "fsdp", None)
    deep = P("seq", None, "fsdp")
    in_specs = (
        rows, rows, rows, line, rows, rows, rows, line, line, rows, line, rows, wide, wide, deep,
    )
    out_specs = (
        rows, rows, line, rows, rows, rows, line, line, rows, line, rows, wide, wide, deep,
    )
    return jax.shard_map(
        on_device, mesh=mesh, in_specs=in_specs, out_specs=out_specs, check_vma=False
    )
```

time: 3080 us -> 920 us (0.30)
  waiting for transfers between devices: 2190 us -> 339 us
  blocking collectives: 272 us -> 30.4 us
  starting transfers between devices: 49.8 us -> 169 us
  local copies, waits for them, and re-layouts: 216 us -> 108 us
  matrix products: 238 us -> 161 us
    reduce_scatter x7 -> x0, waiting for transfers between devices: 1580 us -> none  [the longest x1 709 us: on_device(): lax.psum_scatter(grad_query_w, ('fsdp', 'seq'), scatter_dimension=0, tile...]
    all_to_all x11 -> x3, waiting for transfers between devices: 400 us -> 2.17 us  [the longest x1 2.17 us: on_device(): lax.all_to_all(grad_share.reshape(local_experts, groups, tok_rows).transp...]
    ppermute x0 -> x117, waiting for transfers between devices: none -> 337 us  [the longest x12 85.2 us: scatter(): from_right = lax.ppermute(send_down, 'seq', self.down)]
    all_gather x7 -> x0, waiting for transfers between devices: 213 us -> none  [the longest x1 111 us: on_device(): lax.all_gather(w_query, ('fsdp', 'seq'), axis=0, tiled=True)]
    ppermute x0 -> x117, starting transfers between devices: none -> 153 us  [the longest x4 21.3 us: on_device(): piece = lax.ppermute(piece, ALL, perm).astype(F32)]
    all_gather x1, blocking collectives: 179 us -> 30.4 us  [on_device(): ids_all = lax.all_gather(expert_ids, 'seq', axis=0, tiled=True)]
    unnamed x2 -> x0, blocking collectives: 82.4 us -> none
    dot_general x37 -> x31, matrix products: 237 us -> 161 us  [the longest x6 27.2 us: dot(): lax.dot_general(left, right, (((left_dim,), (right_dim,)), ((), ())), pre...]
  transfers between devices with their start and end apart: 26 -> 120, of which waited for: 17 -> 58; matrix products, arithmetic and copies ran while one was open for 15% -> 25% of each run, Pallas kernels for 0% -> 0%
where the time goes in v1:
time: 920 us; the launch traced here: 907 us
  waiting for transfers between devices  339 us (37%)
  starting transfers between devices  169 us (18%)
  matrix products  161 us (18%)
  local copies, waits for them, and re-layouts  108 us (12%)
  other arithmetic  85.9 us (9%)
  blocking collectives  30.4 us (3%)
  between operations  13.9 us (2%)
    ppermute x12, waiting for transfers between devices, scatter(): from_right = lax.ppermute(send_down, 'seq', self.down)  85.2 us
    ppermute x5, waiting for transfers between devices, scatter(): both = lax.ppermute(both.astype(BF16), 'fsdp', self.shift(step)).astype(F32)  61.7 us
    ppermute x12, waiting for transfers between devices, gather(): from_left = lax.ppermute(from_left, 'seq', self.up)  44.8 us
    ppermute x5, waiting for transfers between devices, gather(): mine = lax.ppermute(block, 'fsdp', self.shift(step)) if step else block  35.3 us
    all_gather x1, blocking collectives, on_device(): ids_all = lax.all_gather(expert_ids, 'seq', axis=0, tiled=True)  30.4 us
    ppermute x12, waiting for transfers between devices, scatter(): from_left = lax.ppermute(send_up, 'seq', self.up)  29.7 us
    dot_general x6, matrix products, dot(): lax.dot_general(left, right, (((left_dim,), (right_dim,)), ((), ())), pre...  27.2 us
    ppermute x4, starting transfers between devices, on_device(): piece = lax.ppermute(piece, ALL, perm).astype(F32)  21.3 us
  transfers between devices with their start and end apart: 120, of which 58 were waited for; matrix products, arithmetic and copies ran while one was open for 25% of the time, Pallas kernels for 0%

profile of v1, /device:TPU:0, one launch (start us, length us, event | category | flops | bytes accessed | tf_op | source)
XLA Modules:
  0.0 907.1 jit_solution(4196816638583925688)
XLA Ops:
  8.5 6.3 all-to-all-start
  49.5 30.4 %all_gather.3 = s32[1024,8]{0,1:T(8,128)S(1)} all-gather(s32[128,8]{0,1:T(8,128)S(1)} %copy-done.72), channel_id=1, replica_groups=mesh['fsdp'=4,'seq'=8] {'seq'}, dimensions={0}, use_global_device_ids=true | all-gather | bytes 36864 | tf_op jit(solution)/shard_map/all_gather | solution.py:246
  157.6 19.0 %collective-permute-done.9 = bf16[512,768]{1,0:T(8,128)(2,1)S(1)} collective-permute-done((bf16[512,768]{1,0:T(8,128)(2,1)S(1)}, bf16[512,768]{1,0:T(8,128)(2,1)S(1)}, u32[]{:S(2)}, u32[]{:S(2)}) %collective-permute-start.9) | collective-permute-done | bytes 786464 | tf_op jit(solution)/shard_map/ppermute | solution.py:149
  181.9 8.3 fusion.130
  252.9 14.2 %collective-permute-done.43 = bf16[2,512,768]{2,1,0:T(8,128)(2,1)S(1)} collective-permute-done((bf16[2,512,768]{2,1,0:T(8,128)(2,1)}, bf16[2,512,768]{2,1,0:T(8,128)(2,1)S(1)}, u32[]{:S(2)}, u32[]{:S(2)}) %collective-permute-start.43) | collective-permute-done | bytes 1572896 | tf_op jit(solution)/shard_map/ppermute | solution.py:149
  292.5 7.3 collective-permute-done.28
  305.6 9.3 %collective-permute-done.29 = bf16[128,2048]{1,0:T(8,128)(2,1)S(1)} collective-permute-done((bf16[128,2048]{1,0:T(8,128)(2,1)S(1)}, bf16[128,2048]{1,0:T(8,128)(2,1)S(1)}, u32[]{:S(2)}, u32[]{:S(2)}) %collective-permute-start.29) | collective-permute-done | bytes 524320 | tf_op jit(solution)/shard_map/ppermute | solution.py:127
  319.7 6.4 collective-permute-done.53
  328.7 8.6 collective-permute-done.30
  343.0 10.8 %collective-permute-done.34 = bf16[128,2048]{1,0:T(8,128)(2,1)S(1)} collective-permute-done((bf16[128,2048]{1,0:T(8,128)(2,1)S(1)}, bf16[128,2048]{1,0:T(8,128)(2,1)S(1)}, u32[]{:S(2)}, u32[]{:S(2)}) %collective-permute-start.34) | collective-permute-done | bytes 524320 | tf_op jit(solution)/shard_map/ppermute | solution.py:100
  355.8 8.9 fusion.21
  367.7 9.8 %collective-permute-done.38 = bf16[128,2048]{1,0:T(8,128)(2,1)S(1)} collective-permute-done((bf16[128,2048]{1,0:T(8,128)(2,1)S(1)}, bf16[128,2048]{1,0:T(8,128)(2,1)S(1)}, u32[]{:S(2)}, u32[]{:S(2)}) %collective-permute-start.38) | collective-permute-done | bytes 524320 | tf_op jit(solution)/shard_map/ppermute | solution.py:100
  386.9 9.1 fusion.27
  396.1 17.7 %fusion.10 = (bf16[2,1024,768]{1,2,0:T(8,128)(2,1)S(1)}, f32[2,1024]{1,0:T(2,128)}, bf16[2,1024,768]{1,2,0:T(8,128)(2,1)}, bf16[2,1024,768]{1,2,0:T(8,128)(2,1)}) fusion(f32[2,768,1024]{2,1,0:T(8,128)} %fusion.27, f32[2,768,1024]{2,1,0:T(8,128)} %fusion.21, f32[2,1024]{1,0:T(2,128)S(1)} %fusion.108, ...), kind=kOutput, calls=%fused_computation.23 | convolution fusion | flops 6472333312 | bytes 32522240 | tf_op jit(solution)/shard_map/td,edf->etf/dot_general | solution.py:353
  413.8 12.0 %fusion.134 = f32[1024,2048,1]{1,0,2:T(8,128)} fusion(bf16[2,1024,768]{1,2,0:T(8,128)(2,1)S(1)} %get-tuple-element.109, bf16[2,2048,768]{2,1,0:T(8,128)(2,1)} %copy-done.23), kind=kOutput, calls=%fused_computation.405 | convolution fusion | flops 6442450944 | bytes 17825792 | tf_op jit(solution)/shard_map/etf,edf->td/dot_general | solution.py:365
  425.8 10.6 %bitcast_add_fusion = f32[1024,2048]{1,0:T(8,128)S(1)} fusion(f32[1024,2048,1]{1,0,2:T(8,128)} %fusion.134, bf16[2,1024,768]{1,2,0:T(8,128)(2,1)S(1)} %copy-done.97, bf16[2,2048,768]{2,1,0:T(8,128)(2,1)} %constant_dynamic-update-slice_fusion.22), kind=kOutput, calls=%fused_computation.9 | convolution fusion | flops 6444548096 | bytes 26214400 | tf_op jit(solution)/shard_map/etf,edf->td/dot_general | solution.py:367
  445.9 12.0 %convolution_bitcast_fusion = f32[1024,2048]{1,0:T(8,128)} fusion(bf16[2,1024,768]{1,2,0:T(8,128)(2,1)} %get-tuple-element.112, bf16[2,768,2048]{2,1,0:T(8,128)(2,1)} %copy-done.21), kind=kOutput, calls=%fused_computation.36 | convolution fusion | flops 6442450944 | bytes 17825792 | tf_op jit(solution)/shard_map/etf,efd->td/dot_general | solution.py:390
  459.6 8.7 convolution_convert_fusion
  470.9 7.3 convolution_convert_fusion.1
  486.4 7.1 convolution_convert_fusion.2
  509.1 7.4 collective-permute-done.59
  555.2 13.6 %collective-permute-done.113 = bf16[2,512,768]{1,2,0:T(8,128)(2,1)S(1)} collective-permute-done((bf16[2,512,768]{1,2,0:T(8,128)(2,1)S(1)}, bf16[2,512,768]{1,2,0:T(8,128)(2,1)S(1)}, u32[]{:S(2)}, u32[]{:S(2)}) %collective-permute-start.113) | collective-permute-done | bytes 1572896 | tf_op jit(solution)/shard_map/ppermute | solution.py:168
  576.8 25.8 %collective-permute-done.110 = bf16[2,512,768]{1,2,0:T(8,128)(2,1)} collective-permute-done((bf16[2,512,768]{1,2,0:T(8,128)(2,1)}, bf16[2,512,768]{1,2,0:T(8,128)(2,1)}, u32[]{:S(2)}, u32[]{:S(2)}) %collective-permute-start.110) | collective-permute-done | bytes 1572896 | tf_op jit(solution)/shard_map/ppermute | solution.py:168
  613.3 22.3 %collective-permute-done.116 = bf16[2,768,512]{2,1,0:T(8,128)(2,1)} collective-permute-done((bf16[2,768,512]{2,1,0:T(8,128)(2,1)}, bf16[2,768,512]{2,1,0:T(8,128)(2,1)}, u32[]{:S(2)}, u32[]{:S(2)}) %collective-permute-start.116) | collective-permute-done | bytes 1572896 | tf_op jit(solution)/shard_map/ppermute | solution.py:168
  646.6 7.6 collective-permute-done.68
  708.8 7.9 convolution_convert_fusion.3
  755.3 9.2 %collective-permute-done.73 = bf16[128,2048]{1,0:T(8,128)(2,1)S(1)} collective-permute-done((bf16[128,2048]{1,0:T(8,128)(2,1)S(1)}, bf16[128,2048]{1,0:T(8,128)(2,1)S(1)}, u32[]{:S(2)}, u32[]{:S(2)}) %collective-permute-start.73) | collective-permute-done | bytes 524320 | tf_op jit(solution)/shard_map/ppermute | solution.py:126
  779.0 14.3 %collective-permute-start.100 = (bf16[128,512]{1,0:T(8,128)(2,1)S(1)}, bf16[128,512]{1,0:T(8,128)(2,1)S(1)}, u32[]{:S(2)}, u32[]{:S(2)}) collective-permute-start(bf16[128,512]{1,0:T(8,128)(2,1)S(1)} %get-tuple-element.149), channel_id=1, source_target_pairs={{8,0},{16,1},{24,2},{0,3},{9,4},{17,5},{25,6},{1,7},{10,8},{18,9},... | collective-permute-start | bytes 393224 | tf_op jit(solution)/shard_map/ppermute | solution.py:482
  834.1 7.6 collective-permute-done.77
  858.5 12.1 %collective-permute-done.78 = bf16[128,2048]{1,0:T(8,128)(2,1)} collective-permute-done((bf16[128,2048]{1,0:T(8,128)(2,1)}, bf16[128,2048]{1,0:T(8,128)(2,1)}, u32[]{:S(2)}, u32[]{:S(2)}) %collective-permute-start.78) | collective-permute-done | bytes 524320 | tf_op jit(solution)/shard_map/ppermute | solution.py:127
  872.8 16.7 %collective-permute-done.87 = bf16[128,2048]{1,0:T(8,128)(2,1)S(1)} collective-permute-done((bf16[128,2048]{1,0:T(8,128)(2,1)S(1)}, bf16[128,2048]{1,0:T(8,128)(2,1)S(1)}, u32[]{:S(2)}, u32[]{:S(2)}) %collective-permute-start.87) | collective-permute-done | bytes 524320 | tf_op jit(solution)/shard_map/ppermute | solution.py:127
  891.3 7.5 collective-permute-done.79
  (703 shorter events, 517.6 us)
Async XLA Ops:
  0.7 114.9 %collective-permute-start = (bf16[128,2048]{1,0:T(8,128)(2,1)}, bf16[128,2048]{1,0:T(8,128)(2,1)}, u32[]{:S(2)}, u32[]{:S(2)}) collective-permute-start(bf16[128,2048]{1,0:T(8,128)(2,1)} %param.17), channel_id=1, source_target_pairs={{0,1},{1,3},{3,5},{5,7},{7,6},{6,4},{4,2},{2,0},{8,9},{9,11},{11,1... | collective-permute-start | bytes 1572872 | tf_op jit(solution)/shard_map/ppermute | solution.py:100
  3.8 117.2 %collective-permute-start.1 = (bf16[128,2048]{1,0:T(8,128)(2,1)}, bf16[128,2048]{1,0:T(8,128)(2,1)S(1)}, u32[]{:S(2)}, u32[]{:S(2)}) collective-permute-start(bf16[128,2048]{1,0:T(8,128)(2,1)} %param.17), channel_id=1, source_target_pairs={{0,2},{1,0},{3,1},{5,3},{7,5},{6,7},{4,6},{2,4},{8,10},{9,8},{11,9... | collective-permute-start | bytes 1572872 | tf_op jit(solution)/shard_map/ppermute | solution.py:101
  8.5 131.9 %all-to-all-start = ((bf16[8,64,768]{2,1,0:T(8,128)(2,1)}), bf16[8,64,768]{2,1,0:T(8,128)(2,1)S(1)}, u32[]{:S(2)}, u32[]{:S(2)}) async-start(bf16[8,64,768]{2,1,0:T(8,128)(2,1)} %fusion.77), calls=%async_computation | async-start | bytes 1572864 | tf_op jit(solution)/shard_map/all_to_all | solution.py:259
  15.2 32.7 %collective-permute-start.11 = (bf16[1,1096]{1,0:T(2,128)(2,1)S(1)}, bf16[1,1096]{1,0:T(2,128)(2,1)S(1)}, u32[]{:S(2)}, u32[]{:S(2)}) collective-permute-start(bf16[1,1096]{1,0:T(2,128)(2,1)S(1)} %broadcast_in_dim.64), channel_id=1, source_target_pairs={{0,1},{1,0},{2,3},{3,2},{4,5},{5,4},{6,7},{7,6},{8,9},{9,8},{10,11... | collective-permute-start | bytes 6584 | tf_op jit(solution)/shard_map/ppermute | solution.py:177
  18.0 78.3 %collective-permute-start.16 = (bf16[128,512]{1,0:T(8,128)(2,1)S(1)}, bf16[128,512]{1,0:T(8,128)(2,1)S(1)}, u32[]{:S(2)}, u32[]{:S(2)}) collective-permute-start(bf16[128,512]{1,0:T(8,128)(2,1)S(1)} %get-tuple-element.162), channel_id=1, source_target_pairs={{0,0},{1,8},{2,16},{3,24},{4,1},{5,9},{6,17},{7,25},{8,2},{9,10},{... | collective-permute-start | bytes 393224 | tf_op jit(solution)/shard_map/ppermute | solution.py:273
  18.7 201.8 %collective-permute-start.45 = (bf16[2,768,512]{2,1,0:T(8,128)(2,1)}, bf16[2,768,512]{2,1,0:T(8,128)(2,1)}, u32[]{:S(2)}, u32[]{:S(2)}) collective-permute-start(bf16[2,768,512]{2,1,0:T(8,128)(2,1)} %param.31), channel_id=1, source_target_pairs={{0,8},{8,0},{16,24},{24,16},{1,9},{9,1},{17,25},{25,17},{2,10},{10... | collective-permute-start | bytes 4718600 | tf_op jit(solution)/shard_map/ppermute | solution.py:151
  47.9 32.0 %collective-permute-start.12 = (bf16[2,1096]{1,0:T(2,128)(2,1)S(1)}, bf16[2,1096]{1,0:T(2,128)(2,1)S(1)}, u32[]{:S(2)}, u32[]{:S(2)}) collective-permute-start(bf16[2,1096]{1,0:T(2,128)(2,1)S(1)} %pad_maximum_fusion.17), channel_id=1, source_target_pairs={{0,2},{1,3},{2,0},{3,1},{4,6},{5,7},{6,4},{7,5},{8,10},{9,11},{10,... | collective-permute-start | bytes 13160 | tf_op jit(solution)/shard_map/ppermute | solution.py:177
  123.7 112.3 %collective-permute-start.46 = (bf16[2,768,512]{2,1,0:T(8,128)(2,1)}, bf16[2,768,512]{2,1,0:T(8,128)(2,1)}, u32[]{:S(2)}, u32[]{:S(2)}) collective-permute-start(bf16[2,768,512]{2,1,0:T(8,128)(2,1)} %param.31), channel_id=1, source_target_pairs={{0,16},{8,24},{16,0},{24,8},{1,17},{9,25},{17,1},{25,9},{2,18},{10... | collective-permute-start | bytes 4718600 | tf_op jit(solution)/shard_map/ppermute | solution.py:149
  140.4 36.2 %collective-permute-start.9 = (bf16[512,768]{1,0:T(8,128)(2,1)S(1)}, bf16[512,768]{1,0:T(8,128)(2,1)S(1)}, u32[]{:S(2)}, u32[]{:S(2)}) collective-permute-start(bf16[512,768]{1,0:T(8,128)(2,1)S(1)} %bitcast.348), channel_id=1, source_target_pairs={{0,16},{8,24},{16,0},{24,8},{1,17},{9,25},{17,1},{25,9},{2,18},{10... | collective-permute-start | bytes 2359304 | tf_op jit(solution)/shard_map/ppermute | solution.py:149
  155.6 85.9 %collective-permute-start.31 = (bf16[2,512,768]{2,1,0:T(8,128)(2,1)}, bf16[2,512,768]{2,1,0:T(8,128)(2,1)}, u32[]{:S(2)}, u32[]{:S(2)}) collective-permute-start(bf16[2,512,768]{2,1,0:T(8,128)(2,1)} %param.29), channel_id=1, source_target_pairs={{0,8},{8,0},{16,24},{24,16},{1,9},{9,1},{17,25},{25,17},{2,10},{10... | collective-permute-start | bytes 4718600 | tf_op jit(solution)/shard_map/ppermute | solution.py:151
  179.8 64.7 %collective-permute-start.32 = (bf16[2,512,768]{2,1,0:T(8,128)(2,1)}, bf16[2,512,768]{2,1,0:T(8,128)(2,1)}, u32[]{:S(2)}, u32[]{:S(2)}) collective-permute-start(bf16[2,512,768]{2,1,0:T(8,128)(2,1)} %param.29), channel_id=1, source_target_pairs={{0,16},{8,24},{16,0},{24,8},{1,17},{9,25},{17,1},{25,9},{2,18},{10... | collective-permute-start | bytes 4718600 | tf_op jit(solution)/shard_map/ppermute | solution.py:149
  181.5 65.6 %collective-permute-start.42 = (bf16[2,512,768]{2,1,0:T(8,128)(2,1)}, bf16[2,512,768]{2,1,0:T(8,128)(2,1)}, u32[]{:S(2)}, u32[]{:S(2)}) collective-permute-start(bf16[2,512,768]{2,1,0:T(8,128)(2,1)} %param.30), channel_id=1, source_target_pairs={{0,8},{8,0},{16,24},{24,16},{1,9},{9,1},{17,25},{25,17},{2,10},{10... | collective-permute-start | bytes 4718600 | tf_op jit(solution)/shard_map/ppermute | solution.py:151
  231.1 36.0 %collective-permute-start.43 = (bf16[2,512,768]{2,1,0:T(8,128)(2,1)}, bf16[2,512,768]{2,1,0:T(8,128)(2,1)S(1)}, u32[]{:S(2)}, u32[]{:S(2)}) collective-permute-start(bf16[2,512,768]{2,1,0:T(8,128)(2,1)} %param.30), channel_id=1, source_target_pairs={{0,16},{8,24},{16,0},{24,8},{1,17},{9,25},{17,1},{25,9},{2,18},{10... | collective-permute-start | bytes 4718600 | tf_op jit(solution)/shard_map/ppermute | solution.py:149
  241.5 62.2 %collective-permute-start.47 = (bf16[2,768,512]{2,1,0:T(8,128)(2,1)}, bf16[2,768,512]{2,1,0:T(8,128)(2,1)S(1)}, u32[]{:S(2)}, u32[]{:S(2)}) collective-permute-start(bf16[2,768,512]{2,1,0:T(8,128)(2,1)} %collective-permute-done.46), channel_id=1, source_target_pairs={{0,8},{8,0},{16,24},{24,16},{1,9},{9,1},{17,25},{25,17},{2,10},{10... | collective-permute-start | bytes 4718600 | tf_op jit(solution)/shard_map/ppermute | solution.py:151
  272.6 43.3 %collective-permute-start.33 = (bf16[2,512,768]{2,1,0:T(8,128)(2,1)}, bf16[2,512,768]{2,1,0:T(8,128)(2,1)S(1)}, u32[]{:S(2)}, u32[]{:S(2)}) collective-permute-start(bf16[2,512,768]{2,1,0:T(8,128)(2,1)} %collective-permute-done.32), channel_id=1, source_target_pairs={{0,8},{8,0},{16,24},{24,16},{1,9},{9,1},{17,25},{25,17},{2,10},{10... | collective-permute-start | bytes 4718600 | tf_op jit(solution)/shard_map/ppermute | solution.py:151
  495.9 32.6 %collective-permute-start.112 = (bf16[2,512,768]{1,2,0:T(8,128)(2,1)}, bf16[2,512,768]{1,2,0:T(8,128)(2,1)}, u32[]{:S(2)}, u32[]{:S(2)}) collective-permute-start(bf16[2,512,768]{1,2,0:T(8,128)(2,1)} %get-tuple-element.124), channel_id=1, source_target_pairs={{0,8},{8,0},{16,24},{24,16},{1,9},{9,1},{17,25},{25,17},{2,10},{10... | collective-permute-start | bytes 4718600 | tf_op jit(solution)/shard_map/ppermute | solution.py:165
  498.2 34.5 %collective-permute-start.109 = (bf16[2,512,768]{1,2,0:T(8,128)(2,1)}, bf16[2,512,768]{1,2,0:T(8,128)(2,1)}, u32[]{:S(2)}, u32[]{:S(2)}) collective-permute-start(bf16[2,512,768]{1,2,0:T(8,128)(2,1)} %get-tuple-element.126), channel_id=1, source_target_pairs={{0,8},{8,0},{16,24},{24,16},{1,9},{9,1},{17,25},{25,17},{2,10},{10... | collective-permute-start | bytes 4718600 | tf_op jit(solution)/shard_map/ppermute | solution.py:165
  531.6 37.2 %collective-permute-start.113 = (bf16[2,512,768]{1,2,0:T(8,128)(2,1)S(1)}, bf16[2,512,768]{1,2,0:T(8,128)(2,1)S(1)}, u32[]{:S(2)}, u32[]{:S(2)}) collective-permute-start(bf16[2,512,768]{1,2,0:T(8,128)(2,1)S(1)} %fusion.33), channel_id=1, source_target_pairs={{0,16},{8,24},{16,0},{24,8},{1,17},{9,25},{17,1},{25,9},{2,18},{10... | collective-permute-start | bytes 4718600 | tf_op jit(solution)/shard_map/ppermute | solution.py:168
  538.1 64.5 %collective-permute-start.110 = (bf16[2,512,768]{1,2,0:T(8,128)(2,1)}, bf16[2,512,768]{1,2,0:T(8,128)(2,1)}, u32[]{:S(2)}, u32[]{:S(2)}) collective-permute-start(bf16[2,512,768]{1,2,0:T(8,128)(2,1)} %fusion.35), channel_id=1, source_target_pairs={{0,16},{8,24},{16,0},{24,8},{1,17},{9,25},{17,1},{25,9},{2,18},{10... | collective-permute-start | bytes 4718600 | tf_op jit(solution)/shard_map/ppermute | solution.py:168
  545.3 68.0 %collective-permute-start.114 = (bf16[2,768,512]{2,1,0:T(8,128)(2,1)}, bf16[2,768,512]{2,1,0:T(8,128)(2,1)}, u32[]{:S(2)}, u32[]{:S(2)}) collective-permute-start(bf16[2,768,512]{2,1,0:T(8,128)(2,1)} %get-tuple-element.121), channel_id=1, source_target_pairs={{0,8},{8,0},{16,24},{24,16},{1,9},{9,1},{17,25},{25,17},{2,10},{10... | collective-permute-start | bytes 4718600 | tf_op jit(solution)/shard_map/ppermute | solution.py:165
  547.5 88.0 %collective-permute-start.116 = (bf16[2,768,512]{2,1,0:T(8,128)(2,1)}, bf16[2,768,512]{2,1,0:T(8,128)(2,1)}, u32[]{:S(2)}, u32[]{:S(2)}) collective-permute-start(bf16[2,768,512]{2,1,0:T(8,128)(2,1)} %add_convert_fusion), channel_id=1, source_target_pairs={{0,16},{8,24},{16,0},{24,8},{1,17},{9,25},{17,1},{25,9},{2,18},{10... | collective-permute-start | bytes 4718600 | tf_op jit(solution)/shard_map/ppermute | solution.py:168
  553.7 57.2 %collective-permute-start.64 = (bf16[128,2048]{1,0:T(8,128)(2,1)}, bf16[128,2048]{1,0:T(8,128)(2,1)S(1)}, u32[]{:S(2)}, u32[]{:S(2)}) collective-permute-start(bf16[128,2048]{1,0:T(8,128)(2,1)} %get-tuple-element.99), channel_id=1, source_target_pairs={{0,1},{1,3},{3,5},{5,7},{7,6},{6,4},{4,2},{2,0},{8,9},{9,11},{11,1... | collective-permute-start | bytes 1572872 | tf_op jit(solution)/shard_map/ppermute | solution.py:100
  568.8 43.5 %collective-permute-start.65 = (bf16[128,2048]{1,0:T(8,128)(2,1)}, bf16[128,2048]{1,0:T(8,128)(2,1)}, u32[]{:S(2)}, u32[]{:S(2)}) collective-permute-start(bf16[128,2048]{1,0:T(8,128)(2,1)} %get-tuple-element.99), channel_id=1, source_target_pairs={{0,2},{1,0},{3,1},{5,3},{7,5},{6,7},{4,6},{2,4},{8,10},{9,8},{11,9... | collective-permute-start | bytes 1572872 | tf_op jit(solution)/shard_map/ppermute | solution.py:101
  723.6 50.4 %collective-permute-start.96 = (bf16[512,512]{1,0:T(8,128)(2,1)}, bf16[512,512]{1,0:T(8,128)(2,1)}, u32[]{:S(2)}, u32[]{:S(2)}) collective-permute-start(bf16[512,512]{1,0:T(8,128)(2,1)} %get-tuple-element.135), channel_id=1, source_target_pairs={{0,8},{8,0},{16,24},{24,16},{1,9},{9,1},{17,25},{25,17},{2,10},{10... | collective-permute-start | bytes 1572872 | tf_op jit(solution)/shard_map/ppermute | solution.py:165
  727.4 50.7 %collective-permute-start.89 = (bf16[512,768]{1,0:T(8,128)(2,1)S(1)}, bf16[512,768]{1,0:T(8,128)(2,1)S(1)}, u32[]{:S(2)}, u32[]{:S(2)}) collective-permute-start(bf16[512,768]{1,0:T(8,128)(2,1)S(1)} %get-tuple-element.130), channel_id=1, source_target_pairs={{0,8},{8,0},{16,24},{24,16},{1,9},{9,1},{17,25},{25,17},{2,10},{10... | collective-permute-start | bytes 2359304 | tf_op jit(solution)/shard_map/ppermute | solution.py:165
  753.2 90.7 %collective-permute-start.88 = (bf16[512,768]{1,0:T(8,128)(2,1)S(1)}, bf16[512,768]{1,0:T(8,128)(2,1)S(1)}, u32[]{:S(2)}, u32[]{:S(2)}) collective-permute-start(bf16[512,768]{1,0:T(8,128)(2,1)S(1)} %get-tuple-element.129), channel_id=1, source_target_pairs={{0,8},{8,0},{16,24},{24,16},{1,9},{9,1},{17,25},{25,17},{2,10},{10... | collective-permute-start | bytes 2359304 | tf_op jit(solution)/shard_map/ppermute | solution.py:165
  772.7 33.2 %collective-permute-start.76 = (bf16[64,2048]{1,0:T(8,128)(2,1)S(1)}, bf16[64,2048]{1,0:T(8,128)(2,1)S(1)}, u32[]{:S(2)}, u32[]{:S(2)}) collective-permute-start(bf16[64,2048]{1,0:T(8,128)(2,1)S(1)} %get-tuple-element.155), channel_id=1, source_target_pairs={{0,2},{1,0},{3,1},{5,3},{7,5},{6,7},{4,6},{2,4},{8,10},{9,8},{11,9... | collective-permute-start | bytes 786440 | tf_op jit(solution)/shard_map/ppermute | solution.py:119
  801.2 44.7 %collective-permute-start.90 = (bf16[512,768]{1,0:T(8,128)(2,1)S(1)}, bf16[512,768]{1,0:T(8,128)(2,1)S(1)}, u32[]{:S(2)}, u32[]{:S(2)}) collective-permute-start(bf16[512,768]{1,0:T(8,128)(2,1)S(1)} %add_convert_fusion.3), channel_id=1, source_target_pairs={{0,16},{8,24},{16,0},{24,8},{1,17},{9,25},{17,1},{25,9},{2,18},{10... | collective-permute-start | bytes 2359304 | tf_op jit(solution)/shard_map/ppermute | solution.py:168
  805.9 66.1 %collective-permute-start.102 = (bf16[128,512]{1,0:T(8,128)(2,1)}, bf16[128,512]{1,0:T(8,128)(2,1)S(1)}, u32[]{:S(2)}, u32[]{:S(2)}) collective-permute-start(bf16[128,512]{1,0:T(8,128)(2,1)} %get-tuple-element.147), channel_id=1, source_target_pairs={{24,0},{0,1},{8,2},{16,3},{25,4},{1,5},{9,6},{17,7},{26,8},{2,9},{... | collective-permute-start | bytes 393224 | tf_op jit(solution)/shard_map/ppermute | solution.py:482
  831.1 60.2 %collective-permute-start.75 = (bf16[128,2048]{1,0:T(8,128)(2,1)}, bf16[128,2048]{1,0:T(8,128)(2,1)}, u32[]{:S(2)}, u32[]{:S(2)}) collective-permute-start(bf16[128,2048]{1,0:T(8,128)(2,1)} %get-tuple-element.115), channel_id=1, source_target_pairs={{0,1},{1,3},{3,5},{5,7},{7,6},{6,4},{4,2},{2,0},{8,9},{9,11},{11,1... | collective-permute-start | bytes 1572872 | tf_op jit(solution)/shard_map/ppermute | solution.py:126
  847.1 55.6 %all-to-all-start.2 = ((bf16[8,64,768]{2,1,0:T(8,128)(2,1)}), bf16[8,64,768]{2,1,0:T(8,128)(2,1)}, u32[]{:S(2)}, u32[]{:S(2)}) async-start(bf16[8,64,768]{2,1,0:T(8,128)(2,1)} %bitcast.351), calls=%async_computation.2 | async-start | bytes 1572864 | tf_op jit(solution)/shard_map/all_to_all | solution.py:456
  858.4 31.1 %collective-permute-start.87 = (bf16[128,2048]{1,0:T(8,128)(2,1)S(1)}, bf16[128,2048]{1,0:T(8,128)(2,1)S(1)}, u32[]{:S(2)}, u32[]{:S(2)}) collective-permute-start(bf16[128,2048]{1,0:T(8,128)(2,1)S(1)} %add_convert_fusion.6), channel_id=1, source_target_pairs={{0,2},{1,0},{3,1},{5,3},{7,5},{6,7},{4,6},{2,4},{8,10},{9,8},{11,9... | collective-permute-start | bytes 1572872 | tf_op jit(solution)/shard_map/ppermute | solution.py:127
  (195 other events, 2962.4 us)

commit v2 on v1

v2 whole, which is shorter than its diff:
```python
import math

import jax
import jax.numpy as jnp
import numpy as np
from jax import lax
from jax.experimental import pallas as pl
from jax.experimental.pallas import tpu as pltpu
from jax.sharding import PartitionSpec as P

NORM_EPS = 1e-06
ROPE_BASE = 1000000.0
NEG_LARGE = -1e30
F32 = jnp.float32
BF16 = jnp.bfloat16
ALL = ("fsdp", "seq")
VMEM_LIMIT = 40 * 1024 * 1024
LARGE_LIMIT = 56 * 1024 * 1024
SMALL_LIMIT = 16 * 1024 * 1024


def dot(left, right, left_dim, right_dim):
    return lax.dot_general(
        left, right, (((left_dim,), (right_dim,)), ((), ())), preferred_element_type=F32
    )


def norm_parts(values):
    row_scale = lax.rsqrt(jnp.mean(values * values, axis=-1, keepdims=True) + NORM_EPS)
    return (values * row_scale, row_scale)


def norm_back(grad_normed, normed, row_scale):
    return row_scale * (
        grad_normed - normed * jnp.mean(grad_normed * normed, axis=-1, keepdims=True)
    )


def rotary_tables(positions, head_size):
    half_size = head_size // 2
    frequency = jnp.exp(
        jnp.arange(half_size, dtype=F32) * (-2.0 * math.log(ROPE_BASE) / head_size)
    )
    angles = positions[:, None] * frequency[None, :]
    cosine, sine = jnp.cos(angles), jnp.sin(angles)
    return jnp.concatenate([cosine, cosine], axis=1), jnp.concatenate([-sine, sine], axis=1)


def swap_halves(values):
    return pltpu.roll(values, values.shape[-1] // 2, 1)


def params(limit=VMEM_LIMIT):
    return pltpu.CompilerParams(vmem_limit_bytes=limit)


def take_piece(step, pieces, halved, store):
    last = len(pieces) - (2 if halved else 0)
    for i in range(last):

        @pl.when(step == i)
        def _(i=i):
            store(0, pieces[i][...])

    if halved:

        @pl.when(step == last)
        def _():
            half = pieces[last].shape[0]
            store(0, pieces[last][...])
            store(half, pieces[last + 1][...])


def lay_kernel(count, halved, order_ref, *refs):
    def store(first, rows):
        refs[-1][first : first + rows.shape[0]] = rows

    take_piece(pl.program_id(0), refs[:count], halved, store)


def lay(pieces, order=None):
    halved = order is None
    members = len(pieces) - (1 if halved else 0)
    if halved:
        order = jnp.arange(members, dtype=jnp.int32)
    rows, cols = pieces[0].shape
    return pl.pallas_call(
        lambda *refs: lay_kernel(len(pieces), halved, *refs),
        grid_spec=pltpu.PrefetchScalarGridSpec(
            num_scalar_prefetch=1,
            grid=(members,),
            in_specs=[pl.BlockSpec(piece.shape, lambda i, order: (0, 0)) for piece in pieces],
            out_specs=pl.BlockSpec((rows, cols), lambda i, order: (order[i], 0)),
        ),
        out_shape=jax.ShapeDtypeStruct((members * rows, cols), pieces[0].dtype),
        compiler_params=params(),
        cost_estimate=pl.CostEstimate(
            flops=0, bytes_accessed=4 * members * rows * cols, transcendentals=0
        ),
    )(order, *pieces)


def project_kernel(heads, parts, count, order_ref, *refs):
    pieces, refs = refs[:count], refs[count:]
    weights, refs = refs[:parts], refs[parts:]
    cos_ref, sin_ref, gain_ref, n_ref, pre_ref, q_ref, k_ref, v_ref = refs
    size = cos_ref.shape[1]

    def store(first, rows):
        n_ref[first : first + rows.shape[0]] = norm_parts(rows.astype(F32))[0].astype(BF16)

    take_piece(pl.program_id(0), pieces, True, store)
    depth = weights[0].shape[0]
    projected = 0.0
    for part, w_ref in enumerate(weights):
        columns = pl.ds(pl.multiple_of(order_ref[part] * depth, depth), depth)
        projected += jnp.dot(n_ref[:, columns], w_ref[...], preferred_element_type=F32)
    pre_ref[...] = projected[:, : (heads + 1) * size]
    for head in range(heads + 1):
        row = 0 if head < heads else 1
        scaled = norm_parts(projected[:, head * size : (head + 1) * size])[0] * gain_ref[row : row + 1]
        turned = (scaled * cos_ref[...] + swap_halves(scaled) * sin_ref[...]).astype(BF16)
        if head < heads:
            q_ref[:, head * size : (head + 1) * size] = turned
        else:
            k_ref[...] = turned
    v_ref[...] = projected[:, (heads + 1) * size :].astype(BF16)


def project(pieces, weights, order, width, cos_table, sine_table, gains):
    block, depth = pieces[0].shape
    rows = block * (len(pieces) - 1)
    size = cos_table.shape[1]
    heads = width // size - 2
    spec = lambda cols: pl.BlockSpec((block, cols), lambda i, order: (i, 0))
    whole = lambda shape: pl.BlockSpec(shape, lambda i, order: (0, 0))
    return pl.pallas_call(
        lambda *refs: project_kernel(heads, len(weights), len(pieces), *refs),
        grid_spec=pltpu.PrefetchScalarGridSpec(
            num_scalar_prefetch=1,
            grid=(rows // block,),
            in_specs=[whole(piece.shape) for piece in pieces]
            + [whole((part.shape[0], width)) for part in weights]
            + [spec(size), spec(size), whole(gains.shape)],
            out_specs=[
                spec(depth), spec((heads + 1) * size), spec(heads * size), spec(size), spec(size),
            ],
        ),
        out_shape=[
            jax.ShapeDtypeStruct((rows, depth), BF16),
            jax.ShapeDtypeStruct((rows, (heads + 1) * size), F32),
            jax.ShapeDtypeStruct((rows, heads * size), BF16),
            jax.ShapeDtypeStruct((rows, size), BF16),
            jax.ShapeDtypeStruct((rows, size), BF16),
        ],
        compiler_params=params(LARGE_LIMIT),
        cost_estimate=pl.CostEstimate(
            flops=2 * rows * depth * width, bytes_accessed=16 << 20, transcendentals=0
        ),
    )(order, *pieces, *weights, cos_table, sine_table, gains)


def fetch(arrays, spots, buffers, sems):
    rows = buffers[0].shape[0]
    copies = [
        pltpu.make_async_copy(array.at[pl.ds(spot * rows, rows)], buffer, sems.at[i])
        for i, (array, spot, buffer) in enumerate(zip(arrays, spots, buffers))
    ]
    for copy in copies:
        copy.start()
    for copy in copies:
        copy.wait()


def ring_add_kernel(spots, up_hbm, down_hbm, left_ref, right_ref, up_ref, down_ref, up_buf, down_buf, sems):
    fetch((up_hbm, down_hbm), spots, (up_buf, down_buf), sems)
    rows, half = up_buf.shape[0], left_ref.shape[0]
    if half == rows:
        up_ref[...] = (up_buf[...].astype(F32) + left_ref[...].astype(F32)).astype(BF16)
        down_ref[...] = (down_buf[...].astype(F32) + right_ref[...].astype(F32)).astype(BF16)
        return
    up_ref[:half] = (up_buf[:half].astype(F32) + left_ref[...].astype(F32)).astype(BF16)
    up_ref[half:] = up_buf[half:]
    down_ref[:half] = down_buf[:half]
    down_ref[half:] = (down_buf[half:].astype(F32) + right_ref[...].astype(F32)).astype(BF16)


HBM = pl.BlockSpec(memory_space=pltpu.HBM)
VMEM = pl.BlockSpec(memory_space=pltpu.VMEM)


def ring_add(mine_up, mine_down, left, right, rows):
    width = left.shape[1]
    return pl.pallas_call(
        lambda *refs: ring_add_kernel((mine_up[1], mine_down[1]), *refs),
        in_specs=[HBM, HBM, VMEM, VMEM],
        out_specs=[VMEM, VMEM],
        out_shape=[jax.ShapeDtypeStruct((rows, width), BF16)] * 2,
        scratch_shapes=[pltpu.VMEM((rows, width), BF16)] * 2 + [pltpu.SemaphoreType.DMA((2,))],
        compiler_params=pltpu.CompilerParams(vmem_limit_bytes=SMALL_LIMIT),
        cost_estimate=pl.CostEstimate(
            flops=2 * rows * width, bytes_accessed=12 * rows * width, transcendentals=0
        ),
    )(mine_up[0], mine_down[0], left, right)


def summed(mine_ref, left_ref, right_ref):
    return mine_ref[...].astype(F32) + left_ref[...].astype(F32) + right_ref[...].astype(F32)


def enter_kernel(mine_ref, left_ref, right_ref, x_ref, gain_ref, middle_ref, mixer_ref):
    middle = x_ref[...].astype(F32) + summed(mine_ref, left_ref, right_ref)
    middle_ref[...] = middle
    mixer_ref[...] = (norm_parts(middle)[0] * gain_ref[...]).astype(BF16)


def mixer_back_kernel(
    mine_ref, left_ref, right_ref, logits_ref, router_ref, middle_ref, cot_ref, gain_ref, *refs
):
    grad_ref, branch_ref, gains_ref = refs
    grad_mixer = summed(mine_ref, left_ref, right_ref) + dot(logits_ref[...], router_ref[...], 1, 1)
    normed, row_scale = norm_parts(middle_ref[...])
    gains_ref[...] = jnp.sum(grad_mixer * normed, axis=0, keepdims=True)
    grad = cot_ref[...].astype(F32) + norm_back(grad_mixer * gain_ref[...], normed, row_scale)
    grad_ref[...] = grad
    branch_ref[...] = grad.astype(BF16)


def tokens_back_kernel(mine_ref, left_ref, right_ref, x_ref, grad_ref, out_ref):
    normed, row_scale = norm_parts(x_ref[...].astype(F32))
    grad = norm_back(summed(mine_ref, left_ref, right_ref), normed, row_scale)
    out_ref[...] = (grad_ref[...] + grad).astype(BF16)


def by_rows(kernel, landed, inputs, outs, sums=()):
    (mine, spot), left, right = landed
    rows, width = left.shape

    def whole(mine_hbm, *refs):
        refs, mine_ref, sems = refs[:-2], refs[-2], refs[-1]
        fetch((mine_hbm,), (spot,), (mine_ref,), sems)
        kernel(mine_ref, *refs)

    return pl.pallas_call(
        whole,
        in_specs=[HBM] + [VMEM] * (2 + len(inputs)),
        out_specs=[VMEM] * (len(outs) + len(sums)),
        out_shape=[jax.ShapeDtypeStruct((rows, width), kind) for kind in outs]
        + [jax.ShapeDtypeStruct(shape, F32) for shape in sums],
        scratch_shapes=[pltpu.VMEM((rows, width), BF16), pltpu.SemaphoreType.DMA((1,))],
        compiler_params=pltpu.CompilerParams(vmem_limit_bytes=SMALL_LIMIT),
        cost_estimate=pl.CostEstimate(
            flops=20 * rows * width, bytes_accessed=16 * rows * width, transcendentals=rows
        ),
    )(mine, left, right, *inputs)


def weights_back_kernel(held, copies, size, came_ref, own_ref, gain_ref, q_ref, k_ref, v_ref, gains_ref, small_ref):
    groups, rows, _ = came_ref.shape
    width = own_ref.shape[2]
    wide = width - 2 * size
    gains = jnp.zeros((rows, 1), F32)
    small = jnp.zeros(small_ref.shape, F32)
    gain = gain_ref[...]
    seen = set()
    for member, group in enumerate(held):
        came = came_ref[member].astype(F32)
        gains += jnp.sum(
            came[:, :width] * own_ref[member].astype(F32), axis=1, keepdims=True
        )
        small += came[:, width:]
        came = came[:, :width] * gain
        q_ref[:, group * wide : (group + 1) * wide] = came[:, :wide]
        lanes = slice(group // copies * size, (group // copies + 1) * size)
        if group // copies not in seen:
            k_ref[:, lanes] = came[:, wide : wide + size]
            v_ref[:, lanes] = came[:, wide + size :]
        else:
            k_ref[:, lanes] += came[:, wide : wide + size]
            v_ref[:, lanes] += came[:, wide + size :]
        seen.add(group // copies)
    gains_ref[...] = jnp.broadcast_to(gains, gains_ref.shape)
    small_ref[...] = small


def weights_back(came, own, gain, held, kv_heads, size):
    groups, rows, total = came.shape
    width = own.shape[2]
    shape = lambda cols: jax.ShapeDtypeStruct((rows, cols), F32)
    return pl.pallas_call(
        lambda *refs: weights_back_kernel(held, groups // kv_heads, size, *refs),
        out_shape=[
            shape(groups * (width - 2 * size)),
            shape(kv_heads * size),
            shape(kv_heads * size),
            shape(128),
            shape(total - width),
        ],
        compiler_params=params(),
        cost_estimate=pl.CostEstimate(
            flops=4 * groups * rows * width, bytes_accessed=4 << 20, transcendentals=0
        ),
    )(came, own, gain)


def output_back_kernel(count, order_ref, left_ref, *refs):
    pieces, outs, (rows_ref, sum_ref) = refs[:count], refs[count:-2], refs[-2:]
    step = pl.program_id(0)

    def store(first, rows):
        rows_ref[first : first + rows.shape[0]] = rows

    take_piece(step, pieces, True, store)

    @pl.when(step == 0)
    def _():
        sum_ref[...] = jnp.zeros_like(sum_ref)

    sum_ref[...] += dot(left_ref[...], rows_ref[...], 0, 0)

    @pl.when(step == pl.num_programs(0) - 1)
    def _():
        for i, out_ref in enumerate(outs):
            rows = out_ref.shape[0]
            first = pl.multiple_of(order_ref[i] * rows, rows)
            out_ref[...] = sum_ref[pl.ds(first, rows), :].astype(BF16)


def output_back(left, pieces, order):
    rows, width = left.shape
    block, cols = pieces[0].shape
    parts = order.shape[0]
    whole = lambda shape: pl.BlockSpec(shape, lambda i, order: (0, 0))
    return pl.pallas_call(
        lambda *refs: output_back_kernel(len(pieces), *refs),
        grid_spec=pltpu.PrefetchScalarGridSpec(
            num_scalar_prefetch=1,
            grid=(rows // block,),
            in_specs=[pl.BlockSpec((block, width), lambda i, order: (i, 0))]
            + [whole(piece.shape) for piece in pieces],
            out_specs=[whole((width // parts, cols))] * parts,
            scratch_shapes=[pltpu.VMEM((block, cols), BF16), pltpu.VMEM((width, cols), F32)],
        ),
        out_shape=[jax.ShapeDtypeStruct((width // parts, cols), BF16)] * parts,
        compiler_params=params(),
        cost_estimate=pl.CostEstimate(
            flops=2 * rows * width * cols, bytes_accessed=8 << 20, transcendentals=0
        ),
    )(order, left, *pieces)


def project_back_kernel(own_rows, order_ref, normed_ref, grad_ref, small_ref, gains_ref, *outs):
    width = grad_ref.shape[1]
    part = dot(normed_ref[...], grad_ref[...], 0, 0).astype(BF16)
    small = small_ref[...]
    size = small.shape[1]
    row = lax.broadcasted_iota(jnp.int32, small.shape, 0) % own_rows
    upper = lax.broadcasted_iota(jnp.int32, small.shape, 1) >= size // 2
    for i in range(2):
        gain = gains_ref[i : i + 1]
        for half, line in enumerate((pltpu.roll(gain, size // 2, 1), gain)):
            small = jnp.where(upper & (row == 2 * i + half), line, small)
    small = small.astype(BF16)
    for i, out_ref in enumerate(outs):

        @pl.when(pl.program_id(0) == i)
        def _(out_ref=out_ref):
            out_ref[:, :width] = part
            out_ref[:, width:] = small


def project_back(normed, grad, small, gains, own_rows, order):
    rows, depth = normed.shape
    width, extra = grad.shape[1], small.shape[1]
    parts = order.shape[0]
    block = depth // parts
    whole = lambda shape: pl.BlockSpec(shape, lambda i, order: (0, 0))
    return pl.pallas_call(
        lambda *refs: project_back_kernel(own_rows, *refs),
        grid_spec=pltpu.PrefetchScalarGridSpec(
            num_scalar_prefetch=1,
            grid=(parts,),
            in_specs=[
                pl.BlockSpec((rows, block), lambda i, order: (0, order[i])),
                whole(grad.shape),
                pl.BlockSpec((block, extra), lambda i, order: (order[i], 0)),
                whole(gains.shape),
            ],
            out_specs=[whole((block, width + extra))] * parts,
        ),
        out_shape=[jax.ShapeDtypeStruct((block, width + extra), BF16)] * parts,
        compiler_params=params(),
        cost_estimate=pl.CostEstimate(
            flops=2 * rows * depth * width, bytes_accessed=12 << 20, transcendentals=0
        ),
    )(order, normed, grad, small, gains)


def row_grads_kernel(first_ref, second_ref, first_grad_ref, second_grad_ref, out_ref):
    part = dot(first_ref[...], first_grad_ref[0], 0, 0)
    out_ref[0] = (part + dot(second_ref[...], second_grad_ref[0], 0, 0)).astype(BF16)


def row_grads(rows, grads):
    experts, _, ff = grads[0].shape
    depth = rows[0].shape[1]
    block = depth // 4
    return pl.pallas_call(
        row_grads_kernel,
        grid=(experts, 4),
        in_specs=[pl.BlockSpec((part.shape[0], block), lambda e, i: (0, i)) for part in rows]
        + [pl.BlockSpec((1,) + part.shape[1:], lambda e, i: (e, 0, 0)) for part in grads],
        out_specs=pl.BlockSpec((1, block, ff), lambda e, i: (e, i, 0)),
        out_shape=jax.ShapeDtypeStruct((experts, depth, ff), BF16),
        compiler_params=params(),
        cost_estimate=pl.CostEstimate(
            flops=2 * experts * sum(part.shape[0] for part in rows) * ff * depth,
            bytes_accessed=16 << 20,
            transcendentals=0,
        ),
    )(*rows, *grads)


def down_grads_kernel(order_ref, first_ref, second_ref, cot_ref, *outs):
    cut = first_ref.shape[1]
    part = dot(first_ref[0], cot_ref[:cut], 0, 0) + dot(second_ref[0], cot_ref[cut:], 0, 0)
    for i, out_ref in enumerate(outs):

        @pl.when(pl.program_id(0) == i)
        def _(out_ref=out_ref):
            out_ref[pl.program_id(1)] = part.astype(BF16)


def down_grads(active, cot, order):
    experts, _, ff = active[0].shape
    rows, depth = cot.shape
    parts = order.shape[0]
    block = depth // parts
    return pl.pallas_call(
        down_grads_kernel,
        grid_spec=pltpu.PrefetchScalarGridSpec(
            num_scalar_prefetch=1,
            grid=(parts, experts),
            in_specs=[
                pl.BlockSpec((1,) + part.shape[1:], lambda i, e, order: (e, 0, 0))
                for part in active
            ]
            + [pl.BlockSpec((rows, block), lambda i, e, order: (0, order[i]))],
            out_specs=[pl.BlockSpec((experts, ff, block), lambda i, e, order: (0, 0, 0))] * parts,
        ),
        out_shape=[jax.ShapeDtypeStruct((experts, ff, block), BF16)] * parts,
        compiler_params=params(),
        cost_estimate=pl.CostEstimate(
            flops=2 * experts * rows * ff * depth, bytes_accessed=16 << 20, transcendentals=0
        ),
    )(order, *active, cot)


def stack_heads(array, size):
    return jnp.concatenate(
        [array[:, i * size : (i + 1) * size] for i in range(array.shape[1] // size)], axis=0
    )


def attend_kernel(scale, q_ref, k_ref, v_ref, at_q_ref, at_k_ref, out_ref, p_ref):
    rows, size = q_ref.shape[0], k_ref.shape[1]
    heads = q_ref.shape[1] // size
    scores = dot(k_ref[...], stack_heads(q_ref[...], size), 1, 1) * scale
    at_q = jnp.concatenate([at_q_ref[...]] * heads, axis=1)
    scores = jnp.where(at_k_ref[...] <= at_q, scores, NEG_LARGE)
    grown = jnp.exp(scores - jnp.max(scores, axis=0, keepdims=True))
    probs = (grown * (1.0 / jnp.sum(grown, axis=0, keepdims=True))).astype(BF16)
    p_ref[...] = probs
    output = dot(v_ref[...].T, probs, 1, 0).T.astype(BF16)
    for head in range(heads):
        out_ref[:, head * size : (head + 1) * size] = output[head * rows : (head + 1) * rows]


def attend(query, key, value, places, scale, block):
    rows, width = query.shape
    size = key.shape[1]
    heads = width // size
    whole = lambda shape: pl.BlockSpec(shape, lambda i: (0, 0))
    return pl.pallas_call(
        lambda *refs: attend_kernel(scale, *refs),
        grid=(rows // block,),
        in_specs=[
            pl.BlockSpec((block, width), lambda i: (i, 0)),
            whole((rows, size)),
            whole((rows, size)),
            pl.BlockSpec((1, block), lambda i: (0, i)),
            whole((rows, 1)),
        ],
        out_specs=[
            pl.BlockSpec((block, width), lambda i: (i, 0)),
            pl.BlockSpec((rows, heads * block), lambda i: (0, i)),
        ],
        out_shape=[
            jax.ShapeDtypeStruct((rows, width), BF16),
            jax.ShapeDtypeStruct((rows, heads * rows), BF16),
        ],
        compiler_params=params(LARGE_LIMIT),
        cost_estimate=pl.CostEstimate(
            flops=4 * heads * rows * rows * size,
            bytes_accessed=12 << 20,
            transcendentals=heads * rows * rows,
        ),
    )(query, key, value, places[None, :], places[:, None])


def head_back(grad_turned, pre, gain, cosine, sine):
    grad = grad_turned * cosine - swap_halves(grad_turned) * sine
    normed, row_scale = norm_parts(pre)
    return (
        jnp.sum(grad * normed, axis=0, keepdims=True),
        norm_back(grad * gain, normed, row_scale).astype(BF16),
    )


def attend_back_kernel(scale, count, first, last, offset, *refs):
    pieces, refs = refs[:count], refs[count:]
    w_ref, p_ref, q_ref, k_ref, v_ref, pre_ref, cos_ref, sin_ref, gain_ref = refs[:9]
    refs = refs[9:]
    before, refs = (() if first else refs[:4]), (refs if first else refs[4:])
    out_ref, gains_ref, dk_ref, dv_ref, rows_ref = refs
    step = pl.program_id(0)
    rows, size = q_ref.shape[0], k_ref.shape[1]
    heads = q_ref.shape[1] // size

    def store(first, rows):
        rows_ref[first : first + rows.shape[0]] = rows

    take_piece(step, pieces, last, store)

    @pl.when(step == 0)
    def _():
        if first:
            dk_ref[...] = jnp.zeros_like(dk_ref)
            dv_ref[...] = jnp.zeros_like(dv_ref)
            gains_ref[...] = jnp.zeros_like(gains_ref)
        else:
            for now_ref, before_ref in zip((out_ref, gains_ref, dk_ref, dv_ref), before):
                now_ref[...] = before_ref[...]

    probs = p_ref[...]
    grads = stack_heads(dot(rows_ref[...], w_ref[...], 1, 1).astype(BF16), size)
    dv_ref[...] += dot(probs, grads, 1, 0)
    grad_probs = dot(v_ref[...], grads, 1, 1)
    probs = probs.astype(F32)
    grad_scores = (
        probs * (grad_probs - jnp.sum(probs * grad_probs, axis=0, keepdims=True))
    ).astype(BF16)
    dk_ref[...] += dot(grad_scores, stack_heads(q_ref[...], size), 1, 0)
    grad_query = dot(k_ref[...].T, grad_scores, 1, 0).T * scale
    start = pl.multiple_of((step + offset) * rows, rows)
    here = pl.ds(start, rows)
    cosine, sine = cos_ref[here, :], sin_ref[here, :]
    for head in range(heads):
        lanes = slice(head * size, (head + 1) * size)
        gain_part, part = head_back(
            grad_query[head * rows : (head + 1) * rows],
            pre_ref[here, lanes],
            gain_ref[0:1],
            cosine,
            sine,
        )
        gains_ref[0:1] += gain_part
        out_ref[here, lanes] = part

    if last:

        @pl.when(step == pl.num_programs(0) - 1)
        def _():
            gain_part, part = head_back(
                dk_ref[...] * scale,
                pre_ref[:, heads * size : (heads + 1) * size],
                gain_ref[1:2],
                cos_ref[...],
                sin_ref[...],
            )
            gains_ref[1:2] = gain_part
            out_ref[:, heads * size : (heads + 1) * size] = part
            out_ref[:, (heads + 1) * size :] = dv_ref[...].astype(BF16)


def attend_back(pieces, offset, before, weights, probs, query, key, value, pre, cos_table, sine_table, gains, scale):
    rows, width = query.shape
    size = key.shape[1]
    heads = width // size
    block, depth = pieces[0].shape
    first, last = before is None, before is not None
    steps = len(pieces) - (1 if last else 0)
    whole = lambda shape: pl.BlockSpec(shape, lambda i: (0, 0))
    shapes = [
        jax.ShapeDtypeStruct((rows, (heads + 2) * size), BF16),
        jax.ShapeDtypeStruct((8, size), F32),
        jax.ShapeDtypeStruct((rows, size), F32),
        jax.ShapeDtypeStruct((rows, size), F32),
    ]
    outs = [whole(shape.shape) for shape in shapes]
    return pl.pallas_call(
        lambda *refs: attend_back_kernel(scale, len(pieces), first, last, offset, *refs),
        grid=(steps,),
        in_specs=[whole(piece.shape) for piece in pieces]
        + [
            whole(weights.shape),
            pl.BlockSpec((rows, heads * block), lambda i: (0, i + offset)),
            pl.BlockSpec((block, width), lambda i: (i + offset, 0)),
            whole((rows, size)),
            whole((rows, size)),
            whole((rows, (heads + 1) * size)),
            whole((rows, size)),
            whole((rows, size)),
            whole(gains.shape),
        ]
        + ([] if first else outs),
        out_specs=outs,
        out_shape=shapes,
        scratch_shapes=[pltpu.VMEM((block, depth), BF16)],
        compiler_params=params(),
        cost_estimate=pl.CostEstimate(
            flops=(8 * heads * rows * size + 2 * depth * width) * steps * block,
            bytes_accessed=(3 << 20) * steps,
            transcendentals=0,
        ),
    )(*pieces, weights, probs, query, key, value, pre, cos_table, sine_table, gains, *(before or ()))


def after(value, *others):
    return lax.optimization_barrier((value, *others))[0]


def ring_order(size):
    if size % 4 or size < 8:
        return list(range(size))
    wide = size // 4
    walk = [(0, y) for y in range(wide)]
    for z in range(1, 4):
        walk += [(z, y) for y in (range(wide - 1, 0, -1) if z % 2 else range(1, wide))]
    walk += [(z, 0) for z in (3, 2, 1)]
    return [z * wide + y for z, y in walk]


def together(*values):
    return lax.optimization_barrier(values)


class Ring:
    def __init__(self, size):
        self.size = size
        self.steps = size // 2
        order = ring_order(size)
        self.up = [(order[i], order[(i + 1) % size]) for i in range(size)]
        self.down = [(order[i], order[(i - 1) % size]) for i in range(size)]
        self.offsets = [0]
        for step in range(1, self.steps):
            self.offsets += [-step, step]
        self.offsets += [self.steps]
        near = np.zeros((size, size), np.int32)
        for i, member in enumerate(order):
            near[member] = [order[(i + offset) % size] for offset in self.offsets]
        seat = lax.axis_index("seq")
        self.members = jnp.asarray(near)[seat]
        self.spots = jnp.asarray(np.argsort(near, axis=1).astype(np.int32))[seat]

    def swap(self, up, down):
        return lax.ppermute(up, "seq", self.up), lax.ppermute(down, "seq", self.down)

    def spot(self, offset):
        return self.offsets.index(offset)


class Gather:
    def __init__(self, ring, block):
        self.ring, self.step, self.pieces = ring, 0, [block]
        self.left = self.right = block
        self.ready = None

    def sends(self):
        if self.step + 1 < self.ring.steps:
            return self.left, self.right
        half = self.left.shape[0] // 2
        return self.left[:half], self.right[half:]

    def start(self):
        ready = self.ready or self.sends()
        self.step += 1
        self.ready = None
        return self.ring.swap(*ready)

    def end(self, left, right):
        self.left, self.right = left, right
        self.pieces += [left, right]


class Scatter:
    def __init__(self, ring, piece, rows):
        self.ring, self.step, self.piece, self.rows = ring, 0, piece, rows
        self.left = self.right = self.ready = None

    def sends(self):
        ring, rows = self.ring, self.rows
        if self.step == 0:
            whole, spot = self.piece(ring.spot(ring.steps))
            start, middle, end = spot * rows, spot * rows + rows // 2, (spot + 1) * rows
            return (
                lax.slice_in_dim(whole, start, middle, axis=0),
                lax.slice_in_dim(whole, middle, end, axis=0),
            )
        place = ring.steps - self.step
        mine_up, mine_down = self.piece(ring.spot(place)), self.piece(ring.spot(-place))
        return ring_add(mine_up, mine_down, self.left, self.right, rows)

    def start(self):
        ready = self.ready or self.sends()
        self.step += 1
        self.ready = None
        return self.ring.swap(*ready)

    def end(self, left, right):
        self.left, self.right = left, right

    def landed(self):
        return self.piece(0), self.left, self.right


def prepare(rings, *values):
    ready, values = together([ring.sends() for ring in rings], values)
    for ring, sends in zip(rings, ready):
        ring.ready = tuple(sends)
    return values


def window(rings, *values):
    moved = [ring.start() for ring in rings]
    moved, values = together(moved, values)
    for ring, (left, right) in zip(rings, moved):
        ring.end(left, right)
    return values


class Fsdp:
    def __init__(self, size):
        self.size = size
        self.across = size // 2

        def blocks(way):
            return np.asarray(
                [
                    [
                        (i // 2 + way * step) % self.across * 2 + (i % 2 ^ flip)
                        for step in range(self.across)
                        for flip in (0, 1)
                    ]
                    for i in range(size)
                ],
                np.int32,
            )

        index = lax.axis_index("fsdp")
        self.blocks = jnp.asarray(blocks(-1))[index]
        self.targets = jnp.asarray(blocks(1))[index]
        self.spots = jnp.asarray(np.argsort(blocks(-1), axis=1).astype(np.int32))[index]

    def swap(self, array):
        return lax.ppermute(array, "fsdp", [(i, i ^ 1) for i in range(self.size)])

    def shift(self, array, step):
        perm = [
            (x * 2 + c, (x + step) % self.across * 2 + c)
            for x in range(self.across)
            for c in (0, 1)
        ]
        return lax.ppermute(array, "fsdp", perm)

    def spread(self, block):
        return [self.shift(block, step) for step in range(1, self.across)]

    def swapped(self, block, others):
        return [part for mine in [block] + others for part in (mine, self.swap(mine))]

    def pair(self, parts):
        return [
            (parts[i].astype(F32) + self.swap(parts[i + 1]).astype(F32)).astype(BF16)
            for i in range(0, self.size, 2)
        ]

    def send(self, paired):
        return [self.shift(part, step) for step, part in enumerate(paired) if step]


def on_device(
    tokens,
    cotangent,
    expert_ids,
    attn_gain,
    w_query,
    w_key,
    w_value,
    query_gain,
    key_gain,
    w_output,
    mlp_gain,
    w_router,
    w_gate,
    w_up,
    w_down,
):
    groups = lax.axis_size("seq")
    splits = lax.axis_size("fsdp")
    counts = groups * splits
    ring, fsdp = Ring(groups), Fsdp(splits)
    seat = lax.axis_index("seq")
    me = lax.axis_index(ALL)
    tok_rows, model_width = tokens.shape
    top_k = expert_ids.shape[1]
    own_rows = w_query.shape[0]
    head_size = query_gain.shape[0] * counts
    heads_all = w_query.shape[1] // head_size
    kv_heads = w_key.shape[1] // head_size
    head_local = heads_all // groups
    copies = groups // kv_heads
    query_width = head_local * head_size
    qkv_width = query_width + 2 * head_size
    experts_all = w_router.shape[1]
    local_experts, _, ff = w_gate.shape
    seq_rows = tok_rows * groups
    scale_qk = 1.0 / math.sqrt(head_size)

    held_groups = [seat % splits * (groups // splits) + seat // splits for seat in range(groups)]
    exchange = [
        (j * groups + part * splits + i, i * groups + part * splits + j)
        for j in range(splits)
        for part in range(groups // splits)
        for i in range(splits)
    ]

    def by_member(weights, group_of):
        width = weights.shape[1] // (max(group_of) + 1)
        return [weights[:, group * width : (group + 1) * width] for group in group_of]

    kv_of = [group // copies for group in held_groups]
    weights_own = jnp.stack(
        [
            jnp.concatenate(parts, axis=1)
            for parts in zip(
                by_member(w_query, held_groups), by_member(w_key, kv_of), by_member(w_value, kv_of)
            )
        ]
    )
    scaled = (weights_own.astype(F32) * attn_gain.astype(F32)[None, :, None]).astype(BF16)

    def placed(gain):
        return lax.dynamic_update_slice(
            jnp.zeros((head_size,), BF16), gain, (me * gain.shape[0],)
        )

    others = jnp.concatenate(
        [mlp_gain, w_router.reshape(-1), expert_ids.T.reshape(-1).astype(BF16)]
    )
    extra = -(-(others.shape[0] + 2 * head_size) // (own_rows * head_size)) * head_size
    spread = jnp.zeros((2, extra), BF16).at[0, :head_size].set(placed(query_gain))
    spread = spread.at[1, :head_size].set(placed(key_gain))
    spare = (own_rows - 2) * extra - others.shape[0]
    others = jnp.pad(others, (0, spare)).reshape(own_rows - 2, extra)
    small = jnp.concatenate([spread, others], axis=0)[None]
    scaled = jnp.concatenate([scaled, jnp.repeat(small, groups, axis=0)], axis=2)
    places = (
        ring.members[:, None] * tok_rows + jnp.arange(tok_rows, dtype=jnp.int32)[None, :]
    ).reshape(seq_rows)
    tables = rotary_tables(places.astype(F32), head_size)

    gate_w = lax.all_gather(w_gate, "fsdp", axis=1, tiled=True)
    token_ring = Gather(ring, tokens)
    (scaled,) = window([token_ring], scaled)
    qkv = lax.all_to_all(scaled, "seq", split_axis=0, concat_axis=0, tiled=True).reshape(
        groups * own_rows, qkv_width + extra
    )
    qkv, w_output = window([token_ring], qkv, w_output)
    part_rows = groups * own_rows // 2
    first_half = fsdp.spread(qkv[:part_rows])
    for step in range(3, ring.steps):
        qkv, first_half, tables, places, w_output = window(
            [token_ring], qkv, first_half, tables, places, w_output
        )
    cos_table, sine_table = tables
    second_half = fsdp.spread(qkv[part_rows:])
    qkv, first_half, second_half, w_output, w_up, cotangent_sent = window(
        [token_ring], qkv, first_half, second_half, w_output, w_up, cotangent
    )
    up_w = lax.all_gather(w_up, "fsdp", axis=1, tiled=True)

    cot_ring = Gather(ring, cotangent_sent)
    qkv_parts = fsdp.swapped(
        qkv, [jnp.concatenate(pair, axis=0) for pair in zip(first_half, second_half)]
    )
    gains_qk = sum(
        jnp.sum(
            part.reshape(groups, own_rows, qkv_width + extra)[
                :, :2, qkv_width : qkv_width + head_size
            ].astype(F32),
            axis=0,
        )
        for part in qkv_parts
    )
    projected = project(
        token_ring.pieces, qkv_parts, fsdp.blocks, qkv_width, cos_table, sine_table, gains_qk
    )
    held = lax.ppermute(w_output, ALL, exchange)
    projected, held, qkv_parts = window([cot_ring], projected, held, qkv_parts)
    normed_all, qk_pre, query_seq, key_seq, value_seq = projected
    attended, probs = attend(query_seq, key_seq, value_seq, places, scale_qk, tok_rows)
    held_others = fsdp.spread(held)
    attended, probs, held, held_others = window([cot_ring], attended, probs, held, held_others)
    output_w = lay(fsdp.swapped(held, held_others), fsdp.blocks)
    branch = jnp.dot(attended, output_w, preferred_element_type=F32).astype(BF16)
    for step in range(3, ring.steps):
        branch, output_w, gate_w, w_down = window([cot_ring], branch, output_w, gate_w, w_down)
    down_w = lax.all_gather(w_down, "fsdp", axis=2, tiled=True)

    branch_ring = Scatter(ring, lambda spot: (branch, spot), tok_rows)
    (qkv_parts,) = window([branch_ring, cot_ring], qkv_parts)

    def small_arrays(parts):
        small = jnp.stack([part[:, qkv_width:].reshape(groups, -1) for part in parts])
        small = jnp.take(small, fsdp.spots, axis=0)[:, :, 2 * extra :]
        cuts = [own_rows, own_rows * experts_all, tok_rows * top_k]
        ends = [sum(cuts[: i + 1]) for i in range(3)]
        gain_mlp = small[:, :, : ends[0]].reshape(1, model_width).astype(F32)
        router_w = small[:, :, ends[0] : ends[1]].reshape(model_width, experts_all)
        ids_all = parts[0][:, qkv_width:].reshape(groups, -1)[:, 2 * extra :]
        ids_near = jnp.take(ids_all[:, ends[1] : ends[2]], ring.members, axis=0)
        ids_near = ids_near.astype(jnp.int32).reshape(groups, top_k, tok_rows)
        return gain_mlp, router_w, ids_near.transpose(1, 0, 2).reshape(top_k, -1)

    (gain_mlp, router_w, ids_near), qkv_parts, cot_pieces = window(
        [branch_ring], small_arrays(qkv_parts), qkv_parts, cot_ring.pieces
    )
    qkv_w, cot_all = lay(qkv_parts, fsdp.blocks), lay(cot_pieces)
    for step in range(3, ring.steps):
        qkv_w, cot_all = window([branch_ring], qkv_w, cot_all)
    (up_w,) = window([branch_ring], up_w)
    middle, mixer_in = by_rows(
        enter_kernel, branch_ring.landed(), [tokens, gain_mlp], [F32, BF16]
    )

    def shares(rows_in, ids):
        logits = jnp.dot(rows_in, router_w, preferred_element_type=F32)
        chosen = jnp.sum(
            (ids[:, :, None] == jnp.arange(experts_all, dtype=jnp.int32)).astype(F32), axis=0
        )
        masked = jnp.where(chosen > 0, logits, NEG_LARGE)
        grown = jnp.exp(masked - jnp.max(masked, axis=-1, keepdims=True)) * chosen
        return grown / jnp.sum(grown, axis=-1, keepdims=True)

    def expert_part(rows_in, first):
        last = first + rows_in.shape[0]
        share = lax.dynamic_slice_in_dim(
            shares(rows_in, ids_near[:, first:last]), seat * local_experts, local_experts, 1
        ).T[:, :, None]
        gate_pre = jnp.einsum("td,edf->etf", rows_in, gate_w, preferred_element_type=F32)
        up_pre = jnp.einsum("td,edf->etf", rows_in, up_w, preferred_element_type=F32)
        back = down_back[:, first:last]
        sigmoid = jax.nn.sigmoid(gate_pre)
        silu_gate = gate_pre * sigmoid
        active = silu_gate * up_pre
        grad_share = jnp.sum(active * back, axis=-1)
        active_shared = (active * share).astype(BF16)
        grad_active = back * share
        grad_up_pre = (grad_active * silu_gate).astype(BF16)
        grad_gate_pre = (
            grad_active * up_pre * sigmoid * (1.0 + gate_pre * (1.0 - sigmoid))
        ).astype(BF16)
        return grad_share, active_shared, grad_gate_pre, grad_up_pre

    def entered_part(part):
        entered = jnp.einsum(
            "etf,edf->td", part[2], gate_w, preferred_element_type=F32
        ) + jnp.einsum("etf,edf->td", part[3], up_w, preferred_element_type=F32)
        return entered.astype(BF16)

    cut = ring.steps // 2
    early = (2 * cut + 1) * tok_rows
    mixer_ring = Gather(ring, mixer_in)
    cot_all, down_w = window([mixer_ring], cot_all, down_w)
    down_back = jnp.einsum("td,efd->etf", cot_all, down_w, preferred_element_type=F32)
    (down_back,) = window([mixer_ring], down_back)
    for step in range(3, cut + 1):
        window([mixer_ring])
    early_rows = jnp.concatenate(mixer_ring.pieces, axis=0)
    early_part = expert_part(early_rows, 0)
    for step in range(cut + 1, ring.steps):
        (early_rows,) = window([mixer_ring], early_rows)
    early_part, early_rows = window([mixer_ring], early_part, early_rows)
    late_rows = jnp.concatenate(mixer_ring.pieces[2 * cut + 1 :], axis=0)
    late_part = expert_part(late_rows, early)
    late_entered = entered_part(late_part)
    late_entered, late_part, early_part, late_rows, early_rows = together(
        late_entered, late_part, early_part, late_rows, early_rows
    )

    def entered_piece(spot):
        if spot * tok_rows >= early:
            return late_entered, spot - early // tok_rows
        return early_entered, spot

    entered_ring = Scatter(ring, entered_piece, tok_rows)
    grad_share = jnp.concatenate([early_part[0], late_part[0]], axis=1)
    grad_share_own = lax.all_to_all(
        jnp.take(grad_share.reshape(local_experts, groups, tok_rows), ring.spots, axis=1).transpose(
            1, 0, 2
        ),
        "seq",
        split_axis=0,
        concat_axis=0,
        tiled=True,
    )
    early_entered = entered_part(early_part)
    window([entered_ring])
    early_entered, early_part, late_part, early_rows, late_rows = window(
        [entered_ring], early_entered, early_part, late_part, early_rows, late_rows
    )
    for step in range(3, ring.steps):
        early_part, late_part, early_rows, late_rows, grad_share_own = window(
            [entered_ring], early_part, late_part, early_rows, late_rows, grad_share_own
        )
    early_part, late_part, early_rows, late_rows, grad_share_own = prepare(
        [entered_ring], early_part, late_part, early_rows, late_rows, grad_share_own
    )
    grad_share_own = grad_share_own.reshape(experts_all, tok_rows).T
    share_own = shares(mixer_in, expert_ids.T)
    grad_logits = (
        share_own
        * (grad_share_own - jnp.sum(share_own * grad_share_own, axis=-1, keepdims=True))
    ).astype(BF16)
    grad_gate = row_grads((early_rows, late_rows), (early_part[2], late_part[2]))
    grad_gate, grad_logits, early_part, late_part, early_rows, late_rows = window(
        [entered_ring], grad_gate, grad_logits, early_part, late_part, early_rows, late_rows
    )
    grad_gate = lax.psum_scatter(grad_gate, "fsdp", scatter_dimension=1, tiled=True)
    grad_middle, grad_branch, grad_gain_m = by_rows(
        mixer_back_kernel,
        entered_ring.landed(),
        [grad_logits, router_w, middle, cotangent, gain_mlp],
        [F32, BF16],
        [(1, model_width)],
    )

    grads_ring = Gather(ring, grad_branch)
    early_part, late_part, early_rows, late_rows = prepare(
        [grads_ring], early_part, late_part, early_rows, late_rows
    )
    grad_up = row_grads((early_rows, late_rows), (early_part[3], late_part[3]))
    grad_up, early_active, late_active = window(
        [grads_ring], grad_up, early_part[1], late_part[1]
    )
    grad_up = lax.psum_scatter(grad_up, "fsdp", scatter_dimension=1, tiled=True)
    produced = [
        jnp.einsum("etf,efd->td", active, down_w, preferred_element_type=F32).astype(BF16)
        for active in (early_active, late_active)
    ]
    produced, early_active, late_active = window(
        [grads_ring], produced, early_active, late_active
    )
    for step in range(3, cut + 1):
        window([grads_ring])

    def two_parts(parts):
        def piece(spot):
            if spot * tok_rows >= early:
                return parts[1], spot - early // tok_rows
            return parts[0], spot

        return piece

    def back(pieces, offset, before):
        return attend_back(
            pieces,
            offset,
            before,
            output_w,
            probs,
            query_seq,
            key_seq,
            value_seq,
            qk_pre,
            cos_table,
            sine_table,
            gains_qk,
            scale_qk,
        )

    grads = back(grads_ring.pieces, 0, None)
    grad_small = jnp.concatenate([dot(mixer_in, grad_logits, 0, 0), grad_gain_m.T], axis=1)
    grad_small = jnp.pad(grad_small, ((0, 0), (0, head_size - grad_small.shape[1])))
    for step in range(cut + 1, ring.steps):
        (grad_small,) = window([grads_ring], grad_small)
    layer_ring = Scatter(ring, two_parts(produced), tok_rows)
    (grads,) = window([grads_ring, layer_ring], grads)
    grads = back(grads_ring.pieces[2 * cut + 1 :], 2 * cut + 1, grads)
    (grads,) = window([layer_ring], grads)

    grads, grad_small = prepare([layer_ring], grads, grad_small)
    grad_qkv = grads[0]
    paired = fsdp.pair(
        project_back(normed_all, grad_qkv, grad_small, grads[1], own_rows, fsdp.targets)
    )
    for step in range(3, ring.steps):
        paired, grad_qkv = window([layer_ring], paired, grad_qkv)
    paired, grad_qkv, early_active, late_active = prepare(
        [layer_ring], paired, grad_qkv, early_active, late_active
    )
    sent = fsdp.send(paired)
    grad_hidden = dot(grad_qkv, qkv_w[:, :qkv_width], 1, 1).astype(BF16)
    grad_hidden, paired, branch_pieces, early_active, late_active = window(
        [layer_ring], grad_hidden, paired, grads_ring.pieces, early_active, late_active
    )
    (produced, spot), left, right = layer_ring.landed()
    layer_out = (
        middle
        + lax.slice_in_dim(produced, 0, tok_rows, axis=0).astype(F32)
        + left.astype(F32)
        + right.astype(F32)
    ).astype(BF16)

    hidden_ring = Scatter(ring, lambda spot: (grad_hidden, spot), tok_rows)
    branch_pieces, paired = prepare([hidden_ring], branch_pieces, paired)
    paired_output = fsdp.pair(output_back(attended, branch_pieces, fsdp.targets))
    paired, sent, paired_output, early_active, late_active = window(
        [hidden_ring], paired, sent, paired_output, early_active, late_active
    )
    total = paired[0].astype(F32) + sum(part.astype(F32) for part in sent)
    grad_qkv_w = lax.all_to_all(
        total.astype(BF16).reshape(groups, own_rows, qkv_width + head_size),
        "seq",
        split_axis=0,
        concat_axis=0,
        tiled=True,
    )
    sent_output = fsdp.send(paired_output)
    early_active, late_active, paired_output = prepare(
        [hidden_ring], early_active, late_active, paired_output
    )
    paired_down = fsdp.pair(down_grads((early_active, late_active), cot_all, fsdp.targets))
    paired_output, sent_output, paired_down = window(
        [hidden_ring], paired_output, sent_output, paired_down
    )
    total = paired_output[0].astype(F32) + sum(part.astype(F32) for part in sent_output)
    grad_output_w = lax.ppermute(total.astype(BF16), ALL, exchange)
    sent_down = fsdp.send(paired_down)

    def corner(array):
        return lax.slice(array, (0,) * array.ndim, (1,) * (array.ndim - 2) + (8, 128))

    grad_gate, grad_up = prepare([hidden_ring], grad_gate, grad_up)
    grad_gate, grad_up = grad_gate.astype(F32), grad_up.astype(F32)
    for step in range(3, ring.steps):
        grad_qkv_w, grad_output_w, _ = window(
            [hidden_ring], grad_qkv_w, grad_output_w, [corner(grad_gate), corner(grad_up)]
        )
    grad_output_w, paired_down, sent_down = prepare(
        [hidden_ring], grad_output_w, paired_down, sent_down
    )
    grad_output_w = grad_output_w.astype(F32)
    grad_down = paired_down[0].astype(F32) + sum(part.astype(F32) for part in sent_down)
    window([hidden_ring], [corner(grad_output_w), corner(grad_down), corner(layer_out)])
    (grad_tokens,) = by_rows(
        tokens_back_kernel, hidden_ring.landed(), [tokens, grad_middle], [BF16]
    )
    grad_query_w, grad_key_w, grad_value_w, grad_gain_a, small = weights_back(
        grad_qkv_w,
        weights_own,
        attn_gain.astype(F32)[:, None],
        held_groups,
        kv_heads,
        head_size,
    )
    gains = small[:4, head_size // 2 :].reshape(2, head_size)
    cut = query_gain.shape[0]
    gains = lax.dynamic_slice(gains, (0, me * cut), (2, cut))
    return (
        layer_out,
        grad_tokens,
        grad_gain_a[:, 0],
        grad_query_w,
        grad_key_w,
        grad_value_w,
        gains[0],
        gains[1],
        grad_output_w,
        small[:, experts_all],
        small[:, :experts_all],
        grad_gate,
        grad_up,
        grad_down,
    )


def solution(mesh):
    rows = P(("fsdp", "seq"), None)
    line = P(("fsdp", "seq"))
    wide = P("seq", "fsdp", None)
    deep = P("seq", None, "fsdp")
    in_specs = (
        rows, rows, rows, line, rows, rows, rows, line, line, rows, line, rows, wide, wide, deep,
    )
    out_specs = (
        rows, rows, line, rows, rows, rows, line, line, rows, line, rows, wide, wide, deep,
    )
    return jax.shard_map(
        on_device, mesh=mesh, in_specs=in_specs, out_specs=out_specs, check_vma=False
    )
```

time: 920 us -> 628 us (0.68)
  waiting for transfers between devices: 339 us -> 171 us
  Pallas kernels: 0 us -> 127 us
  matrix products: 161 us -> 75 us
  starting transfers between devices: 169 us -> 111 us
  other arithmetic: 85.9 us -> 43 us
  local copies, waits for them, and re-layouts: 108 us -> 74.5 us
  blocking collectives: 30.4 us -> 0 us
    ppermute x117 -> x82, waiting for transfers between devices: 337 us -> 161 us  [the longest x32 109 us: swap(): lax.ppermute(up, 'seq', self.up)]
    pallas_call x0 -> x28, Pallas kernels: none -> 127 us  [the longest x2 27.3 us: attend_back(): pl.pallas_call(lambda *refs: attend_back_kernel(scale, len(pieces), first...]
    dot_general x22 -> x11, matrix products: 123 us -> 57.7 us  [the longest x2 14.5 us: expert_part(): jnp.einsum('td,edf->etf', rows_in, up_w, preferred_element_type=F32)]
    ppermute x117 -> x82, starting transfers between devices: 153 us -> 98.3 us  [the longest x32 39.3 us: swap(): lax.ppermute(up, 'seq', self.up)]
    dynamic_update_slice x58 -> x4, local copies, waits for them, and re-layouts: 45.2 us -> 1.56 us  [placed(): lax.dynamic_update_slice(jnp.zeros((head_size,), BF16), gain, (me * gain....]
    all_gather x1 -> x0, blocking collectives: 30.4 us -> none  [on_device(): ids_all = lax.all_gather(expert_ids, 'seq', axis=0, tiled=True)]
    unnamed x218 -> x233, local copies, waits for them, and re-layouts: 18.2 us -> 47.9 us
    dot_general x6 -> x2, matrix products: 27.2 us -> 3.9 us  [dot(): lax.dot_general(left, right, (((left_dim,), (right_dim,)), ((), ())), pre...]
  transfers between devices with their start and end apart: 120 -> 90, of which waited for: 58 -> 42; matrix products, arithmetic and copies ran while one was open for 25% -> 22% of each run, Pallas kernels for 0% -> 20%
where the time goes in v2:
time: 628 us; the launch traced here: 618 us
  waiting for transfers between devices  171 us (27%)
  Pallas kernels  127 us (20%)
  starting transfers between devices  111 us (18%)
  matrix products  75 us (12%)
  local copies, waits for them, and re-layouts  74.5 us (12%)
  other arithmetic  43 us (7%)
  between operations  15.6 us (2%)
    ppermute x32, waiting for transfers between devices, swap(): lax.ppermute(up, 'seq', self.up)  109 us
    unnamed x233, local copies, waits for them, and re-layouts  47.9 us
    ppermute x32, starting transfers between devices, swap(): lax.ppermute(up, 'seq', self.up)  39.3 us
    ppermute x32, starting transfers between devices, swap(): lax.ppermute(down, 'seq', self.down)  37.1 us
    ppermute x6, waiting for transfers between devices, shift(): return lax.ppermute(array, 'fsdp', perm)  33.4 us
    pallas_call x2, Pallas kernels, attend_back(): pl.pallas_call(lambda *refs: attend_back_kernel(scale, len(pieces), first...  27.3 us
    pallas_call x2, Pallas kernels, row_grads(): pl.pallas_call(row_grads_kernel, grid=(experts, 4), in_specs=[pl.BlockSpe...  20.9 us
    ppermute x32, waiting for transfers between devices, swap(): lax.ppermute(down, 'seq', self.down)  18.3 us
  transfers between devices with their start and end apart: 90, of which 42 were waited for; matrix products, arithmetic and copies ran while one was open for 22% of the time, Pallas kernels for 20%

profile of v2, /device:TPU:0, one launch (start us, length us, event | category | flops | bytes accessed | tf_op | source)
XLA Modules:
  0.0 617.6 jit_solution(14272157919648390515)
XLA Ops:
  24.5 4.9 all-to-all-start
  32.2 24.4 %collective-permute-done.2.refs_4_ = bf16[128,2048]{1,0:T(8,128)(2,1)S(1)} collective-permute-done((bf16[128,2048]{1,0:T(8,128)(2,1)S(1)}, bf16[128,2048]{1,0:T(8,128)(2,1)S(1)}, u32[]{:S(2)}, u32[]{:S(2)}) %collective-permute-start.2) | collective-permute-done | bytes 524320 | tf_op jit(solution)/shard_map/ppermute | solution.py:667
  58.1 5.3 collective-permute-start.5
  68.4 5.2 collective-permute-done.6
  89.4 5.4 collective-permute-start.14
  96.9 13.9 %shard_map.299 = (bf16[1024,2048]{1,0:T(8,128)(2,1)}, f32[1024,640]{1,0:T(8,128)}, bf16[1024,512]{1,0:T(8,128)(2,1)}, bf16[1024,128]{1,0:T(8,128)(2,1)}, bf16[1024,128]{1,0:T(8,128)(2,1)}) custom-call(s32[4]{0:T(128)} %fusion.55.refs_0_.order_ref, bf16[128,2048]{1,0:T(8,128)(2,1)} %refs_2_.3, bf16[128,2048]{1,0:T(8,128)(2,1)} %copy-done.97, ...), custom_call_target="tpu_custom_call" | custom-call | flops 3221225472 | bytes 16777216 | tf_op jit(solution)/shard_map/pallas_call | solution.py:137
  117.2 12.5 %shard_map.300 = (bf16[1024,512]{1,0:T(8,128)(2,1)}, bf16[1024,4096]{1,0:T(8,128)(2,1)}) custom-call(bf16[1024,512]{1,0:T(8,128)(2,1)} %get-tuple-element.390.refs_0_.refs_7_.refs_6_, bf16[1024,128]{1,0:T(8,128)(2,1)} %get-tuple-element.391.refs_1_.refs_8_.refs_7_, bf16[1024,128]{1,0:T(8,128)(2,1)} %get-tuple-element.392.refs_2_.refs_9_.refs_8_, ...), custom_call_target="tpu_custom_call" | custom-call | flops 2147483648 | bytes 12582912 | tf_op jit(solution)/shard_map/pallas_call | solution.py:484
  129.8 11.1 %collective-permute-done.17.refs_3_ = bf16[128,2048]{1,0:T(8,128)(2,1)} collective-permute-done((bf16[128,2048]{1,0:T(8,128)(2,1)}, bf16[128,2048]{1,0:T(8,128)(2,1)}, u32[]{:S(2)}, u32[]{:S(2)}) %collective-permute-start.17) | collective-permute-done | bytes 524320 | tf_op jit(solution)/shard_map/ppermute | solution.py:774
  151.1 5.4 collective-permute-done.18.refs_6_
  209.6 8.5 %collective-permute-done.30.refs_0_ = bf16[128,2048]{1,0:T(8,128)(2,1)S(1)} collective-permute-done((bf16[128,2048]{1,0:T(8,128)(2,1)S(1)}, bf16[128,2048]{1,0:T(8,128)(2,1)S(1)}, u32[]{:S(2)}, u32[]{:S(2)}) %collective-permute-start.30) | collective-permute-done | bytes 524320 | tf_op jit(solution)/shard_map/ppermute | solution.py:667
  223.5 8.3 %collective-permute-done.32 = bf16[128,2048]{1,0:T(8,128)(2,1)S(1)} collective-permute-done((bf16[128,2048]{1,0:T(8,128)(2,1)S(1)}, bf16[128,2048]{1,0:T(8,128)(2,1)S(1)}, u32[]{:S(2)}, u32[]{:S(2)}) %collective-permute-start.32) | collective-permute-done | bytes 524320 | tf_op jit(solution)/shard_map/ppermute | solution.py:667
  235.6 11.7 %fusion.12 = f32[2,1024,768]{2,1,0:T(8,128)} fusion(bf16[2,768,2048]{2,1,0:T(8,128)(2,1)} %all-gather.8.cloned.1.call-done, bf16[1024,2048]{1,0:T(8,128)(2,1)} %copy-done.21), kind=kOutput, calls=%fused_computation.32 | convolution fusion | flops 6442450944 | bytes 16777216 | tf_op jit(solution)/shard_map/td,efd->etf/dot_general | solution.py:986
  250.6 7.4 %fusion.15 = f32[2,768,640]{1,2,0:T(8,128)S(1)} fusion(bf16[2,2048,768]{2,1,0:T(8,128)(2,1)} %all-gather.4.cloned.1.call-done, bf16[640,2048]{1,0:T(8,128)(2,1)S(1)} %constant_dynamic-update-slice_fusion.2.first_ref), kind=kOutput, calls=%fused_computation.33 | convolution fusion | flops 4026531840 | bytes 12845056 | tf_op jit(solution)/shard_map/td,edf->etf/dot_general | solution.py:961
  259.0 8.7 %fusion.5 = (bf16[2,640,768]{2,1,0:T(8,128)(2,1)S(1)}, f32[2,640]{1,0:T(2,128)S(1)}, bf16[2,640,768]{2,1,0:T(8,128)(2,1)S(1)}, bf16[2,640,768]{2,1,0:T(8,128)(2,1)}) fusion(f32[2,768,640]{1,2,0:T(8,128)S(1)} %fusion.15, f32[2,1024,768]{2,1,0:T(8,128)} %fusion.12, f32[2,640]{1,0:T(2,128)S(1)} %fusion.50, bf16[2,2048,768]{2,1,0:T(8,128)(2,1)S(1)} %bitcast.263, ...), kind=kOutput, calls=%fused_computation.12 | convolution fusion | flops 4045208320 | bytes 22685696 | tf_op jit(solution)/shard_map/td,edf->etf/dot_general | solution.py:962
  279.1 5.8 multiply_reduce_fusion.1
  292.4 6.0 fusion.70
  303.5 6.3 %fusion.refs_0_.refs_1_.mine_hbm = bf16[640,2048]{1,0:T(8,128)(2,1)S(1)} fusion(f32[640,2048,1]{1,0,2:T(8,128)} %fusion.70, bf16[2,640,768]{2,1,0:T(8,128)(2,1)S(1)} %get-tuple-element.535.first_grad_ref, bf16[2,2048,768]{2,1,0:T(8,128)(2,1)S(1)} %bitcast.263), kind=kOutput, calls=%fused_computation.5 | convolution fusion | flops 4029153280 | bytes 16121856 | tf_op jit(solution)/shard_map/etf,edf->td/dot_general | solution.py:979
  309.8 6.4 %collective-permute-done.42.refs_2_ = bf16[128,2048]{1,0:T(8,128)(2,1)S(1)} collective-permute-done((bf16[128,2048]{1,0:T(8,128)(2,1)S(1)}, bf16[128,2048]{1,0:T(8,128)(2,1)S(1)}, u32[]{:S(2)}, u32[]{:S(2)}) %collective-permute-start.42) | collective-permute-done | bytes 524320 | tf_op jit(solution)/shard_map/ppermute | solution.py:667
  325.9 9.3 %all-to-all-done.1 = f32[8,2,128]{2,1,0:T(2,128)S(1)} async-done(((f32[8,2,128]{2,1,0:T(2,128)}), f32[8,2,128]{2,1,0:T(2,128)S(1)}, u32[]{:S(2)}, u32[]{:S(2)}) %all-to-all-start.1) | async-done | bytes 8224 | tf_op jit(solution)/shard_map/all_to_all | solution.py:1009
  346.3 10.4 %shard_map.311 = bf16[2,2048,768]{2,1,0:T(8,128)(2,1)S(1)} custom-call(bf16[640,2048]{1,0:T(8,128)(2,1)S(1)} %copy-done.26, bf16[384,2048]{1,0:T(8,128)(2,1)S(1)} %copy-done.33, bf16[2,640,768]{2,1,0:T(8,128)(2,1)S(1)} %copy-done.82, bf16[2,384,768]{2,1,0:T(8,128)(2,1)S(1)} %copy-done.74), custom_call_target="tpu_custom_call" | custom-call | flops 6442450944 | bytes 16777216 | tf_op jit(solution)/shard_map/pallas_call | solution.py:408
  369.8 10.4 %shard_map.313 = bf16[2,2048,768]{2,1,0:T(8,128)(2,1)S(1)} custom-call(bf16[640,2048]{1,0:T(8,128)(2,1)S(1)} %copy-done.27, bf16[384,2048]{1,0:T(8,128)(2,1)S(1)} %copy-done.34, bf16[2,640,768]{2,1,0:T(8,128)(2,1)S(1)} %copy-done.80, bf16[2,384,768]{2,1,0:T(8,128)(2,1)S(1)} %copy-done.76), custom_call_target="tpu_custom_call" | custom-call | flops 6442450944 | bytes 16777216 | tf_op jit(solution)/shard_map/pallas_call | solution.py:408
  386.5 7.6 %bitcast_convert_fusion.refs_0_.refs_1_ = bf16[640,2048]{1,0:T(8,128)(2,1)S(1)} fusion(bf16[2,640,768]{2,1,0:T(8,128)(2,1)} %get-tuple-element.645.first_ref, bf16[2,768,2048]{2,1,0:T(8,128)(2,1)} %all-gather.8.cloned.1.call-done), kind=kOutput, calls=%fused_computation.3 | convolution fusion | flops 4027842560 | bytes 10878976 | tf_op jit(solution)/shard_map/etf,efd->td/dot_general | solution.py:1059
  417.1 15.9 %shard_map.314 = (bf16[1024,768]{1,0:T(8,128)(2,1)S(1)}, f32[8,128]{1,0:T(8,128)S(1)}, f32[1024,128]{1,0:T(8,128)S(1)}, f32[1024,128]{1,0:T(8,128)S(1)}) custom-call(bf16[128,2048]{1,0:T(8,128)(2,1)} %get-tuple-element.619.refs_0_.refs_2_, bf16[128,2048]{1,0:T(8,128)(2,1)S(1)} %copy-done.55, bf16[128,2048]{1,0:T(8,128)(2,1)} %collective-permute-done.49.refs_2_.refs_4_, ...), custom_call_target="tpu_custom_call" | custom-call | flops 4026531840 | bytes 15728640 | tf_op jit(solution)/shard_map/pallas_call | solution.py:601
  435.7 11.5 %shard_map.316 = (bf16[1024,768]{1,0:T(8,128)(2,1)S(1)}, f32[8,128]{1,0:T(8,128)S(1)}, f32[1024,128]{1,0:T(8,128)}, f32[1024,128]{1,0:T(8,128)}) custom-call(bf16[128,2048]{1,0:T(8,128)(2,1)} %collective-permute-done.52.refs_0_.refs_7_, bf16[128,2048]{1,0:T(8,128)(2,1)} %collective-permute-done.53.refs_1_.refs_8_, ...), custom_call_target="tpu_custom_call" | custom-call | flops 2415919104 | bytes 9437184 | tf_op jit(solution)/shard_map/pallas_call | solution.py:601
  449.3 5.5 shard_map.318
  458.9 10.4 %collective-permute-done.60.refs_2_ = bf16[128,2048]{1,0:T(8,128)(2,1)S(1)} collective-permute-done((bf16[128,2048]{1,0:T(8,128)(2,1)S(1)}, bf16[128,2048]{1,0:T(8,128)(2,1)S(1)}, u32[]{:S(2)}, u32[]{:S(2)}) %collective-permute-start.60) | collective-permute-done | bytes 524320 | tf_op jit(solution)/shard_map/ppermute | solution.py:667
  476.3 7.1 %collective-permute-done.64 = bf16[128,2048]{1,0:T(8,128)(2,1)S(1)} collective-permute-done((bf16[128,2048]{1,0:T(8,128)(2,1)S(1)}, bf16[128,2048]{1,0:T(8,128)(2,1)S(1)}, u32[]{:S(2)}, u32[]{:S(2)}) %collective-permute-start.64) | collective-permute-done | bytes 524320 | tf_op jit(solution)/shard_map/ppermute | solution.py:667
  484.6 9.5 %shard_map.320 = (bf16[128,2048]{1,0:T(8,128)(2,1)S(1)}, bf16[128,2048]{1,0:T(8,128)(2,1)S(1)}, bf16[128,2048]{1,0:T(8,128)(2,1)S(1)}, bf16[128,2048]{1,0:T(8,128)(2,1)S(1)}) custom-call(s32[4]{0:T(128)S(1)} %copy-done.67, bf16[1024,512]{1,0:T(8,128)(2,1)S(1)} %copy-done.72, bf16[128,2048]{1,0:T(8,128)(2,1)} %get-tuple-element.619.refs_0_.refs_2_, ...), custom_call_target="tpu_custom_call" | custom-call | flops 2147483648 | bytes 8388608 | tf_op jit(solution)/shard_map/pallas_call | solution.py:334
  504.0 13.1 %collective-permute-done.68 = bf16[512,896]{1,0:T(8,128)(2,1)} collective-permute-done((bf16[512,896]{1,0:T(8,128)(2,1)S(1)}, bf16[512,896]{1,0:T(8,128)(2,1)}, u32[]{:S(2)}, u32[]{:S(2)}) %collective-permute-start.68) | collective-permute-done | bytes 917536 | tf_op jit(solution)/shard_map/ppermute | solution.py:774
  518.4 13.0 %shard_map.322 = (bf16[2,768,512]{2,1,0:T(8,128)(2,1)S(1)}, bf16[2,768,512]{2,1,0:T(8,128)(2,1)}, bf16[2,768,512]{2,1,0:T(8,128)(2,1)S(1)}, bf16[2,768,512]{2,1,0:T(8,128)(2,1)}) custom-call(s32[4]{0:T(128)S(1)} %copy-done.67, bf16[2,640,768]{2,1,0:T(8,128)(2,1)S(1)} %copy-done.83, bf16[2,384,768]{2,1,0:T(8,128)(2,1)S(1)} %copy-done.78, ...), custom_call_target="tpu_custom_call" | custom-call | flops 6442450944 | bytes 16777216 | tf_op jit(solution)/shard_map/pallas_call | solution.py:439
  556.6 5.4 collective-permute-start.78
  575.8 11.5 %collective-permute-done.76.refs_2_ = bf16[128,2048]{1,0:T(8,128)(2,1)} collective-permute-done((bf16[128,2048]{1,0:T(8,128)(2,1)}, bf16[128,2048]{1,0:T(8,128)(2,1)}, u32[]{:S(2)}, u32[]{:S(2)}) %collective-permute-start.76) | collective-permute-done | bytes 524320 | tf_op jit(solution)/shard_map/ppermute | solution.py:667
  (553 shorter events, 304.2 us)
Async XLA Ops:
  7.2 150.1 %all-gather.4.cloned.1.call-start = ((), (), s32[]{:S(2)}) async-start(), calls=%async_computation.5 | async-start | bytes 7864320 | tf_op jit(solution)/shard_map/all_gather | solution.py:873
  24.5 32.1 %all-to-all-start = ((bf16[8,64,896]{2,1,0:T(8,128)(2,1)}), bf16[8,64,896]{2,1,0:T(8,128)(2,1)S(1)}, u32[]{:S(2)}, u32[]{:S(2)}) async-start(bf16[8,64,896]{2,1,0:T(8,128)(2,1)} %pad_maximum_fusion), calls=%async_computation | async-start | bytes 1835008 | tf_op jit(solution)/shard_map/all_to_all | solution.py:876
  29.4 188.9 %all-gather.6.cloned.1.call-start = ((), (), s32[]{:S(2)}) async-start(), calls=%async_computation.6 | async-start | bytes 7864320 | tf_op jit(solution)/shard_map/all_gather | solution.py:891
  29.5 27.2 %collective-permute-start.2 = (bf16[128,2048]{1,0:T(8,128)(2,1)S(1)}, bf16[128,2048]{1,0:T(8,128)(2,1)S(1)}, u32[]{:S(2)}, u32[]{:S(2)}) collective-permute-start(bf16[128,2048]{1,0:T(8,128)(2,1)S(1)} %collective-permute-done.refs_2_), channel_id=1, source_target_pairs={{0,1},{1,3},{3,5},{5,7},{7,6},{6,4},{4,2},{2,0},{8,9},{9,11},{11,1... | collective-permute-start | bytes 1572872 | tf_op jit(solution)/shard_map/ppermute | solution.py:667
  31.4 25.2 %collective-permute-start.3 = (bf16[128,2048]{1,0:T(8,128)(2,1)S(1)}, bf16[128,2048]{1,0:T(8,128)(2,1)S(1)}, u32[]{:S(2)}, u32[]{:S(2)}) collective-permute-start(bf16[128,2048]{1,0:T(8,128)(2,1)S(1)} %collective-permute-done.1.refs_3_), channel_id=1, source_target_pairs={{0,2},{1,0},{3,1},{5,3},{7,5},{6,7},{4,6},{2,4},{8,10},{9,8},{11,9... | collective-permute-start | bytes 1572872 | tf_op jit(solution)/shard_map/ppermute | solution.py:667
  56.7 17.0 %collective-permute-start.4 = (bf16[128,2048]{1,0:T(8,128)(2,1)S(1)}, bf16[128,2048]{1,0:T(8,128)(2,1)S(1)}, u32[]{:S(2)}, u32[]{:S(2)}) collective-permute-start(bf16[128,2048]{1,0:T(8,128)(2,1)S(1)} %collective-permute-done.2.refs_4_), channel_id=1, source_target_pairs={{0,1},{1,3},{3,5},{5,7},{7,6},{6,4},{4,2},{2,0},{8,9},{9,11},{11,1... | collective-permute-start | bytes 1572872 | tf_op jit(solution)/shard_map/ppermute | solution.py:667
  86.1 147.5 %all-gather.8.cloned.1.call-start = ((), (), s32[]{:S(2)}) async-start(), calls=%async_computation.7 | async-start | bytes 7864320 | tf_op jit(solution)/shard_map/all_gather | solution.py:919
  87.3 23.4 %collective-permute-start.10 = (bf16[128,2048]{1,0:T(8,128)(2,1)S(1)}, bf16[128,2048]{1,0:T(8,128)(2,1)S(1)}, u32[]{:S(2)}, u32[]{:S(2)}) collective-permute-start(bf16[128,2048]{1,0:T(8,128)(2,1)S(1)} %copy-done.39), channel_id=1, source_target_pairs={{0,1},{1,3},{3,5},{5,7},{7,6},{6,4},{4,2},{2,0},{8,9},{9,11},{11,1... | collective-permute-start | bytes 1572872 | tf_op jit(solution)/shard_map/ppermute | solution.py:667
  89.1 21.7 %collective-permute-start.11 = (bf16[128,2048]{1,0:T(8,128)(2,1)S(1)}, bf16[128,2048]{1,0:T(8,128)(2,1)S(1)}, u32[]{:S(2)}, u32[]{:S(2)}) collective-permute-start(bf16[128,2048]{1,0:T(8,128)(2,1)S(1)} %copy-done.39), channel_id=1, source_target_pairs={{0,2},{1,0},{3,1},{5,3},{7,5},{6,7},{4,6},{2,4},{8,10},{9,8},{11,9... | collective-permute-start | bytes 1572872 | tf_op jit(solution)/shard_map/ppermute | solution.py:667
  89.4 21.5 %collective-permute-start.14 = (bf16[128,2048]{1,0:T(8,128)(2,1)}, bf16[128,2048]{1,0:T(8,128)(2,1)}, u32[]{:S(2)}, u32[]{:S(2)}) collective-permute-start(bf16[128,2048]{1,0:T(8,128)(2,1)} %param.33), channel_id=1, source_target_pairs={{0,0},{1,8},{2,16},{3,24},{4,4},{5,12},{6,20},{7,28},{8,1},{9,9},{... | collective-permute-start | bytes 1572872 | tf_op jit(solution)/shard_map/ppermute | solution.py:909
  110.8 18.9 %collective-permute-start.15 = (bf16[128,2048]{1,0:T(8,128)(2,1)S(1)}, bf16[128,2048]{1,0:T(8,128)(2,1)S(1)}, u32[]{:S(2)}, u32[]{:S(2)}) collective-permute-start(bf16[128,2048]{1,0:T(8,128)(2,1)S(1)} %collective-permute-done.10.refs_2_), channel_id=1, source_target_pairs={{0,1},{1,3},{3,5},{5,7},{7,6},{6,4},{4,2},{2,0},{8,9},{9,11},{11,1... | collective-permute-start | bytes 1572872 | tf_op jit(solution)/shard_map/ppermute | solution.py:667
  110.9 18.9 %collective-permute-start.16 = (bf16[128,2048]{1,0:T(8,128)(2,1)S(1)}, bf16[128,2048]{1,0:T(8,128)(2,1)S(1)}, u32[]{:S(2)}, u32[]{:S(2)}) collective-permute-start(bf16[128,2048]{1,0:T(8,128)(2,1)S(1)} %collective-permute-done.11.refs_3_), channel_id=1, source_target_pairs={{0,2},{1,0},{3,1},{5,3},{7,5},{6,7},{4,6},{2,4},{8,10},{9,8},{11,9... | collective-permute-start | bytes 1572872 | tf_op jit(solution)/shard_map/ppermute | solution.py:667
  115.0 26.0 %collective-permute-start.17 = (bf16[128,2048]{1,0:T(8,128)(2,1)}, bf16[128,2048]{1,0:T(8,128)(2,1)}, u32[]{:S(2)}, u32[]{:S(2)}) collective-permute-start(bf16[128,2048]{1,0:T(8,128)(2,1)} %collective-permute-done.14.refs_1_), channel_id=1, source_target_pairs={{0,16},{8,24},{16,0},{24,8},{1,17},{9,25},{17,1},{25,9},{2,18},{10... | collective-permute-start | bytes 1572872 | tf_op jit(solution)/shard_map/ppermute | solution.py:774
  248.4 19.3 %collective-permute-start.36 = (bf16[128,2048]{1,0:T(8,128)(2,1)S(1)}, bf16[128,2048]{1,0:T(8,128)(2,1)S(1)}, u32[]{:S(2)}, u32[]{:S(2)}) collective-permute-start(bf16[128,2048]{1,0:T(8,128)(2,1)S(1)} %collective-permute-done.34), channel_id=1, source_target_pairs={{0,1},{1,3},{3,5},{5,7},{7,6},{6,4},{4,2},{2,0},{8,9},{9,11},{11,1... | collective-permute-start | bytes 1572872 | tf_op jit(solution)/shard_map/ppermute | solution.py:667
  249.9 17.8 %collective-permute-start.37 = (bf16[128,2048]{1,0:T(8,128)(2,1)S(1)}, bf16[128,2048]{1,0:T(8,128)(2,1)S(1)}, u32[]{:S(2)}, u32[]{:S(2)}) collective-permute-start(bf16[128,2048]{1,0:T(8,128)(2,1)S(1)} %collective-permute-done.35), channel_id=1, source_target_pairs={{0,2},{1,0},{3,1},{5,3},{7,5},{6,7},{4,6},{2,4},{8,10},{9,8},{11,9... | collective-permute-start | bytes 1572872 | tf_op jit(solution)/shard_map/ppermute | solution.py:667
  325.7 241.6 %reduce-scatter.3.cloned.1.call-start = ((), (), s32[]{:S(2)}) async-start(), calls=%async_computation.8 | async-start | bytes 7864320 | tf_op jit(solution)/shard_map/reduce_scatter | solution.py:1040
  337.7 21.7 %collective-permute-start.46 = (bf16[128,2048]{1,0:T(8,128)(2,1)}, bf16[128,2048]{1,0:T(8,128)(2,1)}, u32[]{:S(2)}, u32[]{:S(2)}) collective-permute-start(bf16[128,2048]{1,0:T(8,128)(2,1)} %get-tuple-element.510), channel_id=1, source_target_pairs={{0,1},{1,3},{3,5},{5,7},{7,6},{6,4},{4,2},{2,0},{8,9},{9,11},{11,1... | collective-permute-start | bytes 1572872 | tf_op jit(solution)/shard_map/ppermute | solution.py:667
  338.0 21.4 %collective-permute-start.47 = (bf16[128,2048]{1,0:T(8,128)(2,1)}, bf16[128,2048]{1,0:T(8,128)(2,1)}, u32[]{:S(2)}, u32[]{:S(2)}) collective-permute-start(bf16[128,2048]{1,0:T(8,128)(2,1)} %get-tuple-element.511), channel_id=1, source_target_pairs={{0,2},{1,0},{3,1},{5,3},{7,5},{6,7},{4,6},{2,4},{8,10},{9,8},{11,9... | collective-permute-start | bytes 1572872 | tf_op jit(solution)/shard_map/ppermute | solution.py:667
  359.4 207.8 %reduce-scatter.5.cloned.1.call-start = ((), (), s32[]{:S(2)}) async-start(), calls=%async_computation.9 | async-start | bytes 7864320 | tf_op jit(solution)/shard_map/reduce_scatter | solution.py:1057
  365.7 17.2 %collective-permute-start.48 = (bf16[128,2048]{1,0:T(8,128)(2,1)}, bf16[128,2048]{1,0:T(8,128)(2,1)S(1)}, u32[]{:S(2)}, u32[]{:S(2)}) collective-permute-start(bf16[128,2048]{1,0:T(8,128)(2,1)} %get-tuple-element.619.refs_0_.refs_2_), channel_id=1, source_target_pairs={{0,1},{1,3},{3,5},{5,7},{7,6},{6,4},{4,2},{2,0},{8,9},{9,11},{11,1... | collective-permute-start | bytes 1572872 | tf_op jit(solution)/shard_map/ppermute | solution.py:667
  366.0 16.9 %collective-permute-start.49 = (bf16[128,2048]{1,0:T(8,128)(2,1)}, bf16[128,2048]{1,0:T(8,128)(2,1)}, u32[]{:S(2)}, u32[]{:S(2)}) collective-permute-start(bf16[128,2048]{1,0:T(8,128)(2,1)} %get-tuple-element.619.refs_0_.refs_2_), channel_id=1, source_target_pairs={{0,2},{1,0},{3,1},{5,3},{7,5},{6,7},{4,6},{2,4},{8,10},{9,8},{11,9... | collective-permute-start | bytes 1572872 | tf_op jit(solution)/shard_map/ppermute | solution.py:667
  407.8 25.2 %collective-permute-start.56 = (bf16[64,2048]{1,0:T(8,128)(2,1)S(1)}, bf16[64,2048]{1,0:T(8,128)(2,1)S(1)}, u32[]{:S(2)}, u32[]{:S(2)}) collective-permute-start(bf16[64,2048]{1,0:T(8,128)(2,1)S(1)} %get-tuple-element.775), channel_id=1, source_target_pairs={{0,1},{1,3},{3,5},{5,7},{7,6},{6,4},{4,2},{2,0},{8,9},{9,11},{11,1... | collective-permute-start | bytes 786440 | tf_op jit(solution)/shard_map/ppermute | solution.py:667
  408.4 24.6 %collective-permute-start.57 = (bf16[64,2048]{1,0:T(8,128)(2,1)S(1)}, bf16[64,2048]{1,0:T(8,128)(2,1)S(1)}, u32[]{:S(2)}, u32[]{:S(2)}) collective-permute-start(bf16[64,2048]{1,0:T(8,128)(2,1)S(1)} %get-tuple-element.774), channel_id=1, source_target_pairs={{0,2},{1,0},{3,1},{5,3},{7,5},{6,7},{4,6},{2,4},{8,10},{9,8},{11,9... | collective-permute-start | bytes 786440 | tf_op jit(solution)/shard_map/ppermute | solution.py:667
  411.1 21.8 %collective-permute-start.54 = (bf16[64,2048]{1,0:T(8,128)(2,1)S(1)}, bf16[64,2048]{1,0:T(8,128)(2,1)S(1)}, u32[]{:S(2)}, u32[]{:S(2)}) collective-permute-start(bf16[64,2048]{1,0:T(8,128)(2,1)S(1)} %slice.263), channel_id=1, source_target_pairs={{0,1},{1,3},{3,5},{5,7},{7,6},{6,4},{4,2},{2,0},{8,9},{9,11},{11,1... | collective-permute-start | bytes 786440 | tf_op jit(solution)/shard_map/ppermute | solution.py:667
  413.3 19.6 %collective-permute-start.55 = (bf16[64,2048]{1,0:T(8,128)(2,1)S(1)}, bf16[64,2048]{1,0:T(8,128)(2,1)S(1)}, u32[]{:S(2)}, u32[]{:S(2)}) collective-permute-start(bf16[64,2048]{1,0:T(8,128)(2,1)S(1)} %slice.264), channel_id=1, source_target_pairs={{0,2},{1,0},{3,1},{5,3},{7,5},{6,7},{4,6},{2,4},{8,10},{9,8},{11,9... | collective-permute-start | bytes 786440 | tf_op jit(solution)/shard_map/ppermute | solution.py:667
  494.7 22.4 %collective-permute-start.68 = (bf16[512,896]{1,0:T(8,128)(2,1)S(1)}, bf16[512,896]{1,0:T(8,128)(2,1)}, u32[]{:S(2)}, u32[]{:S(2)}) collective-permute-start(bf16[512,896]{1,0:T(8,128)(2,1)S(1)} %add_convert_fusion.3), channel_id=1, source_target_pairs={{0,16},{8,24},{16,0},{24,8},{1,17},{9,25},{17,1},{25,9},{2,18},{10... | collective-permute-start | bytes 2752520 | tf_op jit(solution)/shard_map/ppermute | solution.py:774
  534.2 17.1 %collective-permute-start.73 = (bf16[128,2048]{1,0:T(8,128)(2,1)}, bf16[128,2048]{1,0:T(8,128)(2,1)}, u32[]{:S(2)}, u32[]{:S(2)}) collective-permute-start(bf16[128,2048]{1,0:T(8,128)(2,1)} %add_convert_fusion.6), channel_id=1, source_target_pairs={{0,16},{8,24},{16,0},{24,8},{1,17},{9,25},{17,1},{25,9},{2,18},{10... | collective-permute-start | bytes 1572872 | tf_op jit(solution)/shard_map/ppermute | solution.py:774
  539.1 36.7 %all-to-all-start.2 = ((bf16[8,64,896]{2,1,0:T(8,128)(2,1)}), bf16[8,64,896]{2,1,0:T(8,128)(2,1)S(1)}, u32[]{:S(2)}, u32[]{:S(2)}) async-start(bf16[8,64,896]{2,1,0:T(8,128)(2,1)} %bitcast.249), calls=%async_computation.4 | async-start | bytes 1835008 | tf_op jit(solution)/shard_map/all_to_all | solution.py:1133
  551.4 44.3 %collective-permute-start.79 = (bf16[2,768,512]{2,1,0:T(8,128)(2,1)}, bf16[2,768,512]{2,1,0:T(8,128)(2,1)}, u32[]{:S(2)}, u32[]{:S(2)}) collective-permute-start(bf16[2,768,512]{2,1,0:T(8,128)(2,1)} %add_convert_fusion), channel_id=1, source_target_pairs={{0,16},{8,24},{16,0},{24,8},{1,17},{9,25},{17,1},{25,9},{2,18},{10... | collective-permute-start | bytes 4718600 | tf_op jit(solution)/shard_map/ppermute | solution.py:774
  556.6 19.2 %collective-permute-start.78 = (bf16[128,2048]{1,0:T(8,128)(2,1)}, bf16[128,2048]{1,0:T(8,128)(2,1)}, u32[]{:S(2)}, u32[]{:S(2)}) collective-permute-start(bf16[128,2048]{1,0:T(8,128)(2,1)} %add_convert_fusion.5), channel_id=1, source_target_pairs={{0,0},{1,8},{2,16},{3,24},{4,4},{5,12},{6,20},{7,28},{8,1},{9,9},{... | collective-permute-start | bytes 1572872 | tf_op jit(solution)/shard_map/ppermute | solution.py:1149
  567.3 20.0 %collective-permute-start.76 = (bf16[128,2048]{1,0:T(8,128)(2,1)}, bf16[128,2048]{1,0:T(8,128)(2,1)}, u32[]{:S(2)}, u32[]{:S(2)}) collective-permute-start(bf16[128,2048]{1,0:T(8,128)(2,1)} %copy-done.69), channel_id=1, source_target_pairs={{0,1},{1,3},{3,5},{5,7},{7,6},{6,4},{4,2},{2,0},{8,9},{9,11},{11,1... | collective-permute-start | bytes 1572872 | tf_op jit(solution)/shard_map/ppermute | solution.py:667
  567.3 20.0 %collective-permute-start.77 = (bf16[128,2048]{1,0:T(8,128)(2,1)}, bf16[128,2048]{1,0:T(8,128)(2,1)}, u32[]{:S(2)}, u32[]{:S(2)}) collective-permute-start(bf16[128,2048]{1,0:T(8,128)(2,1)} %copy-done.68), channel_id=1, source_target_pairs={{0,2},{1,0},{3,1},{5,3},{7,5},{6,7},{4,6},{2,4},{8,10},{9,8},{11,9... | collective-permute-start | bytes 1572872 | tf_op jit(solution)/shard_map/ppermute | solution.py:667
  (169 other events, 1731.5 us)
Sparse Core Ops, SparseCore 0:
  9.6 49.0 all-gather.3
  86.2 65.5 all-gather.5
  157.5 45.9 all-gather.7
  359.6 56.9 reduce-scatter.2
  419.1 58.3 reduce-scatter.4

commit v3 on v2

--- a/solution.py
+++ b/solution.py
@@ -161,9 +161,10 @@
 
 
 def fetch(arrays, spots, buffers, sems):
-    rows = buffers[0].shape[0]
     copies = [
-        pltpu.make_async_copy(array.at[pl.ds(spot * rows, rows)], buffer, sems.at[i])
+        pltpu.make_async_copy(
+            array.at[pl.ds(spot * buffer.shape[0], buffer.shape[0])], buffer, sems.at[i]
+        )
         for i, (array, spot, buffer) in enumerate(zip(arrays, spots, buffers))
     ]
     for copy in copies:
@@ -215,7 +216,7 @@
 
 
 def mixer_back_kernel(
-    mine_ref, left_ref, right_ref, logits_ref, router_ref, middle_ref, cot_ref, gain_ref, *refs
+    mine_ref, left_ref, right_ref, middle_ref, cot_ref, logits_ref, router_ref, gain_ref, *refs
 ):
     grad_ref, branch_ref, gains_ref = refs
     grad_mixer = summed(mine_ref, left_ref, right_ref) + dot(logits_ref[...], router_ref[...], 1, 1)
@@ -232,27 +233,30 @@
     out_ref[...] = (grad_ref[...] + grad).astype(BF16)
 
 
-def by_rows(kernel, landed, inputs, outs, sums=()):
+def by_rows(kernel, landed, lines, inputs, outs, sums=()):
     (mine, spot), left, right = landed
     rows, width = left.shape
-
-    def whole(mine_hbm, *refs):
-        refs, mine_ref, sems = refs[:-2], refs[-2], refs[-1]
-        fetch((mine_hbm,), (spot,), (mine_ref,), sems)
-        kernel(mine_ref, *refs)
+    count = 1 + len(lines)
+
+    def whole(*refs):
+        arrays, refs = refs[:count], refs[count:]
+        refs, buffers, sems = refs[: -count - 1], refs[-count - 1 : -1], refs[-1]
+        fetch(arrays, (spot,) + (0,) * len(lines), buffers, sems)
+        kernel(buffers[0], *refs[:2], *buffers[1:], *refs[2:])
 
     return pl.pallas_call(
         whole,
-        in_specs=[HBM] + [VMEM] * (2 + len(inputs)),
+        in_specs=[HBM] * count + [VMEM] * (2 + len(inputs)),
         out_specs=[VMEM] * (len(outs) + len(sums)),
         out_shape=[jax.ShapeDtypeStruct((rows, width), kind) for kind in outs]
         + [jax.ShapeDtypeStruct(shape, F32) for shape in sums],
-        scratch_shapes=[pltpu.VMEM((rows, width), BF16), pltpu.SemaphoreType.DMA((1,))],
+        scratch_shapes=[pltpu.VMEM((rows, array.shape[1]), array.dtype) for array in [mine] + lines]
+        + [pltpu.SemaphoreType.DMA((count,))],
         compiler_params=pltpu.CompilerParams(vmem_limit_bytes=SMALL_LIMIT),
         cost_estimate=pl.CostEstimate(
             flops=20 * rows * width, bytes_accessed=16 * rows * width, transcendentals=rows
         ),
-    )(mine, left, right, *inputs)
+    )(mine, *lines, left, right, *inputs)
 
 
 def weights_back_kernel(held, copies, size, came_ref, own_ref, gain_ref, q_ref, k_ref, v_ref, gains_ref, small_ref):
@@ -304,42 +308,41 @@
 
 
 def output_back_kernel(count, order_ref, left_ref, *refs):
-    pieces, outs, (rows_ref, sum_ref) = refs[:count], refs[count:-2], refs[-2:]
-    step = pl.program_id(0)
-
-    def store(first, rows):
-        rows_ref[first : first + rows.shape[0]] = rows
-
-    take_piece(step, pieces, True, store)
-
-    @pl.when(step == 0)
+    pieces, outs, (rows_ref, turned_ref, sum_ref) = refs[:count], refs[count:-3], refs[-3:]
+
+    @pl.when(pl.program_id(0) == 0)
     def _():
-        sum_ref[...] = jnp.zeros_like(sum_ref)
-
-    sum_ref[...] += dot(left_ref[...], rows_ref[...], 0, 0)
-
-    @pl.when(step == pl.num_programs(0) - 1)
-    def _():
-        for i, out_ref in enumerate(outs):
-            rows = out_ref.shape[0]
-            first = pl.multiple_of(order_ref[i] * rows, rows)
-            out_ref[...] = sum_ref[pl.ds(first, rows), :].astype(BF16)
+        turned_ref[...] = left_ref[...].T
+
+    first = 0
+    for piece in pieces:
+        rows_ref[first : first + piece.shape[0]] = piece[...]
+        first += piece.shape[0]
+    sum_ref[...] = jnp.dot(turned_ref[...], rows_ref[...], preferred_element_type=F32)
+    for i, out_ref in enumerate(outs):
+        rows = out_ref.shape[0]
+        first = pl.multiple_of(order_ref[i] * rows, rows)
+        out_ref[...] = sum_ref[pl.ds(first, rows), :].astype(BF16)
 
 
 def output_back(left, pieces, order):
     rows, width = left.shape
-    block, cols = pieces[0].shape
+    cols = pieces[0].shape[1]
     parts = order.shape[0]
-    whole = lambda shape: pl.BlockSpec(shape, lambda i, order: (0, 0))
+    block = cols // 4
     return pl.pallas_call(
         lambda *refs: output_back_kernel(len(pieces), *refs),
         grid_spec=pltpu.PrefetchScalarGridSpec(
             num_scalar_prefetch=1,
-            grid=(rows // block,),
-            in_specs=[pl.BlockSpec((block, width), lambda i, order: (i, 0))]
-            + [whole(piece.shape) for piece in pieces],
-            out_specs=[whole((width // parts, cols))] * parts,
-            scratch_shapes=[pltpu.VMEM((block, cols), BF16), pltpu.VMEM((width, cols), F32)],
+            grid=(4,),
+            in_specs=[pl.BlockSpec((rows, width), lambda i, order: (0, 0))]
+            + [pl.BlockSpec((piece.shape[0], block), lambda i, order: (0, i)) for piece in pieces],
+            out_specs=[pl.BlockSpec((width // parts, block), lambda i, order: (0, i))] * parts,
+            scratch_shapes=[
+                pltpu.VMEM((rows, block), BF16),
+                pltpu.VMEM((width, rows), BF16),
+                pltpu.VMEM((width, block), F32),
+            ],
         ),
         out_shape=[jax.ShapeDtypeStruct((width // parts, cols), BF16)] * parts,
         compiler_params=params(),
@@ -349,13 +352,17 @@
     )(order, left, *pieces)
 
 
-def project_back_kernel(own_rows, order_ref, normed_ref, grad_ref, small_ref, gains_ref, *outs):
+def project_back_kernel(
+    own_rows, place, order_ref, normed_ref, grad_ref, small_ref, line_ref, gains_ref, *outs
+):
     width = grad_ref.shape[1]
     part = dot(normed_ref[...], grad_ref[...], 0, 0).astype(BF16)
     small = small_ref[...]
     size = small.shape[1]
     row = lax.broadcasted_iota(jnp.int32, small.shape, 0) % own_rows
-    upper = lax.broadcasted_iota(jnp.int32, small.shape, 1) >= size // 2
+    lane = lax.broadcasted_iota(jnp.int32, small.shape, 1)
+    small = jnp.where(lane == place, jnp.broadcast_to(line_ref[...], (size, small.shape[0])).T, small)
+    upper = lane >= size // 2
     for i in range(2):
         gain = gains_ref[i : i + 1]
         for half, line in enumerate((pltpu.roll(gain, size // 2, 1), gain)):
@@ -369,14 +376,14 @@
             out_ref[:, width:] = small
 
 
-def project_back(normed, grad, small, gains, own_rows, order):
+def project_back(normed, grad, small, line, place, gains, own_rows, order):
     rows, depth = normed.shape
     width, extra = grad.shape[1], small.shape[1]
     parts = order.shape[0]
     block = depth // parts
     whole = lambda shape: pl.BlockSpec(shape, lambda i, order: (0, 0))
     return pl.pallas_call(
-        lambda *refs: project_back_kernel(own_rows, *refs),
+        lambda *refs: project_back_kernel(own_rows, place, *refs),
         grid_spec=pltpu.PrefetchScalarGridSpec(
             num_scalar_prefetch=1,
             grid=(parts,),
@@ -384,6 +391,7 @@
                 pl.BlockSpec((rows, block), lambda i, order: (0, order[i])),
                 whole(grad.shape),
                 pl.BlockSpec((block, extra), lambda i, order: (order[i], 0)),
+                pl.BlockSpec((1, block), lambda i, order: (0, order[i])),
                 whole(gains.shape),
             ],
             out_specs=[whole((block, width + extra))] * parts,
@@ -393,42 +401,56 @@
         cost_estimate=pl.CostEstimate(
             flops=2 * rows * depth * width, bytes_accessed=12 << 20, transcendentals=0
         ),
-    )(order, normed, grad, small, gains)
-
-
-def row_grads_kernel(first_ref, second_ref, first_grad_ref, second_grad_ref, out_ref):
-    part = dot(first_ref[...], first_grad_ref[0], 0, 0)
-    out_ref[0] = (part + dot(second_ref[...], second_grad_ref[0], 0, 0)).astype(BF16)
-
-
-def row_grads(rows, grads):
-    experts, _, ff = grads[0].shape
+    )(order, normed, grad, small, line, gains)
+
+
+def row_grads_kernel(first_ref, second_ref, *refs):
+    count = len(refs) // 3
+    grads, outs = refs[: 2 * count], refs[2 * count :]
+    first, second = first_ref[...].T, second_ref[...].T
+    for i, out_ref in enumerate(outs):
+        for expert in range(out_ref.shape[0]):
+            part = dot(first, grads[2 * i][expert], 1, 0)
+            part += dot(second, grads[2 * i + 1][expert], 1, 0)
+            out_ref[expert] = part.astype(BF16)
+
+
+def row_grads(rows, *grads):
+    experts, _, ff = grads[0][0].shape
     depth = rows[0].shape[1]
-    block = depth // 4
+    block = depth // 8
     return pl.pallas_call(
         row_grads_kernel,
-        grid=(experts, 4),
-        in_specs=[pl.BlockSpec((part.shape[0], block), lambda e, i: (0, i)) for part in rows]
-        + [pl.BlockSpec((1,) + part.shape[1:], lambda e, i: (e, 0, 0)) for part in grads],
-        out_specs=pl.BlockSpec((1, block, ff), lambda e, i: (e, i, 0)),
-        out_shape=jax.ShapeDtypeStruct((experts, depth, ff), BF16),
-        compiler_params=params(),
+        grid=(8,),
+        in_specs=[pl.BlockSpec((part.shape[0], block), lambda i: (0, i)) for part in rows]
+        + [pl.BlockSpec(part.shape, lambda i: (0, 0, 0)) for pair in grads for part in pair],
+        out_specs=[pl.BlockSpec((experts, block, ff), lambda i: (0, i, 0))] * len(grads),
+        out_shape=[jax.ShapeDtypeStruct((experts, depth, ff), BF16)] * len(grads),
+        compiler_params=params(LARGE_LIMIT),
         cost_estimate=pl.CostEstimate(
-            flops=2 * experts * sum(part.shape[0] for part in rows) * ff * depth,
-            bytes_accessed=16 << 20,
+            flops=2 * len(grads) * experts * sum(part.shape[0] for part in rows) * ff * depth,
+            bytes_accessed=24 << 20,
             transcendentals=0,
         ),
-    )(*rows, *grads)
-
-
-def down_grads_kernel(order_ref, first_ref, second_ref, cot_ref, *outs):
+    )(*rows, *(part for pair in grads for part in pair))
+
+
+def down_grads_kernel(order_ref, first_ref, second_ref, cot_ref, *refs):
+    outs, turned_ref = refs[:-1], refs[-1]
+    expert, step = pl.program_id(0), pl.program_id(1)
     cut = first_ref.shape[1]
-    part = dot(first_ref[0], cot_ref[:cut], 0, 0) + dot(second_ref[0], cot_ref[cut:], 0, 0)
+
+    @pl.when(step == 0)
+    def _():
+        turned_ref[:, :cut] = first_ref[0].T
+        turned_ref[:, cut:] = second_ref[0].T
+
+    part = jnp.dot(turned_ref[...], cot_ref[...], preferred_element_type=F32).astype(BF16)
     for i, out_ref in enumerate(outs):
 
-        @pl.when(pl.program_id(0) == i)
+        @pl.when(step == i)
         def _(out_ref=out_ref):
-            out_ref[pl.program_id(1)] = part.astype(BF16)
+            out_ref[expert] = part
 
 
 def down_grads(active, cot, order):
@@ -440,13 +462,14 @@
         down_grads_kernel,
         grid_spec=pltpu.PrefetchScalarGridSpec(
             num_scalar_prefetch=1,
-            grid=(parts, experts),
+            grid=(experts, parts),
             in_specs=[
-                pl.BlockSpec((1,) + part.shape[1:], lambda i, e, order: (e, 0, 0))
+                pl.BlockSpec((1,) + part.shape[1:], lambda e, i, order: (e, 0, 0))
                 for part in active
             ]
-            + [pl.BlockSpec((rows, block), lambda i, e, order: (0, order[i]))],
-            out_specs=[pl.BlockSpec((experts, ff, block), lambda i, e, order: (0, 0, 0))] * parts,
+            + [pl.BlockSpec((rows, block), lambda e, i, order: (0, order[i]))],
+            out_specs=[pl.BlockSpec((experts, ff, block), lambda e, i, order: (0, 0, 0))] * parts,
+            scratch_shapes=[pltpu.VMEM((ff, rows), BF16)],
         ),
         out_shape=[jax.ShapeDtypeStruct((experts, ff, block), BF16)] * parts,
         compiler_params=params(),
@@ -454,6 +477,72 @@
             flops=2 * experts * rows * ff * depth, bytes_accessed=16 << 20, transcendentals=0
         ),
     )(order, *active, cot)
+
+
+def split_rows(result, outs):
+    first = 0
+    for out_ref in outs:
+        out_ref[...] = result[first : first + out_ref.shape[0]].astype(BF16)
+        first += out_ref.shape[0]
+
+
+def split_shapes(rows, block, cols, halved):
+    heights = [block] * (rows // block)
+    if halved:
+        heights[-1:] = [block // 2, block // 2]
+    return [jax.ShapeDtypeStruct((height, cols), BF16) for height in heights]
+
+
+def rows_dot(left, right, right_dim, block):
+    rows, depth = left.shape
+    cols = right.shape[1 - right_dim]
+    each = cols // 4
+    shapes = split_shapes(rows, block, cols, True)
+    if right_dim:
+        spec = pl.BlockSpec((each, depth), lambda i: (i, 0))
+    else:
+        spec = pl.BlockSpec((depth, each), lambda i: (0, i))
+    return pl.pallas_call(
+        lambda left_ref, right_ref, *outs: split_rows(
+            dot(left_ref[...], right_ref[...], 1, right_dim), outs
+        ),
+        grid=(4,),
+        in_specs=[pl.BlockSpec((rows, depth), lambda i: (0, 0)), spec],
+        out_specs=[pl.BlockSpec((shape.shape[0], each), lambda i: (0, i)) for shape in shapes],
+        out_shape=shapes,
+        compiler_params=params(),
+        cost_estimate=pl.CostEstimate(
+            flops=2 * rows * depth * cols, bytes_accessed=8 << 20, transcendentals=0
+        ),
+    )(left, right)
+
+
+def entered_kernel(first_ref, second_ref, first_w_ref, second_w_ref, *outs):
+    total = 0.0
+    for expert in range(first_ref.shape[0]):
+        total += dot(first_ref[expert], first_w_ref[expert], 1, 1)
+        total += dot(second_ref[expert], second_w_ref[expert], 1, 1)
+    split_rows(total, outs)
+
+
+def entered_rows(first, second, first_w, second_w, block):
+    experts, rows, ff = first.shape
+    depth = first_w.shape[1]
+    each = depth // 8
+    whole = pl.BlockSpec(first.shape, lambda i: (0, 0, 0))
+    weight = pl.BlockSpec((experts, each, ff), lambda i: (0, i, 0))
+    shapes = split_shapes(rows, block, depth, False)
+    return pl.pallas_call(
+        entered_kernel,
+        grid=(8,),
+        in_specs=[whole, whole, weight, weight],
+        out_specs=[pl.BlockSpec((block, each), lambda i: (0, i))] * len(shapes),
+        out_shape=shapes,
+        compiler_params=params(LARGE_LIMIT),
+        cost_estimate=pl.CostEstimate(
+            flops=4 * experts * rows * ff * depth, bytes_accessed=20 << 20, transcendentals=0
+        ),
+    )(first, second, first_w, second_w)
 
 
 def stack_heads(array, size):
@@ -694,12 +783,14 @@
 
 
 class Scatter:
-    def __init__(self, ring, piece, rows):
-        self.ring, self.step, self.piece, self.rows = ring, 0, piece, rows
+    def __init__(self, ring, piece, rows, far=None):
+        self.ring, self.step, self.piece, self.rows, self.far = ring, 0, piece, rows, far
         self.left = self.right = self.ready = None
 
     def sends(self):
         ring, rows = self.ring, self.rows
+        if self.step == 0 and self.far:
+            return self.far
         if self.step == 0:
             whole, spot = self.piece(ring.spot(ring.steps))
             start, middle, end = spot * rows, spot * rows + rows // 2, (spot + 1) * rows
@@ -885,10 +976,9 @@
         )
     cos_table, sine_table = tables
     second_half = fsdp.spread(qkv[part_rows:])
-    qkv, first_half, second_half, w_output, w_up, cotangent_sent = window(
-        [token_ring], qkv, first_half, second_half, w_output, w_up, cotangent
-    )
-    up_w = lax.all_gather(w_up, "fsdp", axis=1, tiled=True)
+    qkv, first_half, second_half, w_output, cotangent_sent = window(
+        [token_ring], qkv, first_half, second_half, w_output, cotangent
+    )
 
     cot_ring = Gather(ring, cotangent_sent)
     qkv_parts = fsdp.swapped(
@@ -911,14 +1001,17 @@
     normed_all, qk_pre, query_seq, key_seq, value_seq = projected
     attended, probs = attend(query_seq, key_seq, value_seq, places, scale_qk, tok_rows)
     held_others = fsdp.spread(held)
-    attended, probs, held, held_others = window([cot_ring], attended, probs, held, held_others)
+    attended, probs, held, held_others, w_up = window(
+        [cot_ring], attended, probs, held, held_others, w_up
+    )
+    up_w = lax.all_gather(w_up, "fsdp", axis=1, tiled=True)
     output_w = lay(fsdp.swapped(held, held_others), fsdp.blocks)
-    branch = jnp.dot(attended, output_w, preferred_element_type=F32).astype(BF16)
+    branch = rows_dot(attended, output_w, 0, tok_rows)
     for step in range(3, ring.steps):
         branch, output_w, gate_w, w_down = window([cot_ring], branch, output_w, gate_w, w_down)
     down_w = lax.all_gather(w_down, "fsdp", axis=2, tiled=True)
 
-    branch_ring = Scatter(ring, lambda spot: (branch, spot), tok_rows)
+    branch_ring = Scatter(ring, lambda spot: (branch[spot], 0), tok_rows, tuple(branch[-2:]))
     (qkv_parts,) = window([branch_ring, cot_ring], qkv_parts)
 
     def small_arrays(parts):
@@ -941,7 +1034,7 @@
         qkv_w, cot_all = window([branch_ring], qkv_w, cot_all)
     (up_w,) = window([branch_ring], up_w)
     middle, mixer_in = by_rows(
-        enter_kernel, branch_ring.landed(), [tokens, gain_mlp], [F32, BF16]
+        enter_kernel, branch_ring.landed(), [tokens], [gain_mlp], [F32, BF16]
     )
 
     def shares(rows_in, ids):
@@ -953,12 +1046,15 @@
         grown = jnp.exp(masked - jnp.max(masked, axis=-1, keepdims=True)) * chosen
         return grown / jnp.sum(grown, axis=-1, keepdims=True)
 
-    def expert_part(rows_in, first):
+    def gate_part(rows_in, first):
         last = first + rows_in.shape[0]
         share = lax.dynamic_slice_in_dim(
             shares(rows_in, ids_near[:, first:last]), seat * local_experts, local_experts, 1
         ).T[:, :, None]
-        gate_pre = jnp.einsum("td,edf->etf", rows_in, gate_w, preferred_element_type=F32)
+        return share, jnp.einsum("td,edf->etf", rows_in, gate_w, preferred_element_type=F32)
+
+    def expert_part(rows_in, first, share, gate_pre):
+        last = first + rows_in.shape[0]
         up_pre = jnp.einsum("td,edf->etf", rows_in, up_w, preferred_element_type=F32)
         back = down_back[:, first:last]
         sigmoid = jax.nn.sigmoid(gate_pre)
@@ -982,18 +1078,22 @@
     cut = ring.steps // 2
     early = (2 * cut + 1) * tok_rows
     mixer_ring = Gather(ring, mixer_in)
-    cot_all, down_w = window([mixer_ring], cot_all, down_w)
+    (cot_all,) = window([mixer_ring], cot_all)
+    cot_all, down_w = prepare([mixer_ring], cot_all, down_w)
     down_back = jnp.einsum("td,efd->etf", cot_all, down_w, preferred_element_type=F32)
     (down_back,) = window([mixer_ring], down_back)
     for step in range(3, cut + 1):
         window([mixer_ring])
     early_rows = jnp.concatenate(mixer_ring.pieces, axis=0)
-    early_part = expert_part(early_rows, 0)
+    early_share, early_gate = gate_part(early_rows, 0)
     for step in range(cut + 1, ring.steps):
-        (early_rows,) = window([mixer_ring], early_rows)
+        early_rows, early_share, early_gate = window(
+            [mixer_ring], early_rows, early_share, early_gate
+        )
+    early_part = expert_part(early_rows, 0, early_share, early_gate)
     early_part, early_rows = window([mixer_ring], early_part, early_rows)
     late_rows = jnp.concatenate(mixer_ring.pieces[2 * cut + 1 :], axis=0)
-    late_part = expert_part(late_rows, early)
+    late_part = expert_part(late_rows, early, *gate_part(late_rows, early))
     late_entered = entered_part(late_part)
     late_entered, late_part, early_part, late_rows, early_rows = together(
         late_entered, late_part, early_part, late_rows, early_rows
@@ -1002,7 +1102,7 @@
     def entered_piece(spot):
         if spot * tok_rows >= early:
             return late_entered, spot - early // tok_rows
-        return early_entered, spot
+        return early_entered[spot], 0
 
     entered_ring = Scatter(ring, entered_piece, tok_rows)
     grad_share = jnp.concatenate([early_part[0], late_part[0]], axis=1)
@@ -1015,15 +1115,22 @@
         concat_axis=0,
         tiled=True,
     )
-    early_entered = entered_part(early_part)
+    early_entered = entered_rows(
+        early_part[2], early_part[3], gate_w, up_w, tok_rows
+    )
     window([entered_ring])
     early_entered, early_part, late_part, early_rows, late_rows = window(
         [entered_ring], early_entered, early_part, late_part, early_rows, late_rows
     )
+    early_part, late_part, early_rows, late_rows = prepare(
+        [entered_ring], early_part, late_part, early_rows, late_rows
+    )
+    (grad_gate,) = row_grads((early_rows, late_rows), (early_part[2], late_part[2]))
     for step in range(3, ring.steps):
-        early_part, late_part, early_rows, late_rows, grad_share_own = window(
-            [entered_ring], early_part, late_part, early_rows, late_rows, grad_share_own
+        grad_gate, early_part, late_part, early_rows, late_rows, grad_share_own = window(
+            [entered_ring], grad_gate, early_part, late_part, early_rows, late_rows, grad_share_own
         )
+    grad_gate = lax.psum_scatter(grad_gate, "fsdp", scatter_dimension=1, tiled=True)
     early_part, late_part, early_rows, late_rows, grad_share_own = prepare(
         [entered_ring], early_part, late_part, early_rows, late_rows, grad_share_own
     )
@@ -1033,28 +1140,22 @@
         share_own
         * (grad_share_own - jnp.sum(share_own * grad_share_own, axis=-1, keepdims=True))
     ).astype(BF16)
-    grad_gate = row_grads((early_rows, late_rows), (early_part[2], late_part[2]))
-    grad_gate, grad_logits, early_part, late_part, early_rows, late_rows = window(
-        [entered_ring], grad_gate, grad_logits, early_part, late_part, early_rows, late_rows
-    )
-    grad_gate = lax.psum_scatter(grad_gate, "fsdp", scatter_dimension=1, tiled=True)
+    (grad_up,) = row_grads((early_rows, late_rows), (early_part[3], late_part[3]))
+    grad_up, grad_logits, early_active, late_active = window(
+        [entered_ring], grad_up, grad_logits, early_part[1], late_part[1]
+    )
+    grad_up = lax.psum_scatter(grad_up, "fsdp", scatter_dimension=1, tiled=True)
     grad_middle, grad_branch, grad_gain_m = by_rows(
         mixer_back_kernel,
         entered_ring.landed(),
-        [grad_logits, router_w, middle, cotangent, gain_mlp],
+        [middle, cotangent],
+        [grad_logits, router_w, gain_mlp],
         [F32, BF16],
         [(1, model_width)],
     )
 
     grads_ring = Gather(ring, grad_branch)
-    early_part, late_part, early_rows, late_rows = prepare(
-        [grads_ring], early_part, late_part, early_rows, late_rows
-    )
-    grad_up = row_grads((early_rows, late_rows), (early_part[3], late_part[3]))
-    grad_up, early_active, late_active = window(
-        [grads_ring], grad_up, early_part[1], late_part[1]
-    )
-    grad_up = lax.psum_scatter(grad_up, "fsdp", scatter_dimension=1, tiled=True)
+    early_active, late_active = prepare([grads_ring], early_active, late_active)
     produced = [
         jnp.einsum("etf,efd->td", active, down_w, preferred_element_type=F32).astype(BF16)
         for active in (early_active, late_active)
@@ -1062,6 +1163,10 @@
     produced, early_active, late_active = window(
         [grads_ring], produced, early_active, late_active
     )
+    early_active, late_active = prepare([grads_ring], early_active, late_active)
+    down_parts = down_grads((early_active, late_active), cot_all, fsdp.targets)
+    (down_parts,) = window([grads_ring], down_parts)
+    paired_down = fsdp.pair(down_parts)
     for step in range(3, cut + 1):
         window([grads_ring])
 
@@ -1091,29 +1196,32 @@
         )
 
     grads = back(grads_ring.pieces, 0, None)
-    grad_small = jnp.concatenate([dot(mixer_in, grad_logits, 0, 0), grad_gain_m.T], axis=1)
-    grad_small = jnp.pad(grad_small, ((0, 0), (0, head_size - grad_small.shape[1])))
+    grad_small = dot(mixer_in, jnp.pad(grad_logits, ((0, 0), (0, head_size - experts_all))), 0, 0)
     for step in range(cut + 1, ring.steps):
-        (grad_small,) = window([grads_ring], grad_small)
+        grad_small, paired_down = window([grads_ring], grad_small, paired_down)
     layer_ring = Scatter(ring, two_parts(produced), tok_rows)
     (grads,) = window([grads_ring, layer_ring], grads)
     grads = back(grads_ring.pieces[2 * cut + 1 :], 2 * cut + 1, grads)
     (grads,) = window([layer_ring], grads)
 
-    grads, grad_small = prepare([layer_ring], grads, grad_small)
+    grads, grad_small, branch_pieces = prepare(
+        [layer_ring], grads, grad_small, grads_ring.pieces
+    )
     grad_qkv = grads[0]
-    paired = fsdp.pair(
-        project_back(normed_all, grad_qkv, grad_small, grads[1], own_rows, fsdp.targets)
-    )
+    grad_parts = project_back(
+        normed_all, grad_qkv, grad_small, grad_gain_m, experts_all, grads[1], own_rows, fsdp.targets
+    )
+    output_parts = output_back(attended, branch_pieces, fsdp.targets)
     for step in range(3, ring.steps):
-        paired, grad_qkv = window([layer_ring], paired, grad_qkv)
-    paired, grad_qkv, early_active, late_active = prepare(
-        [layer_ring], paired, grad_qkv, early_active, late_active
-    )
+        grad_parts, grad_qkv, output_parts = window(
+            [layer_ring], grad_parts, grad_qkv, output_parts
+        )
+    paired = fsdp.pair(grad_parts)
     sent = fsdp.send(paired)
-    grad_hidden = dot(grad_qkv, qkv_w[:, :qkv_width], 1, 1).astype(BF16)
-    grad_hidden, paired, branch_pieces, early_active, late_active = window(
-        [layer_ring], grad_hidden, paired, grads_ring.pieces, early_active, late_active
+    paired_output = fsdp.pair(output_parts)
+    grad_hidden = rows_dot(grad_qkv, qkv_w, 1, tok_rows)
+    grad_hidden, paired, sent, paired_output = window(
+        [layer_ring], grad_hidden, paired, sent, paired_output
     )
     (produced, spot), left, right = layer_ring.landed()
     layer_out = (
@@ -1123,11 +1231,8 @@
         + right.astype(F32)
     ).astype(BF16)
 
-    hidden_ring = Scatter(ring, lambda spot: (grad_hidden, spot), tok_rows)
-    branch_pieces, paired = prepare([hidden_ring], branch_pieces, paired)
-    paired_output = fsdp.pair(output_back(attended, branch_pieces, fsdp.targets))
-    paired, sent, paired_output, early_active, late_active = window(
-        [hidden_ring], paired, sent, paired_output, early_active, late_active
+    hidden_ring = Scatter(
+        ring, lambda spot: (grad_hidden[spot], 0), tok_rows, tuple(grad_hidden[-2:])
     )
     total = paired[0].astype(F32) + sum(part.astype(F32) for part in sent)
     grad_qkv_w = lax.all_to_all(
@@ -1138,34 +1243,33 @@
         tiled=True,
     )
     sent_output = fsdp.send(paired_output)
-    early_active, late_active, paired_output = prepare(
-        [hidden_ring], early_active, late_active, paired_output
-    )
-    paired_down = fsdp.pair(down_grads((early_active, late_active), cot_all, fsdp.targets))
     paired_output, sent_output, paired_down = window(
+        [hidden_ring], paired_output, sent_output, paired_down
+    )
+    paired_output, sent_output, paired_down = prepare(
         [hidden_ring], paired_output, sent_output, paired_down
     )
     total = paired_output[0].astype(F32) + sum(part.astype(F32) for part in sent_output)
     grad_output_w = lax.ppermute(total.astype(BF16), ALL, exchange)
     sent_down = fsdp.send(paired_down)
+    grad_qkv_w, grad_output_w, grad_gate, grad_up = window(
+        [hidden_ring], grad_qkv_w, grad_output_w, grad_gate, grad_up
+    )
 
     def corner(array):
         return lax.slice(array, (0,) * array.ndim, (1,) * (array.ndim - 2) + (8, 128))
 
-    grad_gate, grad_up = prepare([hidden_ring], grad_gate, grad_up)
+    grad_gate, grad_up, grad_output_w = prepare([hidden_ring], grad_gate, grad_up, grad_output_w)
     grad_gate, grad_up = grad_gate.astype(F32), grad_up.astype(F32)
+    grad_output_w = grad_output_w.astype(F32)
+    corners = [corner(array) for array in (grad_gate, grad_up, grad_output_w, layer_out)]
     for step in range(3, ring.steps):
-        grad_qkv_w, grad_output_w, _ = window(
-            [hidden_ring], grad_qkv_w, grad_output_w, [corner(grad_gate), corner(grad_up)]
-        )
-    grad_output_w, paired_down, sent_down = prepare(
-        [hidden_ring], grad_output_w, paired_down, sent_down
-    )
-    grad_output_w = grad_output_w.astype(F32)
+        paired_down, corners = window([hidden_ring], paired_down, corners)
+    (paired_down,) = prepare([hidden_ring], paired_down)
     grad_down = paired_down[0].astype(F32) + sum(part.astype(F32) for part in sent_down)
-    window([hidden_ring], [corner(grad_output_w), corner(grad_down), corner(layer_out)])
+    window([hidden_ring], [corner(grad_down)])
     (grad_tokens,) = by_rows(
-        tokens_back_kernel, hidden_ring.landed(), [tokens, grad_middle], [BF16]
+        tokens_back_kernel, hidden_ring.landed(), [tokens, grad_middle], [], [BF16]
     )
     grad_query_w, grad_key_w, grad_value_w, grad_gain_a, small = weights_back(
         grad_qkv_w,

time: 628 us -> 593 us (0.944)
  waiting for transfers between devices: 171 us -> 138 us
  Pallas kernels: 127 us -> 148 us
  matrix products: 75 us -> 55 us
  starting transfers between devices: 111 us -> 127 us
  local copies, waits for them, and re-layouts: 74.5 us -> 59.6 us
    pallas_call x6 -> x9, Pallas kernels: 31.5 us -> 59.3 us  [the longest x2 27.4 us: row_grads(): pl.pallas_call(row_grads_kernel, grid=(8,), in_specs=[pl.BlockSpec((part....]
    ppermute x32, starting transfers between devices: 37.1 us -> 55.5 us  [swap(): lax.ppermute(down, 'seq', self.down)]
    ppermute x6, waiting for transfers between devices: 33.4 us -> 20.3 us  [shift(): return lax.ppermute(array, 'fsdp', perm)]
    ppermute x32, waiting for transfers between devices: 18.3 us -> 8.38 us  [swap(): lax.ppermute(down, 'seq', self.down)]
    all_to_all x1, waiting for transfers between devices: 9.33 us -> 0.01 us  [on_device(): lax.all_to_all(jnp.take(grad_share.reshape(local_experts, groups, tok_row...]
    unnamed x233 -> x259, local copies, waits for them, and re-layouts: 47.9 us -> 39.4 us
    dot_general x2 -> x1, matrix products: 8.95 us -> 2.63 us  [entered_part(): jnp.einsum('etf,edf->td', part[3], up_w, preferred_element_type=F32)]
    dot_general x3 -> x2, matrix products: 14.3 us -> 10.4 us  [gate_part(): jnp.einsum('td,edf->etf', rows_in, gate_w, preferred_element_type=F32)]
  transfers between devices with their start and end apart: 90 -> 90, of which waited for: 42 -> 27; matrix products, arithmetic and copies ran while one was open for 22% -> 18% of each run, Pallas kernels for 20% -> 25%
where the time goes in v3:
time: 593 us; the launch traced here: 582 us
  Pallas kernels  148 us (25%)
  waiting for transfers between devices  138 us (23%)
  starting transfers between devices  127 us (21%)
  local copies, waits for them, and re-layouts  59.6 us (10%)
  matrix products  55 us (9%)
  other arithmetic  37.5 us (6%)
  between operations  16.1 us (3%)
    ppermute x32, waiting for transfers between devices, swap(): lax.ppermute(up, 'seq', self.up)  109 us
    ppermute x32, starting transfers between devices, swap(): lax.ppermute(down, 'seq', self.down)  55.5 us
    unnamed x259, local copies, waits for them, and re-layouts  39.4 us
    ppermute x32, starting transfers between devices, swap(): lax.ppermute(up, 'seq', self.up)  36.2 us
    pallas_call x2, Pallas kernels, row_grads(): pl.pallas_call(row_grads_kernel, grid=(8,), in_specs=[pl.BlockSpec((part....  27.4 us
    pallas_call x2, Pallas kernels, attend_back(): pl.pallas_call(lambda *refs: attend_back_kernel(scale, len(pieces), first...  27.1 us
    ppermute x6, waiting for transfers between devices, shift(): return lax.ppermute(array, 'fsdp', perm)  20.3 us
    dot_general x2, matrix products, expert_part(): jnp.einsum('td,edf->etf', rows_in, up_w, preferred_element_type=F32)  14.1 us
  transfers between devices with their start and end apart: 90, of which 27 were waited for; matrix products, arithmetic and copies ran while one was open for 18% of the time, Pallas kernels for 25%

profile of v3, /device:TPU:0, one launch (start us, length us, event | category | flops | bytes accessed | tf_op | source)
XLA Modules:
  0.0 581.8 jit_solution(15880935318598795852)
XLA Ops:
  24.5 4.9 all-to-all-start
  32.2 24.4 %collective-permute-done.2.refs_4_ = bf16[128,2048]{1,0:T(8,128)(2,1)S(1)} collective-permute-done((bf16[128,2048]{1,0:T(8,128)(2,1)S(1)}, bf16[128,2048]{1,0:T(8,128)(2,1)S(1)}, u32[]{:S(2)}, u32[]{:S(2)}) %collective-permute-start.2) | collective-permute-done | bytes 524320 | tf_op jit(solution)/shard_map/ppermute | solution.py:756
  58.1 5.3 collective-permute-start.5
  68.4 5.2 collective-permute-done.6
  88.7 5.4 collective-permute-start.14
  96.2 13.8 %shard_map.299 = (bf16[1024,2048]{1,0:T(8,128)(2,1)}, f32[1024,640]{1,0:T(8,128)}, bf16[1024,512]{1,0:T(8,128)(2,1)}, bf16[1024,128]{1,0:T(8,128)(2,1)}, bf16[1024,128]{1,0:T(8,128)(2,1)}) custom-call(s32[4]{0:T(128)} %fusion.55.refs_0_.order_ref, bf16[128,2048]{1,0:T(8,128)(2,1)} %refs_1_.6, bf16[128,2048]{1,0:T(8,128)(2,1)} %copy-done.108, ...), custom_call_target="tpu_custom_call" | custom-call | flops 3221225472 | bytes 16777216 | tf_op jit(solution)/shard_map/pallas_call | solution.py:137
  110.1 4.7 collective-permute-start.16
  116.8 12.5 %shard_map.300 = (bf16[1024,512]{1,0:T(8,128)(2,1)}, bf16[1024,4096]{1,0:T(8,128)(2,1)}) custom-call(bf16[1024,512]{1,0:T(8,128)(2,1)} %get-tuple-element.429.refs_0_.refs_7_.refs_6_, bf16[1024,128]{1,0:T(8,128)(2,1)} %get-tuple-element.430.refs_1_.refs_8_.refs_7_, bf16[1024,128]{1,0:T(8,128)(2,1)} %get-tuple-element.431.refs_2_.refs_9_.refs_8_, ...), custom_call_target="tpu_custom_call" | custom-call | flops 2147483648 | bytes 12582912 | tf_op jit(solution)/shard_map/pallas_call | solution.py:573
  157.3 4.8 collective-permute-done.24.refs_8_
  200.3 9.9 %collective-permute-done.30.refs_2_ = bf16[128,2048]{1,0:T(8,128)(2,1)S(1)} collective-permute-done((bf16[128,2048]{1,0:T(8,128)(2,1)S(1)}, bf16[128,2048]{1,0:T(8,128)(2,1)S(1)}, u32[]{:S(2)}, u32[]{:S(2)}) %collective-permute-start.30) | collective-permute-done | bytes 524320 | tf_op jit(solution)/shard_map/ppermute | solution.py:756
  217.4 8.2 %collective-permute-done.32 = bf16[128,2048]{1,0:T(8,128)(2,1)S(1)} collective-permute-done((bf16[128,2048]{1,0:T(8,128)(2,1)S(1)}, bf16[128,2048]{1,0:T(8,128)(2,1)S(1)}, u32[]{:S(2)}, u32[]{:S(2)}) %collective-permute-start.32) | collective-permute-done | bytes 524320 | tf_op jit(solution)/shard_map/ppermute | solution.py:756
  229.6 10.1 %fusion.7 = f32[2,1024,768]{2,1,0:T(8,128)S(1)} fusion(bf16[2,768,2048]{2,1,0:T(8,128)(2,1)} %all-gather.8.cloned.1.call-done, bf16[1024,2048]{1,0:T(8,128)(2,1)} %copy-done.11), kind=kOutput, calls=%fused_computation.22 | convolution fusion | flops 6442450944 | bytes 16777216 | tf_op jit(solution)/shard_map/td,efd->etf/dot_general | solution.py:1083
  243.4 7.8 %fusion.21 = f32[2,640,768]{2,1,0:T(8,128)S(1)} fusion(bf16[2,2048,768]{2,1,0:T(8,128)(2,1)} %all-gather.4.cloned.1.call-done.first_w_ref, bf16[640,2048]{1,0:T(8,128)(2,1)} %constant_dynamic-update-slice_fusion.2.first_ref), kind=kOutput, calls=%fused_computation.42 | convolution fusion | flops 4026531840 | bytes 12845056 | tf_op jit(solution)/shard_map/td,edf->etf/dot_general | solution.py:1054
  256.6 9.5 %fusion.4 = (bf16[2,640,768]{2,1,0:T(8,128)(2,1)}, f32[2,640]{1,0:T(2,128)S(1)}, bf16[2,640,768]{2,1,0:T(8,128)(2,1)}, bf16[2,640,768]{2,1,0:T(8,128)(2,1)}) fusion(f32[2,640,768]{2,1,0:T(8,128)S(1)} %fusion.21, f32[2,1024,768]{2,1,0:T(8,128)S(1)} %fusion.7, f32[2,640]{1,0:T(2,128)S(1)} %bitcast.224, bf16[2,2048,768]{2,1,0:T(8,128)(2,1)S(1)} %bitcast.232, ...), kind=kOutput, calls=%fused_computation.10 | convolution fusion | flops 4045208320 | bytes 22685696 | tf_op jit(solution)/shard_map/td,edf->etf/dot_general | solution.py:1058
  290.4 13.7 %shard_map.310 = (bf16[128,2048]{1,0:T(8,128)(2,1)}, bf16[128,2048]{1,0:T(8,128)(2,1)}, bf16[128,2048]{1,0:T(8,128)(2,1)}, bf16[128,2048]{1,0:T(8,128)(2,1)}, bf16[128,2048]{1,0:T(8,128)(2,1)}) custom-call(bf16[2,640,768]{2,1,0:T(8,128)(2,1)} %get-tuple-element.571.first_ref.refs_0_, bf16[2,640,768]{2,1,0:T(8,128)(2,1)} %get-tuple-element.592.second_ref.refs_0_, ...), custom_call_target="tpu_custom_call" | custom-call | flops 8053063680 | bytes 20971520 | tf_op jit(solution)/shard_map/pallas_call | solution.py:535
  309.6 13.2 %shard_map.312 = bf16[2,2048,768]{2,1,0:T(8,128)(2,1)} custom-call(bf16[640,2048]{1,0:T(8,128)(2,1)} %constant_dynamic-update-slice_fusion.2.first_ref, bf16[384,2048]{1,0:T(8,128)(2,1)} %copy-done.98, bf16[2,640,768]{2,1,0:T(8,128)(2,1)} %get-tuple-element.571.first_ref.refs_0_, bf16[2,384,768]{2,1,0:T(8,128)(2,1)} %copy-done.116), custom_call_target="tpu_custom_call" | custom-call | flops 6442450944 | bytes 25165824 | tf_op jit(solution)/shard_map/pallas_call | solution.py:422
  327.9 14.3 %shard_map.314 = bf16[2,2048,768]{2,1,0:T(8,128)(2,1)} custom-call(bf16[640,2048]{1,0:T(8,128)(2,1)} %constant_dynamic-update-slice_fusion.2.first_ref, bf16[384,2048]{1,0:T(8,128)(2,1)} %copy-done.98, bf16[2,640,768]{2,1,0:T(8,128)(2,1)} %get-tuple-element.592.second_ref.refs_0_, bf16[2,384,768]{2,1,0:T(8,128)(2,1)} %copy-done.117), custom_call_target="tpu_custom_call" | custom-call | flops 6442450944 | bytes 25165824 | tf_op jit(solution)/shard_map/pallas_call | solution.py:422
  349.3 7.6 %bitcast_convert_fusion.refs_0_.refs_1_ = bf16[640,2048]{1,0:T(8,128)(2,1)S(1)} fusion(bf16[2,640,768]{2,1,0:T(8,128)(2,1)S(1)} %copy-done.96, bf16[2,768,2048]{2,1,0:T(8,128)(2,1)} %all-gather.8.cloned.1.call-done), kind=kOutput, calls=%fused_computation.3 | convolution fusion | flops 4027842560 | bytes 10878976 | tf_op jit(solution)/shard_map/etf,efd->td/dot_general | solution.py:1160
  361.7 10.8 %shard_map.316 = (bf16[2,768,512]{2,1,0:T(8,128)(2,1)S(1)}, bf16[2,768,512]{2,1,0:T(8,128)(2,1)S(1)}, bf16[2,768,512]{2,1,0:T(8,128)(2,1)S(1)}, bf16[2,768,512]{2,1,0:T(8,128)(2,1)S(1)}) custom-call(s32[4]{0:T(128)S(1)} %copy-done.87, bf16[2,640,768]{2,1,0:T(8,128)(2,1)S(1)} %copy-done.96, bf16[2,384,768]{2,1,0:T(8,128)(2,1)S(1)} %copy-done.95, ...), custom_call_target="tpu_custom_call" | custom-call | flops 6442450944 | bytes 16777216 | tf_op jit(solution)/shard_map/pallas_call | solution.py:461
  382.2 12.0 %collective-permute-done.52.refs_0_.refs_7_ = bf16[128,2048]{1,0:T(8,128)(2,1)S(1)} collective-permute-done((bf16[128,2048]{1,0:T(8,128)(2,1)}, bf16[128,2048]{1,0:T(8,128)(2,1)S(1)}, u32[]{:S(2)}, u32[]{:S(2)}) %collective-permute-start.52) | collective-permute-done | bytes 524320 | tf_op jit(solution)/shard_map/ppermute | solution.py:756
  397.0 15.8 %shard_map.317 = (bf16[1024,768]{1,0:T(8,128)(2,1)S(1)}, f32[8,128]{1,0:T(8,128)S(1)}, f32[1024,128]{1,0:T(8,128)S(1)}, f32[1024,128]{1,0:T(8,128)S(1)}) custom-call(bf16[128,2048]{1,0:T(8,128)(2,1)S(1)} %get-tuple-element.666.refs_0_.refs_2_, bf16[128,2048]{1,0:T(8,128)(2,1)S(1)} %copy-done.43, bf16[128,2048]{1,0:T(8,128)(2,1)S(1)} %copy-done.45, ...), custom_call_target="tpu_custom_call" | custom-call | flops 4026531840 | bytes 15728640 | tf_op jit(solution)/shard_map/pallas_call | solution.py:690
  415.2 11.3 %shard_map.319 = (bf16[1024,768]{1,0:T(8,128)(2,1)S(1)}, f32[8,128]{1,0:T(8,128)S(1)}, f32[1024,128]{1,0:T(8,128)}, f32[1024,128]{1,0:T(8,128)}) custom-call(bf16[128,2048]{1,0:T(8,128)(2,1)S(1)} %collective-permute-done.52.refs_0_.refs_7_, bf16[128,2048]{1,0:T(8,128)(2,1)S(1)} %collective-permute-done.53.refs_1_.refs_8_, ...), custom_call_target="tpu_custom_call" | custom-call | flops 2415919104 | bytes 9437184 | tf_op jit(solution)/shard_map/pallas_call | solution.py:690
  429.0 5.5 shard_map.322
  436.7 5.5 shard_map.321
  458.3 15.0 %collective-permute-done.68 = bf16[512,896]{1,0:T(8,128)(2,1)S(1)} collective-permute-done((bf16[512,896]{1,0:T(8,128)(2,1)S(1)}, bf16[512,896]{1,0:T(8,128)(2,1)S(1)}, u32[]{:S(2)}, u32[]{:S(2)}) %collective-permute-start.68) | collective-permute-done | bytes 917536 | tf_op jit(solution)/shard_map/ppermute | solution.py:865
  474.5 5.5 all-to-all-start.2
  482.2 17.3 %collective-permute-done.71.refs_2_ = bf16[64,2048]{1,0:T(8,128)(2,1)S(1)} collective-permute-done((bf16[64,2048]{1,0:T(8,128)(2,1)}, bf16[64,2048]{1,0:T(8,128)(2,1)S(1)}, u32[]{:S(2)}, u32[]{:S(2)}) %collective-permute-start.71) | collective-permute-done | bytes 262176 | tf_op jit(solution)/shard_map/ppermute | solution.py:756
  505.7 6.8 %collective-permute-start.75 = (bf16[128,2048]{1,0:T(8,128)(2,1)}, bf16[128,2048]{1,0:T(8,128)(2,1)}, u32[]{:S(2)}, u32[]{:S(2)}) collective-permute-start(bf16[128,2048]{1,0:T(8,128)(2,1)} %get-tuple-element.727), channel_id=1, source_target_pairs={{0,2},{1,0},{3,1},{5,3},{7,5},{6,7},{4,6},{2,4},{8,10},{9,8},{11,9... | collective-permute-start | bytes 1572872 | tf_op jit(solution)/shard_map/ppermute | solution.py:756
  514.4 5.4 collective-permute-start.76
  520.5 5.0 collective-permute-done.74.refs_2_
  534.7 6.6 %collective-permute-start.78 = (bf16[128,2048]{1,0:T(8,128)(2,1)}, bf16[128,2048]{1,0:T(8,128)(2,1)}, u32[]{:S(2)}, u32[]{:S(2)}) collective-permute-start(bf16[128,2048]{1,0:T(8,128)(2,1)} %get-tuple-element.742), channel_id=1, source_target_pairs={{0,2},{1,0},{3,1},{5,3},{7,5},{6,7},{4,6},{2,4},{8,10},{9,8},{11,9... | collective-permute-start | bytes 1572872 | tf_op jit(solution)/shard_map/ppermute | solution.py:756
  545.6 8.5 %collective-permute-done.77.refs_2_ = bf16[128,2048]{1,0:T(8,128)(2,1)} collective-permute-done((bf16[128,2048]{1,0:T(8,128)(2,1)}, bf16[128,2048]{1,0:T(8,128)(2,1)}, u32[]{:S(2)}, u32[]{:S(2)}) %collective-permute-start.77) | collective-permute-done | bytes 524320 | tf_op jit(solution)/shard_map/ppermute | solution.py:756
  (573 shorter events, 259.6 us)
Async XLA Ops:
  7.2 139.5 %all-gather.4.cloned.1.call-start = ((), (), s32[]{:S(2)}) async-start(), calls=%async_computation.5 | async-start | bytes 7864320 | tf_op jit(solution)/shard_map/all_gather | solution.py:964
  24.5 32.1 %all-to-all-start = ((bf16[8,64,896]{2,1,0:T(8,128)(2,1)}), bf16[8,64,896]{2,1,0:T(8,128)(2,1)S(1)}, u32[]{:S(2)}, u32[]{:S(2)}) async-start(bf16[8,64,896]{2,1,0:T(8,128)(2,1)} %pad_maximum_fusion), calls=%async_computation | async-start | bytes 1835008 | tf_op jit(solution)/shard_map/all_to_all | solution.py:967
  29.4 182.3 %all-gather.6.cloned.1.call-start = ((), (), s32[]{:S(2)}) async-start(), calls=%async_computation.6 | async-start | bytes 7864320 | tf_op jit(solution)/shard_map/all_gather | solution.py:1007
  29.5 27.2 %collective-permute-start.2 = (bf16[128,2048]{1,0:T(8,128)(2,1)S(1)}, bf16[128,2048]{1,0:T(8,128)(2,1)S(1)}, u32[]{:S(2)}, u32[]{:S(2)}) collective-permute-start(bf16[128,2048]{1,0:T(8,128)(2,1)S(1)} %collective-permute-done.refs_2_), channel_id=1, source_target_pairs={{0,1},{1,3},{3,5},{5,7},{7,6},{6,4},{4,2},{2,0},{8,9},{9,11},{11,1... | collective-permute-start | bytes 1572872 | tf_op jit(solution)/shard_map/ppermute | solution.py:756
  31.4 25.2 %collective-permute-start.3 = (bf16[128,2048]{1,0:T(8,128)(2,1)S(1)}, bf16[128,2048]{1,0:T(8,128)(2,1)S(1)}, u32[]{:S(2)}, u32[]{:S(2)}) collective-permute-start(bf16[128,2048]{1,0:T(8,128)(2,1)S(1)} %collective-permute-done.1.refs_3_), channel_id=1, source_target_pairs={{0,2},{1,0},{3,1},{5,3},{7,5},{6,7},{4,6},{2,4},{8,10},{9,8},{11,9... | collective-permute-start | bytes 1572872 | tf_op jit(solution)/shard_map/ppermute | solution.py:756
  56.7 17.0 %collective-permute-start.4 = (bf16[128,2048]{1,0:T(8,128)(2,1)S(1)}, bf16[128,2048]{1,0:T(8,128)(2,1)S(1)}, u32[]{:S(2)}, u32[]{:S(2)}) collective-permute-start(bf16[128,2048]{1,0:T(8,128)(2,1)S(1)} %collective-permute-done.2.refs_4_), channel_id=1, source_target_pairs={{0,1},{1,3},{3,5},{5,7},{7,6},{6,4},{4,2},{2,0},{8,9},{9,11},{11,1... | collective-permute-start | bytes 1572872 | tf_op jit(solution)/shard_map/ppermute | solution.py:756
  58.1 16.9 %collective-permute-start.5 = (bf16[128,2048]{1,0:T(8,128)(2,1)S(1)}, bf16[128,2048]{1,0:T(8,128)(2,1)S(1)}, u32[]{:S(2)}, u32[]{:S(2)}) collective-permute-start(bf16[128,2048]{1,0:T(8,128)(2,1)S(1)} %collective-permute-done.3.refs_5_), channel_id=1, source_target_pairs={{0,2},{1,0},{3,1},{5,3},{7,5},{6,7},{4,6},{2,4},{8,10},{9,8},{11,9... | collective-permute-start | bytes 1572872 | tf_op jit(solution)/shard_map/ppermute | solution.py:756
  86.6 23.4 %collective-permute-start.10 = (bf16[128,2048]{1,0:T(8,128)(2,1)S(1)}, bf16[128,2048]{1,0:T(8,128)(2,1)S(1)}, u32[]{:S(2)}, u32[]{:S(2)}) collective-permute-start(bf16[128,2048]{1,0:T(8,128)(2,1)S(1)} %copy-done.19), channel_id=1, source_target_pairs={{0,1},{1,3},{3,5},{5,7},{7,6},{6,4},{4,2},{2,0},{8,9},{9,11},{11,1... | collective-permute-start | bytes 1572872 | tf_op jit(solution)/shard_map/ppermute | solution.py:756
  88.6 21.5 %collective-permute-start.11 = (bf16[128,2048]{1,0:T(8,128)(2,1)S(1)}, bf16[128,2048]{1,0:T(8,128)(2,1)S(1)}, u32[]{:S(2)}, u32[]{:S(2)}) collective-permute-start(bf16[128,2048]{1,0:T(8,128)(2,1)S(1)} %copy-done.19), channel_id=1, source_target_pairs={{0,2},{1,0},{3,1},{5,3},{7,5},{6,7},{4,6},{2,4},{8,10},{9,8},{11,9... | collective-permute-start | bytes 1572872 | tf_op jit(solution)/shard_map/ppermute | solution.py:756
  88.7 21.4 %collective-permute-start.14 = (bf16[128,2048]{1,0:T(8,128)(2,1)}, bf16[128,2048]{1,0:T(8,128)(2,1)}, u32[]{:S(2)}, u32[]{:S(2)}) collective-permute-start(bf16[128,2048]{1,0:T(8,128)(2,1)} %param.33), channel_id=1, source_target_pairs={{0,0},{1,8},{2,16},{3,24},{4,4},{5,12},{6,20},{7,28},{8,1},{9,9},{... | collective-permute-start | bytes 1572872 | tf_op jit(solution)/shard_map/ppermute | solution.py:999
  110.0 19.2 %collective-permute-start.15 = (bf16[128,2048]{1,0:T(8,128)(2,1)S(1)}, bf16[128,2048]{1,0:T(8,128)(2,1)S(1)}, u32[]{:S(2)}, u32[]{:S(2)}) collective-permute-start(bf16[128,2048]{1,0:T(8,128)(2,1)S(1)} %collective-permute-done.10.refs_2_), channel_id=1, source_target_pairs={{0,1},{1,3},{3,5},{5,7},{7,6},{6,4},{4,2},{2,0},{8,9},{9,11},{11,1... | collective-permute-start | bytes 1572872 | tf_op jit(solution)/shard_map/ppermute | solution.py:756
  110.1 19.2 %collective-permute-start.16 = (bf16[128,2048]{1,0:T(8,128)(2,1)S(1)}, bf16[128,2048]{1,0:T(8,128)(2,1)S(1)}, u32[]{:S(2)}, u32[]{:S(2)}) collective-permute-start(bf16[128,2048]{1,0:T(8,128)(2,1)S(1)} %collective-permute-done.11.refs_3_), channel_id=1, source_target_pairs={{0,2},{1,0},{3,1},{5,3},{7,5},{6,7},{4,6},{2,4},{8,10},{9,8},{11,9... | collective-permute-start | bytes 1572872 | tf_op jit(solution)/shard_map/ppermute | solution.py:756
  129.4 98.2 %all-gather.8.cloned.1.call-start = ((), (), s32[]{:S(2)}) async-start(), calls=%async_computation.7 | async-start | bytes 7864320 | tf_op jit(solution)/shard_map/all_gather | solution.py:1012
  283.5 39.2 %all-to-all-start.1 = ((f32[8,2,128]{2,1,0:T(2,128)}), f32[8,2,128]{2,1,0:T(2,128)S(1)}, u32[]{:S(2)}, u32[]{:S(2)}) async-start(f32[8,2,128]{2,1,0:T(2,128)} %broadcast_select_fusion.1), calls=%async_computation.1 | async-start | bytes 16384 | tf_op jit(solution)/shard_map/all_to_all | solution.py:1109
  287.1 238.5 %reduce-scatter.3.cloned.1.call-start = ((), (), s32[]{:S(2)}) async-start(), calls=%async_computation.8 | async-start | bytes 7864320 | tf_op jit(solution)/shard_map/reduce_scatter | solution.py:1133
  322.8 202.8 %reduce-scatter.5.cloned.1.call-start = ((), (), s32[]{:S(2)}) async-start(), calls=%async_computation.9 | async-start | bytes 7864320 | tf_op jit(solution)/shard_map/reduce_scatter | solution.py:1147
  325.5 16.8 %collective-permute-start.46 = (bf16[128,2048]{1,0:T(8,128)(2,1)}, bf16[128,2048]{1,0:T(8,128)(2,1)}, u32[]{:S(2)}, u32[]{:S(2)}) collective-permute-start(bf16[128,2048]{1,0:T(8,128)(2,1)} %get-tuple-element.588), channel_id=1, source_target_pairs={{0,1},{1,3},{3,5},{5,7},{7,6},{6,4},{4,2},{2,0},{8,9},{9,11},{11,1... | collective-permute-start | bytes 1572872 | tf_op jit(solution)/shard_map/ppermute | solution.py:756
  374.5 38.3 %collective-permute-start.58 = (bf16[64,2048]{1,0:T(8,128)(2,1)S(1)}, bf16[64,2048]{1,0:T(8,128)(2,1)S(1)}, u32[]{:S(2)}, u32[]{:S(2)}) collective-permute-start(bf16[64,2048]{1,0:T(8,128)(2,1)S(1)} %get-tuple-element.835), channel_id=1, source_target_pairs={{0,1},{1,3},{3,5},{5,7},{7,6},{6,4},{4,2},{2,0},{8,9},{9,11},{11,1... | collective-permute-start | bytes 786440 | tf_op jit(solution)/shard_map/ppermute | solution.py:756
  375.5 37.4 %collective-permute-start.59 = (bf16[64,2048]{1,0:T(8,128)(2,1)S(1)}, bf16[64,2048]{1,0:T(8,128)(2,1)S(1)}, u32[]{:S(2)}, u32[]{:S(2)}) collective-permute-start(bf16[64,2048]{1,0:T(8,128)(2,1)S(1)} %get-tuple-element.834), channel_id=1, source_target_pairs={{0,2},{1,0},{3,1},{5,3},{7,5},{6,7},{4,6},{2,4},{8,10},{9,8},{11,9... | collective-permute-start | bytes 786440 | tf_op jit(solution)/shard_map/ppermute | solution.py:756
  376.6 17.6 %collective-permute-start.52 = (bf16[128,2048]{1,0:T(8,128)(2,1)}, bf16[128,2048]{1,0:T(8,128)(2,1)S(1)}, u32[]{:S(2)}, u32[]{:S(2)}) collective-permute-start(bf16[128,2048]{1,0:T(8,128)(2,1)} %collective-permute-done.50.refs_3_.refs_5_), channel_id=1, source_target_pairs={{0,1},{1,3},{3,5},{5,7},{7,6},{6,4},{4,2},{2,0},{8,9},{9,11},{11,1... | collective-permute-start | bytes 1572872 | tf_op jit(solution)/shard_map/ppermute | solution.py:756
  377.5 17.2 %collective-permute-start.53 = (bf16[128,2048]{1,0:T(8,128)(2,1)}, bf16[128,2048]{1,0:T(8,128)(2,1)S(1)}, u32[]{:S(2)}, u32[]{:S(2)}) collective-permute-start(bf16[128,2048]{1,0:T(8,128)(2,1)} %collective-permute-done.51.refs_4_.refs_6_), channel_id=1, source_target_pairs={{0,2},{1,0},{3,1},{5,3},{7,5},{6,7},{4,6},{2,4},{8,10},{9,8},{11,9... | collective-permute-start | bytes 1572872 | tf_op jit(solution)/shard_map/ppermute | solution.py:756
  394.7 18.1 %collective-permute-start.56 = (bf16[64,2048]{1,0:T(8,128)(2,1)S(1)}, bf16[64,2048]{1,0:T(8,128)(2,1)S(1)}, u32[]{:S(2)}, u32[]{:S(2)}) collective-permute-start(bf16[64,2048]{1,0:T(8,128)(2,1)S(1)} %slice.246), channel_id=1, source_target_pairs={{0,1},{1,3},{3,5},{5,7},{7,6},{6,4},{4,2},{2,0},{8,9},{9,11},{11,1... | collective-permute-start | bytes 786440 | tf_op jit(solution)/shard_map/ppermute | solution.py:756
  450.5 22.8 %collective-permute-start.68 = (bf16[512,896]{1,0:T(8,128)(2,1)S(1)}, bf16[512,896]{1,0:T(8,128)(2,1)S(1)}, u32[]{:S(2)}, u32[]{:S(2)}) collective-permute-start(bf16[512,896]{1,0:T(8,128)(2,1)S(1)} %add_convert_fusion.3), channel_id=1, source_target_pairs={{0,16},{8,24},{16,0},{24,8},{1,17},{9,25},{17,1},{25,9},{2,18},{10... | collective-permute-start | bytes 2752520 | tf_op jit(solution)/shard_map/ppermute | solution.py:865
  474.5 51.1 %all-to-all-start.2 = ((bf16[8,64,896]{2,1,0:T(8,128)(2,1)}), bf16[8,64,896]{2,1,0:T(8,128)(2,1)S(1)}, u32[]{:S(2)}, u32[]{:S(2)}) async-start(bf16[8,64,896]{2,1,0:T(8,128)(2,1)} %bitcast.217), calls=%async_computation.2 | async-start | bytes 1835008 | tf_op jit(solution)/shard_map/all_to_all | solution.py:1238
  479.9 20.5 %collective-permute-start.73 = (bf16[128,2048]{1,0:T(8,128)(2,1)}, bf16[128,2048]{1,0:T(8,128)(2,1)S(1)}, u32[]{:S(2)}, u32[]{:S(2)}) collective-permute-start(bf16[128,2048]{1,0:T(8,128)(2,1)} %add_convert_fusion.7), channel_id=1, source_target_pairs={{0,16},{8,24},{16,0},{24,8},{1,17},{9,25},{17,1},{25,9},{2,18},{10... | collective-permute-start | bytes 1572872 | tf_op jit(solution)/shard_map/ppermute | solution.py:865
  480.2 19.4 %collective-permute-start.71 = (bf16[64,2048]{1,0:T(8,128)(2,1)}, bf16[64,2048]{1,0:T(8,128)(2,1)S(1)}, u32[]{:S(2)}, u32[]{:S(2)}) collective-permute-start(bf16[64,2048]{1,0:T(8,128)(2,1)} %copy-done.89), channel_id=1, source_target_pairs={{0,1},{1,3},{3,5},{5,7},{7,6},{6,4},{4,2},{2,0},{8,9},{9,11},{11,1... | collective-permute-start | bytes 786440 | tf_op jit(solution)/shard_map/ppermute | solution.py:756
  482.2 18.2 %collective-permute-start.72 = (bf16[64,2048]{1,0:T(8,128)(2,1)}, bf16[64,2048]{1,0:T(8,128)(2,1)S(1)}, u32[]{:S(2)}, u32[]{:S(2)}) collective-permute-start(bf16[64,2048]{1,0:T(8,128)(2,1)} %copy-done.88), channel_id=1, source_target_pairs={{0,2},{1,0},{3,1},{5,3},{7,5},{6,7},{4,6},{2,4},{8,10},{9,8},{11,9... | collective-permute-start | bytes 786440 | tf_op jit(solution)/shard_map/ppermute | solution.py:756
  503.7 21.9 %collective-permute-start.74 = (bf16[128,2048]{1,0:T(8,128)(2,1)}, bf16[128,2048]{1,0:T(8,128)(2,1)}, u32[]{:S(2)}, u32[]{:S(2)}) collective-permute-start(bf16[128,2048]{1,0:T(8,128)(2,1)} %get-tuple-element.726), channel_id=1, source_target_pairs={{0,1},{1,3},{3,5},{5,7},{7,6},{6,4},{4,2},{2,0},{8,9},{9,11},{11,1... | collective-permute-start | bytes 1572872 | tf_op jit(solution)/shard_map/ppermute | solution.py:756
  505.7 19.9 %collective-permute-start.75 = (bf16[128,2048]{1,0:T(8,128)(2,1)}, bf16[128,2048]{1,0:T(8,128)(2,1)}, u32[]{:S(2)}, u32[]{:S(2)}) collective-permute-start(bf16[128,2048]{1,0:T(8,128)(2,1)} %get-tuple-element.727), channel_id=1, source_target_pairs={{0,2},{1,0},{3,1},{5,3},{7,5},{6,7},{4,6},{2,4},{8,10},{9,8},{11,9... | collective-permute-start | bytes 1572872 | tf_op jit(solution)/shard_map/ppermute | solution.py:756
  519.8 49.6 %collective-permute-start.81 = (bf16[2,768,512]{2,1,0:T(8,128)(2,1)}, bf16[2,768,512]{2,1,0:T(8,128)(2,1)}, u32[]{:S(2)}, u32[]{:S(2)}) collective-permute-start(bf16[2,768,512]{2,1,0:T(8,128)(2,1)} %add_convert_fusion), channel_id=1, source_target_pairs={{0,16},{8,24},{16,0},{24,8},{1,17},{9,25},{17,1},{25,9},{2,18},{10... | collective-permute-start | bytes 4718600 | tf_op jit(solution)/shard_map/ppermute | solution.py:865
  530.2 23.9 %collective-permute-start.77 = (bf16[128,2048]{1,0:T(8,128)(2,1)}, bf16[128,2048]{1,0:T(8,128)(2,1)}, u32[]{:S(2)}, u32[]{:S(2)}) collective-permute-start(bf16[128,2048]{1,0:T(8,128)(2,1)} %get-tuple-element.741), channel_id=1, source_target_pairs={{0,1},{1,3},{3,5},{5,7},{7,6},{6,4},{4,2},{2,0},{8,9},{9,11},{11,1... | collective-permute-start | bytes 1572872 | tf_op jit(solution)/shard_map/ppermute | solution.py:756
  534.7 19.4 %collective-permute-start.78 = (bf16[128,2048]{1,0:T(8,128)(2,1)}, bf16[128,2048]{1,0:T(8,128)(2,1)}, u32[]{:S(2)}, u32[]{:S(2)}) collective-permute-start(bf16[128,2048]{1,0:T(8,128)(2,1)} %get-tuple-element.742), channel_id=1, source_target_pairs={{0,2},{1,0},{3,1},{5,3},{7,5},{6,7},{4,6},{2,4},{8,10},{9,8},{11,9... | collective-permute-start | bytes 1572872 | tf_op jit(solution)/shard_map/ppermute | solution.py:756
  (182 other events, 1825.8 us)
Sparse Core Ops, SparseCore 0:
  9.6 49.0 all-gather.3
  129.5 45.6 all-gather.5
  176.8 46.3 all-gather.7
  322.9 58.7 reduce-scatter.2
  384.3 58.3 reduce-scatter.4

commit v4 on v3

--- a/solution.py
+++ b/solution.py
@@ -1217,12 +1217,11 @@
             [layer_ring], grad_parts, grad_qkv, output_parts
         )
     paired = fsdp.pair(grad_parts)
+    paired, grad_qkv, output_parts = together(paired, grad_qkv, output_parts)
     sent = fsdp.send(paired)
     paired_output = fsdp.pair(output_parts)
     grad_hidden = rows_dot(grad_qkv, qkv_w, 1, tok_rows)
-    grad_hidden, paired, sent, paired_output = window(
-        [layer_ring], grad_hidden, paired, sent, paired_output
-    )
+    grad_hidden, paired_output = window([layer_ring], grad_hidden, paired_output)
     (produced, spot), left, right = layer_ring.landed()
     layer_out = (
         middle
@@ -1234,6 +1233,12 @@
     hidden_ring = Scatter(
         ring, lambda spot: (grad_hidden[spot], 0), tok_rows, tuple(grad_hidden[-2:])
     )
+    paired, sent, paired_output, paired_down = window(
+        [hidden_ring], paired, sent, paired_output, paired_down
+    )
+    paired, sent, paired_output, paired_down = prepare(
+        [hidden_ring], paired, sent, paired_output, paired_down
+    )
     total = paired[0].astype(F32) + sum(part.astype(F32) for part in sent)
     grad_qkv_w = lax.all_to_all(
         total.astype(BF16).reshape(groups, own_rows, qkv_width + head_size),
@@ -1243,31 +1248,39 @@
         tiled=True,
     )
     sent_output = fsdp.send(paired_output)
-    paired_output, sent_output, paired_down = window(
-        [hidden_ring], paired_output, sent_output, paired_down
-    )
-    paired_output, sent_output, paired_down = prepare(
-        [hidden_ring], paired_output, sent_output, paired_down
+    down_first = fsdp.send([part[:1] for part in paired_down])
+    paired_output, sent_output, paired_down, down_first, grad_qkv_w, grad_gate, grad_up = window(
+        [hidden_ring],
+        paired_output,
+        sent_output,
+        paired_down,
+        down_first,
+        grad_qkv_w,
+        grad_gate,
+        grad_up,
+    )
+    paired_output, sent_output, paired_down, grad_gate, grad_up = prepare(
+        [hidden_ring], paired_output, sent_output, paired_down, grad_gate, grad_up
     )
     total = paired_output[0].astype(F32) + sum(part.astype(F32) for part in sent_output)
     grad_output_w = lax.ppermute(total.astype(BF16), ALL, exchange)
-    sent_down = fsdp.send(paired_down)
-    grad_qkv_w, grad_output_w, grad_gate, grad_up = window(
-        [hidden_ring], grad_qkv_w, grad_output_w, grad_gate, grad_up
-    )
+    down_rest = fsdp.send([part[1:] for part in paired_down])
 
     def corner(array):
         return lax.slice(array, (0,) * array.ndim, (1,) * (array.ndim - 2) + (8, 128))
 
-    grad_gate, grad_up, grad_output_w = prepare([hidden_ring], grad_gate, grad_up, grad_output_w)
     grad_gate, grad_up = grad_gate.astype(F32), grad_up.astype(F32)
+    corners = [corner(array) for array in (grad_gate, grad_up, layer_out)]
+    for step in range(3, ring.steps):
+        grad_output_w, paired_down, corners = window(
+            [hidden_ring], grad_output_w, paired_down, corners
+        )
+    grad_output_w, paired_down = prepare([hidden_ring], grad_output_w, paired_down)
     grad_output_w = grad_output_w.astype(F32)
-    corners = [corner(array) for array in (grad_gate, grad_up, grad_output_w, layer_out)]
-    for step in range(3, ring.steps):
-        paired_down, corners = window([hidden_ring], paired_down, corners)
-    (paired_down,) = prepare([hidden_ring], paired_down)
-    grad_down = paired_down[0].astype(F32) + sum(part.astype(F32) for part in sent_down)
-    window([hidden_ring], [corner(grad_down)])
+    grad_down = paired_down[0].astype(F32) + sum(
+        jnp.concatenate(pair, axis=0).astype(F32) for pair in zip(down_first, down_rest)
+    )
+    window([hidden_ring], [corner(grad_down), corner(grad_output_w)])
     (grad_tokens,) = by_rows(
         tokens_back_kernel, hidden_ring.landed(), [tokens, grad_middle], [], [BF16]
     )

time: 593 us -> 580 us (0.978)
  starting transfers between devices: 127 us -> 117 us
    ppermute x32, starting transfers between devices: 55.5 us -> 47.4 us  [swap(): lax.ppermute(down, 'seq', self.down)]
    unnamed x259 -> x257, local copies, waits for them, and re-layouts: 39.4 us -> 36.2 us
    ppermute x6 -> x7, waiting for transfers between devices: 20.3 us -> 19 us  [shift(): return lax.ppermute(array, 'fsdp', perm)]
  transfers between devices with their start and end apart: 90 -> 91, of which waited for: 27 -> 30; matrix products, arithmetic and copies ran while one was open for 18% -> 19% of each run, Pallas kernels for 25% -> 25%
where the time goes in v4:
time: 580 us; the launch traced here: 569 us
  Pallas kernels  147 us (25%)
  waiting for transfers between devices  138 us (24%)
  starting transfers between devices  117 us (20%)
  local copies, waits for them, and re-layouts  59.4 us (10%)
  matrix products  55 us (9%)
  other arithmetic  36.4 us (6%)
  between operations  16.1 us (3%)
    ppermute x32, waiting for transfers between devices, swap(): lax.ppermute(up, 'seq', self.up)  106 us
    ppermute x32, starting transfers between devices, swap(): lax.ppermute(down, 'seq', self.down)  47.4 us
    unnamed x257, local copies, waits for them, and re-layouts  36.2 us
    ppermute x32, starting transfers between devices, swap(): lax.ppermute(up, 'seq', self.up)  32.5 us
    pallas_call x2, Pallas kernels, row_grads(): pl.pallas_call(row_grads_kernel, grid=(8,), in_specs=[pl.BlockSpec((part....  27.4 us
    pallas_call x2, Pallas kernels, attend_back(): pl.pallas_call(lambda *refs: attend_back_kernel(scale, len(pieces), first...  27.1 us
    ppermute x7, waiting for transfers between devices, shift(): return lax.ppermute(array, 'fsdp', perm)  19 us
    dot_general x2, matrix products, expert_part(): jnp.einsum('td,edf->etf', rows_in, up_w, preferred_element_type=F32)  14.1 us
  transfers between devices with their start and end apart: 91, of which 30 were waited for; matrix products, arithmetic and copies ran while one was open for 19% of the time, Pallas kernels for 25%

profile of v4, /device:TPU:0, one launch (start us, length us, event | category | flops | bytes accessed | tf_op | source)
XLA Modules:
  0.0 568.7 jit_solution(16023308710187959865)
XLA Ops:
  24.5 4.9 all-to-all-start
  32.2 24.4 %collective-permute-done.2.refs_4_ = bf16[128,2048]{1,0:T(8,128)(2,1)S(1)} collective-permute-done((bf16[128,2048]{1,0:T(8,128)(2,1)S(1)}, bf16[128,2048]{1,0:T(8,128)(2,1)S(1)}, u32[]{:S(2)}, u32[]{:S(2)}) %collective-permute-start.2) | collective-permute-done | bytes 524320 | tf_op jit(solution)/shard_map/ppermute | solution.py:756
  58.1 5.3 collective-permute-start.5
  68.4 5.2 collective-permute-done.6
  88.7 5.4 collective-permute-start.14
  96.2 13.8 %shard_map.299 = (bf16[1024,2048]{1,0:T(8,128)(2,1)}, f32[1024,640]{1,0:T(8,128)}, bf16[1024,512]{1,0:T(8,128)(2,1)}, bf16[1024,128]{1,0:T(8,128)(2,1)}, bf16[1024,128]{1,0:T(8,128)(2,1)}) custom-call(s32[4]{0:T(128)} %fusion.55.refs_0_.order_ref, bf16[128,2048]{1,0:T(8,128)(2,1)} %refs_1_.6, bf16[128,2048]{1,0:T(8,128)(2,1)} %copy-done.107, ...), custom_call_target="tpu_custom_call" | custom-call | flops 3221225472 | bytes 16777216 | tf_op jit(solution)/shard_map/pallas_call | solution.py:137
  110.1 4.7 collective-permute-start.16
  116.8 12.5 %shard_map.300 = (bf16[1024,512]{1,0:T(8,128)(2,1)}, bf16[1024,4096]{1,0:T(8,128)(2,1)}) custom-call(bf16[1024,512]{1,0:T(8,128)(2,1)} %get-tuple-element.447.refs_0_.refs_7_.refs_6_, bf16[1024,128]{1,0:T(8,128)(2,1)} %get-tuple-element.448.refs_1_.refs_8_.refs_7_, bf16[1024,128]{1,0:T(8,128)(2,1)} %get-tuple-element.449.refs_2_.refs_9_.refs_8_, ...), custom_call_target="tpu_custom_call" | custom-call | flops 2147483648 | bytes 12582912 | tf_op jit(solution)/shard_map/pallas_call | solution.py:573
  157.3 4.8 collective-permute-done.24.refs_8_
  200.3 9.9 %collective-permute-done.30.refs_2_ = bf16[128,2048]{1,0:T(8,128)(2,1)S(1)} collective-permute-done((bf16[128,2048]{1,0:T(8,128)(2,1)S(1)}, bf16[128,2048]{1,0:T(8,128)(2,1)S(1)}, u32[]{:S(2)}, u32[]{:S(2)}) %collective-permute-start.30) | collective-permute-done | bytes 524320 | tf_op jit(solution)/shard_map/ppermute | solution.py:756
  217.4 8.2 %collective-permute-done.32 = bf16[128,2048]{1,0:T(8,128)(2,1)S(1)} collective-permute-done((bf16[128,2048]{1,0:T(8,128)(2,1)S(1)}, bf16[128,2048]{1,0:T(8,128)(2,1)S(1)}, u32[]{:S(2)}, u32[]{:S(2)}) %collective-permute-start.32) | collective-permute-done | bytes 524320 | tf_op jit(solution)/shard_map/ppermute | solution.py:756
  229.6 10.1 %fusion.7 = f32[2,1024,768]{2,1,0:T(8,128)S(1)} fusion(bf16[2,768,2048]{2,1,0:T(8,128)(2,1)} %all-gather.8.cloned.1.call-done, bf16[1024,2048]{1,0:T(8,128)(2,1)} %copy-done.11), kind=kOutput, calls=%fused_computation.22 | convolution fusion | flops 6442450944 | bytes 16777216 | tf_op jit(solution)/shard_map/td,efd->etf/dot_general | solution.py:1083
  243.4 7.8 %fusion.21 = f32[2,640,768]{2,1,0:T(8,128)S(1)} fusion(bf16[2,2048,768]{2,1,0:T(8,128)(2,1)} %all-gather.4.cloned.1.call-done.first_w_ref, bf16[640,2048]{1,0:T(8,128)(2,1)} %constant_dynamic-update-slice_fusion.2.first_ref), kind=kOutput, calls=%fused_computation.42 | convolution fusion | flops 4026531840 | bytes 12845056 | tf_op jit(solution)/shard_map/td,edf->etf/dot_general | solution.py:1054
  256.6 9.5 %fusion.4 = (bf16[2,640,768]{2,1,0:T(8,128)(2,1)}, f32[2,640]{1,0:T(2,128)S(1)}, bf16[2,640,768]{2,1,0:T(8,128)(2,1)}, bf16[2,640,768]{2,1,0:T(8,128)(2,1)}) fusion(f32[2,640,768]{2,1,0:T(8,128)S(1)} %fusion.21, f32[2,1024,768]{2,1,0:T(8,128)S(1)} %fusion.7, f32[2,640]{1,0:T(2,128)S(1)} %bitcast.224, bf16[2,2048,768]{2,1,0:T(8,128)(2,1)S(1)} %bitcast.232, ...), kind=kOutput, calls=%fused_computation.10 | convolution fusion | flops 4045208320 | bytes 22685696 | tf_op jit(solution)/shard_map/td,edf->etf/dot_general | solution.py:1058
  269.6 4.6 multiply_reduce_fusion.1
  290.4 13.7 %shard_map.310 = (bf16[128,2048]{1,0:T(8,128)(2,1)}, bf16[128,2048]{1,0:T(8,128)(2,1)}, bf16[128,2048]{1,0:T(8,128)(2,1)}, bf16[128,2048]{1,0:T(8,128)(2,1)}, bf16[128,2048]{1,0:T(8,128)(2,1)}) custom-call(bf16[2,640,768]{2,1,0:T(8,128)(2,1)} %get-tuple-element.589.first_ref.refs_0_, bf16[2,640,768]{2,1,0:T(8,128)(2,1)} %get-tuple-element.610.second_ref.refs_0_, ...), custom_call_target="tpu_custom_call" | custom-call | flops 8053063680 | bytes 20971520 | tf_op jit(solution)/shard_map/pallas_call | solution.py:535
  309.6 13.2 %shard_map.312 = bf16[2,2048,768]{2,1,0:T(8,128)(2,1)} custom-call(bf16[640,2048]{1,0:T(8,128)(2,1)} %constant_dynamic-update-slice_fusion.2.first_ref, bf16[384,2048]{1,0:T(8,128)(2,1)} %copy-done.95, bf16[2,640,768]{2,1,0:T(8,128)(2,1)} %get-tuple-element.589.first_ref.refs_0_, bf16[2,384,768]{2,1,0:T(8,128)(2,1)} %copy-done.115), custom_call_target="tpu_custom_call" | custom-call | flops 6442450944 | bytes 25165824 | tf_op jit(solution)/shard_map/pallas_call | solution.py:422
  327.9 14.3 %shard_map.314 = bf16[2,2048,768]{2,1,0:T(8,128)(2,1)} custom-call(bf16[640,2048]{1,0:T(8,128)(2,1)} %constant_dynamic-update-slice_fusion.2.first_ref, bf16[384,2048]{1,0:T(8,128)(2,1)} %copy-done.95, bf16[2,640,768]{2,1,0:T(8,128)(2,1)} %get-tuple-element.610.second_ref.refs_0_, bf16[2,384,768]{2,1,0:T(8,128)(2,1)} %copy-done.116), custom_call_target="tpu_custom_call" | custom-call | flops 6442450944 | bytes 25165824 | tf_op jit(solution)/shard_map/pallas_call | solution.py:422
  349.3 7.6 %bitcast_convert_fusion.refs_0_.refs_1_ = bf16[640,2048]{1,0:T(8,128)(2,1)S(1)} fusion(bf16[2,640,768]{2,1,0:T(8,128)(2,1)S(1)} %copy-done.92, bf16[2,768,2048]{2,1,0:T(8,128)(2,1)} %all-gather.8.cloned.1.call-done), kind=kOutput, calls=%fused_computation.3 | convolution fusion | flops 4027842560 | bytes 10878976 | tf_op jit(solution)/shard_map/etf,efd->td/dot_general | solution.py:1160
  361.7 10.8 %shard_map.316 = (bf16[2,768,512]{2,1,0:T(8,128)(2,1)S(1)}, bf16[2,768,512]{2,1,0:T(8,128)(2,1)S(1)}, bf16[2,768,512]{2,1,0:T(8,128)(2,1)S(1)}, bf16[2,768,512]{2,1,0:T(8,128)(2,1)S(1)}) custom-call(s32[4]{0:T(128)S(1)} %copy-done.83, bf16[2,640,768]{2,1,0:T(8,128)(2,1)S(1)} %copy-done.92, bf16[2,384,768]{2,1,0:T(8,128)(2,1)S(1)} %copy-done.91, ...), custom_call_target="tpu_custom_call" | custom-call | flops 6442450944 | bytes 16777216 | tf_op jit(solution)/shard_map/pallas_call | solution.py:461
  382.2 12.0 %collective-permute-done.52.refs_0_.refs_7_ = bf16[128,2048]{1,0:T(8,128)(2,1)S(1)} collective-permute-done((bf16[128,2048]{1,0:T(8,128)(2,1)}, bf16[128,2048]{1,0:T(8,128)(2,1)S(1)}, u32[]{:S(2)}, u32[]{:S(2)}) %collective-permute-start.52) | collective-permute-done | bytes 524320 | tf_op jit(solution)/shard_map/ppermute | solution.py:756
  397.0 15.8 %shard_map.317 = (bf16[1024,768]{1,0:T(8,128)(2,1)S(1)}, f32[8,128]{1,0:T(8,128)S(1)}, f32[1024,128]{1,0:T(8,128)S(1)}, f32[1024,128]{1,0:T(8,128)S(1)}) custom-call(bf16[128,2048]{1,0:T(8,128)(2,1)S(1)} %get-tuple-element.684.refs_0_.refs_2_, bf16[128,2048]{1,0:T(8,128)(2,1)S(1)} %copy-done.43, bf16[128,2048]{1,0:T(8,128)(2,1)S(1)} %copy-done.45, ...), custom_call_target="tpu_custom_call" | custom-call | flops 4026531840 | bytes 15728640 | tf_op jit(solution)/shard_map/pallas_call | solution.py:690
  415.2 11.3 %shard_map.319 = (bf16[1024,768]{1,0:T(8,128)(2,1)S(1)}, f32[8,128]{1,0:T(8,128)S(1)}, f32[1024,128]{1,0:T(8,128)}, f32[1024,128]{1,0:T(8,128)}) custom-call(bf16[128,2048]{1,0:T(8,128)(2,1)S(1)} %collective-permute-done.52.refs_0_.refs_7_, bf16[128,2048]{1,0:T(8,128)(2,1)S(1)} %collective-permute-done.53.refs_1_.refs_8_, ...), custom_call_target="tpu_custom_call" | custom-call | flops 2415919104 | bytes 9437184 | tf_op jit(solution)/shard_map/pallas_call | solution.py:690
  429.0 5.5 shard_map.322
  436.7 5.5 shard_map.321
  450.4 4.6 shard_map.324
  464.4 5.4 collective-permute-done.70.refs_2_
  474.3 5.5 all-to-all-start.2
  486.6 21.5 %collective-permute-done.73.refs_2_ = bf16[128,2048]{1,0:T(8,128)(2,1)} collective-permute-done((bf16[128,2048]{1,0:T(8,128)(2,1)}, bf16[128,2048]{1,0:T(8,128)(2,1)}, u32[]{:S(2)}, u32[]{:S(2)}) %collective-permute-start.73) | collective-permute-done | bytes 524320 | tf_op jit(solution)/shard_map/ppermute | solution.py:756
  521.7 5.5 collective-permute-start.79
  539.7 5.5 collective-permute-start.81
  547.8 8.6 %collective-permute-done.82 = bf16[1,768,512]{2,1,0:T(8,128)(2,1)} collective-permute-done((bf16[1,768,512]{2,1,0:T(8,128)(2,1)}, bf16[1,768,512]{2,1,0:T(8,128)(2,1)}, u32[]{:S(2)}, u32[]{:S(2)}) %collective-permute-start.82) | collective-permute-done | bytes 786464 | tf_op jit(solution)/shard_map/ppermute | solution.py:865
  (575 shorter events, 255.4 us)
Async XLA Ops:
  7.2 139.5 %all-gather.4.cloned.1.call-start = ((), (), s32[]{:S(2)}) async-start(), calls=%async_computation.5 | async-start | bytes 7864320 | tf_op jit(solution)/shard_map/all_gather | solution.py:964
  24.5 32.1 %all-to-all-start = ((bf16[8,64,896]{2,1,0:T(8,128)(2,1)}), bf16[8,64,896]{2,1,0:T(8,128)(2,1)S(1)}, u32[]{:S(2)}, u32[]{:S(2)}) async-start(bf16[8,64,896]{2,1,0:T(8,128)(2,1)} %pad_maximum_fusion), calls=%async_computation | async-start | bytes 1835008 | tf_op jit(solution)/shard_map/all_to_all | solution.py:967
  29.4 182.3 %all-gather.6.cloned.1.call-start = ((), (), s32[]{:S(2)}) async-start(), calls=%async_computation.6 | async-start | bytes 7864320 | tf_op jit(solution)/shard_map/all_gather | solution.py:1007
  29.5 27.2 %collective-permute-start.2 = (bf16[128,2048]{1,0:T(8,128)(2,1)S(1)}, bf16[128,2048]{1,0:T(8,128)(2,1)S(1)}, u32[]{:S(2)}, u32[]{:S(2)}) collective-permute-start(bf16[128,2048]{1,0:T(8,128)(2,1)S(1)} %collective-permute-done.refs_2_), channel_id=1, source_target_pairs={{0,1},{1,3},{3,5},{5,7},{7,6},{6,4},{4,2},{2,0},{8,9},{9,11},{11,1... | collective-permute-start | bytes 1572872 | tf_op jit(solution)/shard_map/ppermute | solution.py:756
  31.4 25.2 %collective-permute-start.3 = (bf16[128,2048]{1,0:T(8,128)(2,1)S(1)}, bf16[128,2048]{1,0:T(8,128)(2,1)S(1)}, u32[]{:S(2)}, u32[]{:S(2)}) collective-permute-start(bf16[128,2048]{1,0:T(8,128)(2,1)S(1)} %collective-permute-done.1.refs_3_), channel_id=1, source_target_pairs={{0,2},{1,0},{3,1},{5,3},{7,5},{6,7},{4,6},{2,4},{8,10},{9,8},{11,9... | collective-permute-start | bytes 1572872 | tf_op jit(solution)/shard_map/ppermute | solution.py:756
  56.7 17.0 %collective-permute-start.4 = (bf16[128,2048]{1,0:T(8,128)(2,1)S(1)}, bf16[128,2048]{1,0:T(8,128)(2,1)S(1)}, u32[]{:S(2)}, u32[]{:S(2)}) collective-permute-start(bf16[128,2048]{1,0:T(8,128)(2,1)S(1)} %collective-permute-done.2.refs_4_), channel_id=1, source_target_pairs={{0,1},{1,3},{3,5},{5,7},{7,6},{6,4},{4,2},{2,0},{8,9},{9,11},{11,1... | collective-permute-start | bytes 1572872 | tf_op jit(solution)/shard_map/ppermute | solution.py:756
  58.1 16.9 %collective-permute-start.5 = (bf16[128,2048]{1,0:T(8,128)(2,1)S(1)}, bf16[128,2048]{1,0:T(8,128)(2,1)S(1)}, u32[]{:S(2)}, u32[]{:S(2)}) collective-permute-start(bf16[128,2048]{1,0:T(8,128)(2,1)S(1)} %collective-permute-done.3.refs_5_), channel_id=1, source_target_pairs={{0,2},{1,0},{3,1},{5,3},{7,5},{6,7},{4,6},{2,4},{8,10},{9,8},{11,9... | collective-permute-start | bytes 1572872 | tf_op jit(solution)/shard_map/ppermute | solution.py:756
  86.6 23.4 %collective-permute-start.10 = (bf16[128,2048]{1,0:T(8,128)(2,1)S(1)}, bf16[128,2048]{1,0:T(8,128)(2,1)S(1)}, u32[]{:S(2)}, u32[]{:S(2)}) collective-permute-start(bf16[128,2048]{1,0:T(8,128)(2,1)S(1)} %copy-done.19), channel_id=1, source_target_pairs={{0,1},{1,3},{3,5},{5,7},{7,6},{6,4},{4,2},{2,0},{8,9},{9,11},{11,1... | collective-permute-start | bytes 1572872 | tf_op jit(solution)/shard_map/ppermute | solution.py:756
  88.6 21.5 %collective-permute-start.11 = (bf16[128,2048]{1,0:T(8,128)(2,1)S(1)}, bf16[128,2048]{1,0:T(8,128)(2,1)S(1)}, u32[]{:S(2)}, u32[]{:S(2)}) collective-permute-start(bf16[128,2048]{1,0:T(8,128)(2,1)S(1)} %copy-done.19), channel_id=1, source_target_pairs={{0,2},{1,0},{3,1},{5,3},{7,5},{6,7},{4,6},{2,4},{8,10},{9,8},{11,9... | collective-permute-start | bytes 1572872 | tf_op jit(solution)/shard_map/ppermute | solution.py:756
  88.7 21.4 %collective-permute-start.14 = (bf16[128,2048]{1,0:T(8,128)(2,1)}, bf16[128,2048]{1,0:T(8,128)(2,1)}, u32[]{:S(2)}, u32[]{:S(2)}) collective-permute-start(bf16[128,2048]{1,0:T(8,128)(2,1)} %param.33), channel_id=1, source_target_pairs={{0,0},{1,8},{2,16},{3,24},{4,4},{5,12},{6,20},{7,28},{8,1},{9,9},{... | collective-permute-start | bytes 1572872 | tf_op jit(solution)/shard_map/ppermute | solution.py:999
  110.0 19.2 %collective-permute-start.15 = (bf16[128,2048]{1,0:T(8,128)(2,1)S(1)}, bf16[128,2048]{1,0:T(8,128)(2,1)S(1)}, u32[]{:S(2)}, u32[]{:S(2)}) collective-permute-start(bf16[128,2048]{1,0:T(8,128)(2,1)S(1)} %collective-permute-done.10.refs_2_), channel_id=1, source_target_pairs={{0,1},{1,3},{3,5},{5,7},{7,6},{6,4},{4,2},{2,0},{8,9},{9,11},{11,1... | collective-permute-start | bytes 1572872 | tf_op jit(solution)/shard_map/ppermute | solution.py:756
  110.1 19.2 %collective-permute-start.16 = (bf16[128,2048]{1,0:T(8,128)(2,1)S(1)}, bf16[128,2048]{1,0:T(8,128)(2,1)S(1)}, u32[]{:S(2)}, u32[]{:S(2)}) collective-permute-start(bf16[128,2048]{1,0:T(8,128)(2,1)S(1)} %collective-permute-done.11.refs_3_), channel_id=1, source_target_pairs={{0,2},{1,0},{3,1},{5,3},{7,5},{6,7},{4,6},{2,4},{8,10},{9,8},{11,9... | collective-permute-start | bytes 1572872 | tf_op jit(solution)/shard_map/ppermute | solution.py:756
  129.4 98.2 %all-gather.8.cloned.1.call-start = ((), (), s32[]{:S(2)}) async-start(), calls=%async_computation.7 | async-start | bytes 7864320 | tf_op jit(solution)/shard_map/all_gather | solution.py:1012
  283.5 39.2 %all-to-all-start.1 = ((f32[8,2,128]{2,1,0:T(2,128)}), f32[8,2,128]{2,1,0:T(2,128)S(1)}, u32[]{:S(2)}, u32[]{:S(2)}) async-start(f32[8,2,128]{2,1,0:T(2,128)} %broadcast_select_fusion.1), calls=%async_computation.1 | async-start | bytes 16384 | tf_op jit(solution)/shard_map/all_to_all | solution.py:1109
  287.1 225.2 %reduce-scatter.3.cloned.1.call-start = ((), (), s32[]{:S(2)}) async-start(), calls=%async_computation.8 | async-start | bytes 7864320 | tf_op jit(solution)/shard_map/reduce_scatter | solution.py:1133
  322.8 189.5 %reduce-scatter.5.cloned.1.call-start = ((), (), s32[]{:S(2)}) async-start(), calls=%async_computation.9 | async-start | bytes 7864320 | tf_op jit(solution)/shard_map/reduce_scatter | solution.py:1147
  374.5 38.3 %collective-permute-start.58 = (bf16[64,2048]{1,0:T(8,128)(2,1)S(1)}, bf16[64,2048]{1,0:T(8,128)(2,1)S(1)}, u32[]{:S(2)}, u32[]{:S(2)}) collective-permute-start(bf16[64,2048]{1,0:T(8,128)(2,1)S(1)} %get-tuple-element.871), channel_id=1, source_target_pairs={{0,1},{1,3},{3,5},{5,7},{7,6},{6,4},{4,2},{2,0},{8,9},{9,11},{11,1... | collective-permute-start | bytes 786440 | tf_op jit(solution)/shard_map/ppermute | solution.py:756
  375.5 37.3 %collective-permute-start.59 = (bf16[64,2048]{1,0:T(8,128)(2,1)S(1)}, bf16[64,2048]{1,0:T(8,128)(2,1)S(1)}, u32[]{:S(2)}, u32[]{:S(2)}) collective-permute-start(bf16[64,2048]{1,0:T(8,128)(2,1)S(1)} %get-tuple-element.870), channel_id=1, source_target_pairs={{0,2},{1,0},{3,1},{5,3},{7,5},{6,7},{4,6},{2,4},{8,10},{9,8},{11,9... | collective-permute-start | bytes 786440 | tf_op jit(solution)/shard_map/ppermute | solution.py:756
  376.6 17.6 %collective-permute-start.52 = (bf16[128,2048]{1,0:T(8,128)(2,1)}, bf16[128,2048]{1,0:T(8,128)(2,1)S(1)}, u32[]{:S(2)}, u32[]{:S(2)}) collective-permute-start(bf16[128,2048]{1,0:T(8,128)(2,1)} %collective-permute-done.50.refs_3_.refs_5_), channel_id=1, source_target_pairs={{0,1},{1,3},{3,5},{5,7},{7,6},{6,4},{4,2},{2,0},{8,9},{9,11},{11,1... | collective-permute-start | bytes 1572872 | tf_op jit(solution)/shard_map/ppermute | solution.py:756
  377.5 17.2 %collective-permute-start.53 = (bf16[128,2048]{1,0:T(8,128)(2,1)}, bf16[128,2048]{1,0:T(8,128)(2,1)S(1)}, u32[]{:S(2)}, u32[]{:S(2)}) collective-permute-start(bf16[128,2048]{1,0:T(8,128)(2,1)} %collective-permute-done.51.refs_4_.refs_6_), channel_id=1, source_target_pairs={{0,2},{1,0},{3,1},{5,3},{7,5},{6,7},{4,6},{2,4},{8,10},{9,8},{11,9... | collective-permute-start | bytes 1572872 | tf_op jit(solution)/shard_map/ppermute | solution.py:756
  394.7 18.1 %collective-permute-start.56 = (bf16[64,2048]{1,0:T(8,128)(2,1)S(1)}, bf16[64,2048]{1,0:T(8,128)(2,1)S(1)}, u32[]{:S(2)}, u32[]{:S(2)}) collective-permute-start(bf16[64,2048]{1,0:T(8,128)(2,1)S(1)} %slice.252), channel_id=1, source_target_pairs={{0,1},{1,3},{3,5},{5,7},{7,6},{6,4},{4,2},{2,0},{8,9},{9,11},{11,1... | collective-permute-start | bytes 786440 | tf_op jit(solution)/shard_map/ppermute | solution.py:756
  449.1 22.8 %collective-permute-start.72 = (bf16[512,896]{1,0:T(8,128)(2,1)S(1)}, bf16[512,896]{1,0:T(8,128)(2,1)S(1)}, u32[]{:S(2)}, u32[]{:S(2)}) collective-permute-start(bf16[512,896]{1,0:T(8,128)(2,1)S(1)} %add_convert_fusion.3), channel_id=1, source_target_pairs={{0,16},{8,24},{16,0},{24,8},{1,17},{9,25},{17,1},{25,9},{2,18},{10... | collective-permute-start | bytes 2752520 | tf_op jit(solution)/shard_map/ppermute | solution.py:865
  474.3 38.0 %all-to-all-start.2 = ((bf16[8,64,896]{2,1,0:T(8,128)(2,1)}), bf16[8,64,896]{2,1,0:T(8,128)(2,1)S(1)}, u32[]{:S(2)}, u32[]{:S(2)}) async-start(bf16[8,64,896]{2,1,0:T(8,128)(2,1)} %bitcast.217), calls=%async_computation.2 | async-start | bytes 1835008 | tf_op jit(solution)/shard_map/all_to_all | solution.py:1243
  481.8 30.4 %collective-permute-start.76 = (bf16[1,768,512]{2,1,0:T(8,128)(2,1)}, bf16[1,768,512]{2,1,0:T(8,128)(2,1)}, u32[]{:S(2)}, u32[]{:S(2)}) collective-permute-start(bf16[1,768,512]{2,1,0:T(8,128)(2,1)} %slice.256), channel_id=1, source_target_pairs={{0,16},{8,24},{16,0},{24,8},{1,17},{9,25},{17,1},{25,9},{2,18},{10... | collective-permute-start | bytes 2359304 | tf_op jit(solution)/shard_map/ppermute | solution.py:865
  482.1 26.0 %collective-permute-start.73 = (bf16[128,2048]{1,0:T(8,128)(2,1)}, bf16[128,2048]{1,0:T(8,128)(2,1)}, u32[]{:S(2)}, u32[]{:S(2)}) collective-permute-start(bf16[128,2048]{1,0:T(8,128)(2,1)} %copy-done.85), channel_id=1, source_target_pairs={{0,1},{1,3},{3,5},{5,7},{7,6},{6,4},{4,2},{2,0},{8,9},{9,11},{11,1... | collective-permute-start | bytes 1572872 | tf_op jit(solution)/shard_map/ppermute | solution.py:756
  484.1 24.0 %collective-permute-start.74 = (bf16[128,2048]{1,0:T(8,128)(2,1)}, bf16[128,2048]{1,0:T(8,128)(2,1)}, u32[]{:S(2)}, u32[]{:S(2)}) collective-permute-start(bf16[128,2048]{1,0:T(8,128)(2,1)} %copy-done.84), channel_id=1, source_target_pairs={{0,2},{1,0},{3,1},{5,3},{7,5},{6,7},{4,6},{2,4},{8,10},{9,8},{11,9... | collective-permute-start | bytes 1572872 | tf_op jit(solution)/shard_map/ppermute | solution.py:756
  484.1 28.1 %collective-permute-start.75 = (bf16[128,2048]{1,0:T(8,128)(2,1)}, bf16[128,2048]{1,0:T(8,128)(2,1)}, u32[]{:S(2)}, u32[]{:S(2)}) collective-permute-start(bf16[128,2048]{1,0:T(8,128)(2,1)} %add_convert_fusion.7), channel_id=1, source_target_pairs={{0,16},{8,24},{16,0},{24,8},{1,17},{9,25},{17,1},{25,9},{2,18},{10... | collective-permute-start | bytes 1572872 | tf_op jit(solution)/shard_map/ppermute | solution.py:865
  517.0 21.1 %collective-permute-start.77 = (bf16[128,2048]{1,0:T(8,128)(2,1)}, bf16[128,2048]{1,0:T(8,128)(2,1)}, u32[]{:S(2)}, u32[]{:S(2)}) collective-permute-start(bf16[128,2048]{1,0:T(8,128)(2,1)} %get-tuple-element.773), channel_id=1, source_target_pairs={{0,1},{1,3},{3,5},{5,7},{7,6},{6,4},{4,2},{2,0},{8,9},{9,11},{11,1... | collective-permute-start | bytes 1572872 | tf_op jit(solution)/shard_map/ppermute | solution.py:756
  518.8 19.3 %collective-permute-start.78 = (bf16[128,2048]{1,0:T(8,128)(2,1)}, bf16[128,2048]{1,0:T(8,128)(2,1)}, u32[]{:S(2)}, u32[]{:S(2)}) collective-permute-start(bf16[128,2048]{1,0:T(8,128)(2,1)} %get-tuple-element.774), channel_id=1, source_target_pairs={{0,2},{1,0},{3,1},{5,3},{7,5},{6,7},{4,6},{2,4},{8,10},{9,8},{11,9... | collective-permute-start | bytes 1572872 | tf_op jit(solution)/shard_map/ppermute | solution.py:756
  528.1 28.4 %collective-permute-start.82 = (bf16[1,768,512]{2,1,0:T(8,128)(2,1)}, bf16[1,768,512]{2,1,0:T(8,128)(2,1)}, u32[]{:S(2)}, u32[]{:S(2)}) collective-permute-start(bf16[1,768,512]{2,1,0:T(8,128)(2,1)} %slice.263), channel_id=1, source_target_pairs={{0,16},{8,24},{16,0},{24,8},{1,17},{9,25},{17,1},{25,9},{2,18},{10... | collective-permute-start | bytes 2359304 | tf_op jit(solution)/shard_map/ppermute | solution.py:865
  539.6 20.3 %collective-permute-start.80 = (bf16[128,2048]{1,0:T(8,128)(2,1)S(1)}, bf16[128,2048]{1,0:T(8,128)(2,1)S(1)}, u32[]{:S(2)}, u32[]{:S(2)}) collective-permute-start(bf16[128,2048]{1,0:T(8,128)(2,1)S(1)} %get-tuple-element.785), channel_id=1, source_target_pairs={{0,1},{1,3},{3,5},{5,7},{7,6},{6,4},{4,2},{2,0},{8,9},{9,11},{11,1... | collective-permute-start | bytes 1572872 | tf_op jit(solution)/shard_map/ppermute | solution.py:756
  539.7 20.3 %collective-permute-start.81 = (bf16[128,2048]{1,0:T(8,128)(2,1)S(1)}, bf16[128,2048]{1,0:T(8,128)(2,1)S(1)}, u32[]{:S(2)}, u32[]{:S(2)}) collective-permute-start(bf16[128,2048]{1,0:T(8,128)(2,1)S(1)} %get-tuple-element.786), channel_id=1, source_target_pairs={{0,2},{1,0},{3,1},{5,3},{7,5},{6,7},{4,6},{2,4},{8,10},{9,8},{11,9... | collective-permute-start | bytes 1572872 | tf_op jit(solution)/shard_map/ppermute | solution.py:756
  (182 other events, 1883.8 us)
Sparse Core Ops, SparseCore 0:
  9.6 49.0 all-gather.3
  129.5 45.6 all-gather.5
  176.8 46.3 all-gather.7
  322.9 58.7 reduce-scatter.2
  384.3 58.3 reduce-scatter.4

commit v5 on v4

--- a/solution.py
+++ b/solution.py
@@ -418,10 +418,10 @@
 def row_grads(rows, *grads):
     experts, _, ff = grads[0][0].shape
     depth = rows[0].shape[1]
-    block = depth // 8
+    block = depth // 4
     return pl.pallas_call(
         row_grads_kernel,
-        grid=(8,),
+        grid=(4,),
         in_specs=[pl.BlockSpec((part.shape[0], block), lambda i: (0, i)) for part in rows]
         + [pl.BlockSpec(part.shape, lambda i: (0, 0, 0)) for pair in grads for part in pair],
         out_specs=[pl.BlockSpec((experts, block, ff), lambda i: (0, i, 0))] * len(grads),
@@ -528,13 +528,13 @@
 def entered_rows(first, second, first_w, second_w, block):
     experts, rows, ff = first.shape
     depth = first_w.shape[1]
-    each = depth // 8
+    each = depth // 4
     whole = pl.BlockSpec(first.shape, lambda i: (0, 0, 0))
     weight = pl.BlockSpec((experts, each, ff), lambda i: (0, i, 0))
     shapes = split_shapes(rows, block, depth, False)
     return pl.pallas_call(
         entered_kernel,
-        grid=(8,),
+        grid=(4,),
         in_specs=[whole, whole, weight, weight],
         out_specs=[pl.BlockSpec((block, each), lambda i: (0, i))] * len(shapes),
         out_shape=shapes,

time: 580 us -> 577 us (level)
  transfers between devices with their start and end apart: 91 -> 91, of which waited for: 30 -> 31; matrix products, arithmetic and copies ran while one was open for 19% -> 19% of each run, Pallas kernels for 25% -> 25%
where the time goes in v5:
time: 577 us; the launch traced here: 566 us
  Pallas kernels  144 us (25%)
  waiting for transfers between devices  138 us (24%)
  starting transfers between devices  117 us (20%)
  local copies, waits for them, and re-layouts  59.4 us (10%)
  matrix products  55 us (10%)
  other arithmetic  36.4 us (6%)
  between operations  16 us (3%)
    ppermute x32, waiting for transfers between devices, swap(): lax.ppermute(up, 'seq', self.up)  106 us
    ppermute x32, starting transfers between devices, swap(): lax.ppermute(down, 'seq', self.down)  46.3 us
    unnamed x257, local copies, waits for them, and re-layouts  36.2 us
    ppermute x32, starting transfers between devices, swap(): lax.ppermute(up, 'seq', self.up)  34.4 us
    pallas_call x2, Pallas kernels, attend_back(): pl.pallas_call(lambda *refs: attend_back_kernel(scale, len(pieces), first...  27.1 us
    pallas_call x2, Pallas kernels, row_grads(): pl.pallas_call(row_grads_kernel, grid=(4,), in_specs=[pl.BlockSpec((part....  25.8 us
    ppermute x7, waiting for transfers between devices, shift(): return lax.ppermute(array, 'fsdp', perm)  18.1 us
    dot_general x2, matrix products, expert_part(): jnp.einsum('td,edf->etf', rows_in, up_w, preferred_element_type=F32)  14.1 us
  transfers between devices with their start and end apart: 91, of which 31 were waited for; matrix products, arithmetic and copies ran while one was open for 19% of the time, Pallas kernels for 25%

profile of v5, /device:TPU:0, one launch (start us, length us, event | category | flops | bytes accessed | tf_op | source)
XLA Modules:
  0.0 565.8 jit_solution(6362369613321577715)
XLA Ops:
  24.5 4.9 all-to-all-start
  32.2 24.4 %collective-permute-done.2.refs_4_ = bf16[128,2048]{1,0:T(8,128)(2,1)S(1)} collective-permute-done((bf16[128,2048]{1,0:T(8,128)(2,1)S(1)}, bf16[128,2048]{1,0:T(8,128)(2,1)S(1)}, u32[]{:S(2)}, u32[]{:S(2)}) %collective-permute-start.2) | collective-permute-done | bytes 524320 | tf_op jit(solution)/shard_map/ppermute | solution.py:756
  58.1 5.3 collective-permute-start.5
  68.4 5.2 collective-permute-done.6
  88.7 5.4 collective-permute-start.14
  96.2 13.8 %shard_map.299 = (bf16[1024,2048]{1,0:T(8,128)(2,1)}, f32[1024,640]{1,0:T(8,128)}, bf16[1024,512]{1,0:T(8,128)(2,1)}, bf16[1024,128]{1,0:T(8,128)(2,1)}, bf16[1024,128]{1,0:T(8,128)(2,1)}) custom-call(s32[4]{0:T(128)} %fusion.55.refs_0_.order_ref, bf16[128,2048]{1,0:T(8,128)(2,1)} %refs_1_.6, bf16[128,2048]{1,0:T(8,128)(2,1)} %copy-done.107, ...), custom_call_target="tpu_custom_call" | custom-call | flops 3221225472 | bytes 16777216 | tf_op jit(solution)/shard_map/pallas_call | solution.py:137
  110.1 4.7 collective-permute-start.16
  116.8 12.5 %shard_map.300 = (bf16[1024,512]{1,0:T(8,128)(2,1)}, bf16[1024,4096]{1,0:T(8,128)(2,1)}) custom-call(bf16[1024,512]{1,0:T(8,128)(2,1)} %get-tuple-element.447.refs_0_.refs_7_.refs_6_, bf16[1024,128]{1,0:T(8,128)(2,1)} %get-tuple-element.448.refs_1_.refs_8_.refs_7_, bf16[1024,128]{1,0:T(8,128)(2,1)} %get-tuple-element.449.refs_2_.refs_9_.refs_8_, ...), custom_call_target="tpu_custom_call" | custom-call | flops 2147483648 | bytes 12582912 | tf_op jit(solution)/shard_map/pallas_call | solution.py:573
  157.3 4.8 collective-permute-done.24.refs_8_
  200.3 9.9 %collective-permute-done.30.refs_2_ = bf16[128,2048]{1,0:T(8,128)(2,1)S(1)} collective-permute-done((bf16[128,2048]{1,0:T(8,128)(2,1)S(1)}, bf16[128,2048]{1,0:T(8,128)(2,1)S(1)}, u32[]{:S(2)}, u32[]{:S(2)}) %collective-permute-start.30) | collective-permute-done | bytes 524320 | tf_op jit(solution)/shard_map/ppermute | solution.py:756
  217.4 8.2 %collective-permute-done.32 = bf16[128,2048]{1,0:T(8,128)(2,1)S(1)} collective-permute-done((bf16[128,2048]{1,0:T(8,128)(2,1)S(1)}, bf16[128,2048]{1,0:T(8,128)(2,1)S(1)}, u32[]{:S(2)}, u32[]{:S(2)}) %collective-permute-start.32) | collective-permute-done | bytes 524320 | tf_op jit(solution)/shard_map/ppermute | solution.py:756
  229.6 10.1 %fusion.7 = f32[2,1024,768]{2,1,0:T(8,128)S(1)} fusion(bf16[2,768,2048]{2,1,0:T(8,128)(2,1)} %all-gather.8.cloned.1.call-done, bf16[1024,2048]{1,0:T(8,128)(2,1)} %copy-done.11), kind=kOutput, calls=%fused_computation.22 | convolution fusion | flops 6442450944 | bytes 16777216 | tf_op jit(solution)/shard_map/td,efd->etf/dot_general | solution.py:1083
  243.4 7.8 %fusion.21 = f32[2,640,768]{2,1,0:T(8,128)S(1)} fusion(bf16[2,2048,768]{2,1,0:T(8,128)(2,1)} %all-gather.4.cloned.1.call-done.first_w_ref, bf16[640,2048]{1,0:T(8,128)(2,1)} %constant_dynamic-update-slice_fusion.2.first_ref), kind=kOutput, calls=%fused_computation.42 | convolution fusion | flops 4026531840 | bytes 12845056 | tf_op jit(solution)/shard_map/td,edf->etf/dot_general | solution.py:1054
  256.6 9.5 %fusion.4 = (bf16[2,640,768]{2,1,0:T(8,128)(2,1)}, f32[2,640]{1,0:T(2,128)S(1)}, bf16[2,640,768]{2,1,0:T(8,128)(2,1)}, bf16[2,640,768]{2,1,0:T(8,128)(2,1)}) fusion(f32[2,640,768]{2,1,0:T(8,128)S(1)} %fusion.21, f32[2,1024,768]{2,1,0:T(8,128)S(1)} %fusion.7, f32[2,640]{1,0:T(2,128)S(1)} %bitcast.224, bf16[2,2048,768]{2,1,0:T(8,128)(2,1)S(1)} %bitcast.232, ...), kind=kOutput, calls=%fused_computation.10 | convolution fusion | flops 4045208320 | bytes 22685696 | tf_op jit(solution)/shard_map/td,edf->etf/dot_general | solution.py:1058
  269.6 4.6 multiply_reduce_fusion.1
  290.4 12.8 %shard_map.310 = (bf16[128,2048]{1,0:T(8,128)(2,1)}, bf16[128,2048]{1,0:T(8,128)(2,1)}, bf16[128,2048]{1,0:T(8,128)(2,1)}, bf16[128,2048]{1,0:T(8,128)(2,1)}, bf16[128,2048]{1,0:T(8,128)(2,1)}) custom-call(bf16[2,640,768]{2,1,0:T(8,128)(2,1)} %get-tuple-element.589.first_ref.refs_0_, bf16[2,640,768]{2,1,0:T(8,128)(2,1)} %get-tuple-element.610.second_ref.refs_0_, ...), custom_call_target="tpu_custom_call" | custom-call | flops 8053063680 | bytes 20971520 | tf_op jit(solution)/shard_map/pallas_call | solution.py:535
  308.7 12.5 %shard_map.312 = bf16[2,2048,768]{2,1,0:T(8,128)(2,1)} custom-call(bf16[640,2048]{1,0:T(8,128)(2,1)} %constant_dynamic-update-slice_fusion.2.first_ref, bf16[384,2048]{1,0:T(8,128)(2,1)} %copy-done.95, bf16[2,640,768]{2,1,0:T(8,128)(2,1)} %get-tuple-element.589.first_ref.refs_0_, bf16[2,384,768]{2,1,0:T(8,128)(2,1)} %copy-done.115), custom_call_target="tpu_custom_call" | custom-call | flops 6442450944 | bytes 25165824 | tf_op jit(solution)/shard_map/pallas_call | solution.py:422
  326.4 13.3 %shard_map.314 = bf16[2,2048,768]{2,1,0:T(8,128)(2,1)} custom-call(bf16[640,2048]{1,0:T(8,128)(2,1)} %constant_dynamic-update-slice_fusion.2.first_ref, bf16[384,2048]{1,0:T(8,128)(2,1)} %copy-done.95, bf16[2,640,768]{2,1,0:T(8,128)(2,1)} %get-tuple-element.610.second_ref.refs_0_, bf16[2,384,768]{2,1,0:T(8,128)(2,1)} %copy-done.116), custom_call_target="tpu_custom_call" | custom-call | flops 6442450944 | bytes 25165824 | tf_op jit(solution)/shard_map/pallas_call | solution.py:422
  346.5 7.6 %bitcast_convert_fusion.refs_0_.refs_1_ = bf16[640,2048]{1,0:T(8,128)(2,1)S(1)} fusion(bf16[2,640,768]{2,1,0:T(8,128)(2,1)S(1)} %copy-done.92, bf16[2,768,2048]{2,1,0:T(8,128)(2,1)} %all-gather.8.cloned.1.call-done), kind=kOutput, calls=%fused_computation.3 | convolution fusion | flops 4027842560 | bytes 10878976 | tf_op jit(solution)/shard_map/etf,efd->td/dot_general | solution.py:1160
  359.1 10.8 %shard_map.316 = (bf16[2,768,512]{2,1,0:T(8,128)(2,1)S(1)}, bf16[2,768,512]{2,1,0:T(8,128)(2,1)S(1)}, bf16[2,768,512]{2,1,0:T(8,128)(2,1)S(1)}, bf16[2,768,512]{2,1,0:T(8,128)(2,1)S(1)}) custom-call(s32[4]{0:T(128)S(1)} %copy-done.83, bf16[2,640,768]{2,1,0:T(8,128)(2,1)S(1)} %copy-done.92, bf16[2,384,768]{2,1,0:T(8,128)(2,1)S(1)} %copy-done.91, ...), custom_call_target="tpu_custom_call" | custom-call | flops 6442450944 | bytes 16777216 | tf_op jit(solution)/shard_map/pallas_call | solution.py:461
  379.4 12.2 %collective-permute-done.52.refs_0_.refs_7_ = bf16[128,2048]{1,0:T(8,128)(2,1)S(1)} collective-permute-done((bf16[128,2048]{1,0:T(8,128)(2,1)}, bf16[128,2048]{1,0:T(8,128)(2,1)S(1)}, u32[]{:S(2)}, u32[]{:S(2)}) %collective-permute-start.52) | collective-permute-done | bytes 524320 | tf_op jit(solution)/shard_map/ppermute | solution.py:756
  394.7 15.8 %shard_map.317 = (bf16[1024,768]{1,0:T(8,128)(2,1)S(1)}, f32[8,128]{1,0:T(8,128)S(1)}, f32[1024,128]{1,0:T(8,128)S(1)}, f32[1024,128]{1,0:T(8,128)S(1)}) custom-call(bf16[128,2048]{1,0:T(8,128)(2,1)S(1)} %get-tuple-element.684.refs_0_.refs_2_, bf16[128,2048]{1,0:T(8,128)(2,1)S(1)} %copy-done.43, bf16[128,2048]{1,0:T(8,128)(2,1)S(1)} %copy-done.45, ...), custom_call_target="tpu_custom_call" | custom-call | flops 4026531840 | bytes 15728640 | tf_op jit(solution)/shard_map/pallas_call | solution.py:690
  412.9 11.3 %shard_map.319 = (bf16[1024,768]{1,0:T(8,128)(2,1)S(1)}, f32[8,128]{1,0:T(8,128)S(1)}, f32[1024,128]{1,0:T(8,128)}, f32[1024,128]{1,0:T(8,128)}) custom-call(bf16[128,2048]{1,0:T(8,128)(2,1)S(1)} %collective-permute-done.52.refs_0_.refs_7_, bf16[128,2048]{1,0:T(8,128)(2,1)S(1)} %collective-permute-done.53.refs_1_.refs_8_, ...), custom_call_target="tpu_custom_call" | custom-call | flops 2415919104 | bytes 9437184 | tf_op jit(solution)/shard_map/pallas_call | solution.py:690
  427.2 5.5 shard_map.322
  434.9 5.5 shard_map.321
  448.4 4.6 shard_map.324
  462.5 5.4 collective-permute-done.70.refs_2_
  472.3 4.5 all-to-all-start.2
  483.7 21.5 %collective-permute-done.73.refs_2_ = bf16[128,2048]{1,0:T(8,128)(2,1)} collective-permute-done((bf16[128,2048]{1,0:T(8,128)(2,1)}, bf16[128,2048]{1,0:T(8,128)(2,1)}, u32[]{:S(2)}, u32[]{:S(2)}) %collective-permute-start.73) | collective-permute-done | bytes 524320 | tf_op jit(solution)/shard_map/ppermute | solution.py:756
  518.7 5.5 collective-permute-start.79
  536.8 6.3 %collective-permute-start.81 = (bf16[128,2048]{1,0:T(8,128)(2,1)S(1)}, bf16[128,2048]{1,0:T(8,128)(2,1)S(1)}, u32[]{:S(2)}, u32[]{:S(2)}) collective-permute-start(bf16[128,2048]{1,0:T(8,128)(2,1)S(1)} %get-tuple-element.786), channel_id=1, source_target_pairs={{0,2},{1,0},{3,1},{5,3},{7,5},{6,7},{4,6},{2,4},{8,10},{9,8},{11,9... | collective-permute-start | bytes 1572872 | tf_op jit(solution)/shard_map/ppermute | solution.py:756
  545.7 7.9 %collective-permute-done.82 = bf16[1,768,512]{2,1,0:T(8,128)(2,1)} collective-permute-done((bf16[1,768,512]{2,1,0:T(8,128)(2,1)}, bf16[1,768,512]{2,1,0:T(8,128)(2,1)}, u32[]{:S(2)}, u32[]{:S(2)}) %collective-permute-start.82) | collective-permute-done | bytes 786464 | tf_op jit(solution)/shard_map/ppermute | solution.py:865
  (575 shorter events, 255.7 us)
Async XLA Ops:
  7.2 139.5 %all-gather.4.cloned.1.call-start = ((), (), s32[]{:S(2)}) async-start(), calls=%async_computation.5 | async-start | bytes 7864320 | tf_op jit(solution)/shard_map/all_gather | solution.py:964
  24.5 32.1 %all-to-all-start = ((bf16[8,64,896]{2,1,0:T(8,128)(2,1)}), bf16[8,64,896]{2,1,0:T(8,128)(2,1)S(1)}, u32[]{:S(2)}, u32[]{:S(2)}) async-start(bf16[8,64,896]{2,1,0:T(8,128)(2,1)} %pad_maximum_fusion), calls=%async_computation | async-start | bytes 1835008 | tf_op jit(solution)/shard_map/all_to_all | solution.py:967
  29.4 182.3 %all-gather.6.cloned.1.call-start = ((), (), s32[]{:S(2)}) async-start(), calls=%async_computation.6 | async-start | bytes 7864320 | tf_op jit(solution)/shard_map/all_gather | solution.py:1007
  29.5 27.2 %collective-permute-start.2 = (bf16[128,2048]{1,0:T(8,128)(2,1)S(1)}, bf16[128,2048]{1,0:T(8,128)(2,1)S(1)}, u32[]{:S(2)}, u32[]{:S(2)}) collective-permute-start(bf16[128,2048]{1,0:T(8,128)(2,1)S(1)} %collective-permute-done.refs_2_), channel_id=1, source_target_pairs={{0,1},{1,3},{3,5},{5,7},{7,6},{6,4},{4,2},{2,0},{8,9},{9,11},{11,1... | collective-permute-start | bytes 1572872 | tf_op jit(solution)/shard_map/ppermute | solution.py:756
  31.4 25.2 %collective-permute-start.3 = (bf16[128,2048]{1,0:T(8,128)(2,1)S(1)}, bf16[128,2048]{1,0:T(8,128)(2,1)S(1)}, u32[]{:S(2)}, u32[]{:S(2)}) collective-permute-start(bf16[128,2048]{1,0:T(8,128)(2,1)S(1)} %collective-permute-done.1.refs_3_), channel_id=1, source_target_pairs={{0,2},{1,0},{3,1},{5,3},{7,5},{6,7},{4,6},{2,4},{8,10},{9,8},{11,9... | collective-permute-start | bytes 1572872 | tf_op jit(solution)/shard_map/ppermute | solution.py:756
  56.7 17.0 %collective-permute-start.4 = (bf16[128,2048]{1,0:T(8,128)(2,1)S(1)}, bf16[128,2048]{1,0:T(8,128)(2,1)S(1)}, u32[]{:S(2)}, u32[]{:S(2)}) collective-permute-start(bf16[128,2048]{1,0:T(8,128)(2,1)S(1)} %collective-permute-done.2.refs_4_), channel_id=1, source_target_pairs={{0,1},{1,3},{3,5},{5,7},{7,6},{6,4},{4,2},{2,0},{8,9},{9,11},{11,1... | collective-permute-start | bytes 1572872 | tf_op jit(solution)/shard_map/ppermute | solution.py:756
  58.1 16.9 %collective-permute-start.5 = (bf16[128,2048]{1,0:T(8,128)(2,1)S(1)}, bf16[128,2048]{1,0:T(8,128)(2,1)S(1)}, u32[]{:S(2)}, u32[]{:S(2)}) collective-permute-start(bf16[128,2048]{1,0:T(8,128)(2,1)S(1)} %collective-permute-done.3.refs_5_), channel_id=1, source_target_pairs={{0,2},{1,0},{3,1},{5,3},{7,5},{6,7},{4,6},{2,4},{8,10},{9,8},{11,9... | collective-permute-start | bytes 1572872 | tf_op jit(solution)/shard_map/ppermute | solution.py:756
  86.6 23.4 %collective-permute-start.10 = (bf16[128,2048]{1,0:T(8,128)(2,1)S(1)}, bf16[128,2048]{1,0:T(8,128)(2,1)S(1)}, u32[]{:S(2)}, u32[]{:S(2)}) collective-permute-start(bf16[128,2048]{1,0:T(8,128)(2,1)S(1)} %copy-done.19), channel_id=1, source_target_pairs={{0,1},{1,3},{3,5},{5,7},{7,6},{6,4},{4,2},{2,0},{8,9},{9,11},{11,1... | collective-permute-start | bytes 1572872 | tf_op jit(solution)/shard_map/ppermute | solution.py:756
  88.6 21.5 %collective-permute-start.11 = (bf16[128,2048]{1,0:T(8,128)(2,1)S(1)}, bf16[128,2048]{1,0:T(8,128)(2,1)S(1)}, u32[]{:S(2)}, u32[]{:S(2)}) collective-permute-start(bf16[128,2048]{1,0:T(8,128)(2,1)S(1)} %copy-done.19), channel_id=1, source_target_pairs={{0,2},{1,0},{3,1},{5,3},{7,5},{6,7},{4,6},{2,4},{8,10},{9,8},{11,9... | collective-permute-start | bytes 1572872 | tf_op jit(solution)/shard_map/ppermute | solution.py:756
  88.7 21.4 %collective-permute-start.14 = (bf16[128,2048]{1,0:T(8,128)(2,1)}, bf16[128,2048]{1,0:T(8,128)(2,1)}, u32[]{:S(2)}, u32[]{:S(2)}) collective-permute-start(bf16[128,2048]{1,0:T(8,128)(2,1)} %param.33), channel_id=1, source_target_pairs={{0,0},{1,8},{2,16},{3,24},{4,4},{5,12},{6,20},{7,28},{8,1},{9,9},{... | collective-permute-start | bytes 1572872 | tf_op jit(solution)/shard_map/ppermute | solution.py:999
  110.0 19.2 %collective-permute-start.15 = (bf16[128,2048]{1,0:T(8,128)(2,1)S(1)}, bf16[128,2048]{1,0:T(8,128)(2,1)S(1)}, u32[]{:S(2)}, u32[]{:S(2)}) collective-permute-start(bf16[128,2048]{1,0:T(8,128)(2,1)S(1)} %collective-permute-done.10.refs_2_), channel_id=1, source_target_pairs={{0,1},{1,3},{3,5},{5,7},{7,6},{6,4},{4,2},{2,0},{8,9},{9,11},{11,1... | collective-permute-start | bytes 1572872 | tf_op jit(solution)/shard_map/ppermute | solution.py:756
  110.1 19.2 %collective-permute-start.16 = (bf16[128,2048]{1,0:T(8,128)(2,1)S(1)}, bf16[128,2048]{1,0:T(8,128)(2,1)S(1)}, u32[]{:S(2)}, u32[]{:S(2)}) collective-permute-start(bf16[128,2048]{1,0:T(8,128)(2,1)S(1)} %collective-permute-done.11.refs_3_), channel_id=1, source_target_pairs={{0,2},{1,0},{3,1},{5,3},{7,5},{6,7},{4,6},{2,4},{8,10},{9,8},{11,9... | collective-permute-start | bytes 1572872 | tf_op jit(solution)/shard_map/ppermute | solution.py:756
  129.4 98.2 %all-gather.8.cloned.1.call-start = ((), (), s32[]{:S(2)}) async-start(), calls=%async_computation.7 | async-start | bytes 7864320 | tf_op jit(solution)/shard_map/all_gather | solution.py:1012
  283.5 37.7 %all-to-all-start.1 = ((f32[8,2,128]{2,1,0:T(2,128)}), f32[8,2,128]{2,1,0:T(2,128)S(1)}, u32[]{:S(2)}, u32[]{:S(2)}) async-start(f32[8,2,128]{2,1,0:T(2,128)} %broadcast_select_fusion.1), calls=%async_computation.1 | async-start | bytes 16384 | tf_op jit(solution)/shard_map/all_to_all | solution.py:1109
  287.1 222.3 %reduce-scatter.3.cloned.1.call-start = ((), (), s32[]{:S(2)}) async-start(), calls=%async_computation.8 | async-start | bytes 7864320 | tf_op jit(solution)/shard_map/reduce_scatter | solution.py:1133
  321.2 188.1 %reduce-scatter.5.cloned.1.call-start = ((), (), s32[]{:S(2)}) async-start(), calls=%async_computation.9 | async-start | bytes 7864320 | tf_op jit(solution)/shard_map/reduce_scatter | solution.py:1147
  371.9 38.6 %collective-permute-start.58 = (bf16[64,2048]{1,0:T(8,128)(2,1)S(1)}, bf16[64,2048]{1,0:T(8,128)(2,1)S(1)}, u32[]{:S(2)}, u32[]{:S(2)}) collective-permute-start(bf16[64,2048]{1,0:T(8,128)(2,1)S(1)} %get-tuple-element.871), channel_id=1, source_target_pairs={{0,1},{1,3},{3,5},{5,7},{7,6},{6,4},{4,2},{2,0},{8,9},{9,11},{11,1... | collective-permute-start | bytes 786440 | tf_op jit(solution)/shard_map/ppermute | solution.py:756
  373.2 37.3 %collective-permute-start.59 = (bf16[64,2048]{1,0:T(8,128)(2,1)S(1)}, bf16[64,2048]{1,0:T(8,128)(2,1)S(1)}, u32[]{:S(2)}, u32[]{:S(2)}) collective-permute-start(bf16[64,2048]{1,0:T(8,128)(2,1)S(1)} %get-tuple-element.870), channel_id=1, source_target_pairs={{0,2},{1,0},{3,1},{5,3},{7,5},{6,7},{4,6},{2,4},{8,10},{9,8},{11,9... | collective-permute-start | bytes 786440 | tf_op jit(solution)/shard_map/ppermute | solution.py:756
  374.0 17.6 %collective-permute-start.52 = (bf16[128,2048]{1,0:T(8,128)(2,1)}, bf16[128,2048]{1,0:T(8,128)(2,1)S(1)}, u32[]{:S(2)}, u32[]{:S(2)}) collective-permute-start(bf16[128,2048]{1,0:T(8,128)(2,1)} %collective-permute-done.50.refs_3_.refs_5_), channel_id=1, source_target_pairs={{0,1},{1,3},{3,5},{5,7},{7,6},{6,4},{4,2},{2,0},{8,9},{9,11},{11,1... | collective-permute-start | bytes 1572872 | tf_op jit(solution)/shard_map/ppermute | solution.py:756
  375.2 17.2 %collective-permute-start.53 = (bf16[128,2048]{1,0:T(8,128)(2,1)}, bf16[128,2048]{1,0:T(8,128)(2,1)S(1)}, u32[]{:S(2)}, u32[]{:S(2)}) collective-permute-start(bf16[128,2048]{1,0:T(8,128)(2,1)} %collective-permute-done.51.refs_4_.refs_6_), channel_id=1, source_target_pairs={{0,2},{1,0},{3,1},{5,3},{7,5},{6,7},{4,6},{2,4},{8,10},{9,8},{11,9... | collective-permute-start | bytes 1572872 | tf_op jit(solution)/shard_map/ppermute | solution.py:756
  392.5 18.1 %collective-permute-start.56 = (bf16[64,2048]{1,0:T(8,128)(2,1)S(1)}, bf16[64,2048]{1,0:T(8,128)(2,1)S(1)}, u32[]{:S(2)}, u32[]{:S(2)}) collective-permute-start(bf16[64,2048]{1,0:T(8,128)(2,1)S(1)} %slice.252), channel_id=1, source_target_pairs={{0,1},{1,3},{3,5},{5,7},{7,6},{6,4},{4,2},{2,0},{8,9},{9,11},{11,1... | collective-permute-start | bytes 786440 | tf_op jit(solution)/shard_map/ppermute | solution.py:756
  447.1 22.8 %collective-permute-start.72 = (bf16[512,896]{1,0:T(8,128)(2,1)S(1)}, bf16[512,896]{1,0:T(8,128)(2,1)S(1)}, u32[]{:S(2)}, u32[]{:S(2)}) collective-permute-start(bf16[512,896]{1,0:T(8,128)(2,1)S(1)} %add_convert_fusion.3), channel_id=1, source_target_pairs={{0,16},{8,24},{16,0},{24,8},{1,17},{9,25},{17,1},{25,9},{2,18},{10... | collective-permute-start | bytes 2752520 | tf_op jit(solution)/shard_map/ppermute | solution.py:865
  472.3 37.1 %all-to-all-start.2 = ((bf16[8,64,896]{2,1,0:T(8,128)(2,1)}), bf16[8,64,896]{2,1,0:T(8,128)(2,1)S(1)}, u32[]{:S(2)}, u32[]{:S(2)}) async-start(bf16[8,64,896]{2,1,0:T(8,128)(2,1)} %bitcast.217), calls=%async_computation.2 | async-start | bytes 1835008 | tf_op jit(solution)/shard_map/all_to_all | solution.py:1243
  478.9 30.4 %collective-permute-start.76 = (bf16[1,768,512]{2,1,0:T(8,128)(2,1)}, bf16[1,768,512]{2,1,0:T(8,128)(2,1)}, u32[]{:S(2)}, u32[]{:S(2)}) collective-permute-start(bf16[1,768,512]{2,1,0:T(8,128)(2,1)} %slice.256), channel_id=1, source_target_pairs={{0,16},{8,24},{16,0},{24,8},{1,17},{9,25},{17,1},{25,9},{2,18},{10... | collective-permute-start | bytes 2359304 | tf_op jit(solution)/shard_map/ppermute | solution.py:865
  480.1 25.1 %collective-permute-start.73 = (bf16[128,2048]{1,0:T(8,128)(2,1)}, bf16[128,2048]{1,0:T(8,128)(2,1)}, u32[]{:S(2)}, u32[]{:S(2)}) collective-permute-start(bf16[128,2048]{1,0:T(8,128)(2,1)} %copy-done.85), channel_id=1, source_target_pairs={{0,1},{1,3},{3,5},{5,7},{7,6},{6,4},{4,2},{2,0},{8,9},{9,11},{11,1... | collective-permute-start | bytes 1572872 | tf_op jit(solution)/shard_map/ppermute | solution.py:756
  482.1 23.1 %collective-permute-start.74 = (bf16[128,2048]{1,0:T(8,128)(2,1)}, bf16[128,2048]{1,0:T(8,128)(2,1)}, u32[]{:S(2)}, u32[]{:S(2)}) collective-permute-start(bf16[128,2048]{1,0:T(8,128)(2,1)} %copy-done.84), channel_id=1, source_target_pairs={{0,2},{1,0},{3,1},{5,3},{7,5},{6,7},{4,6},{2,4},{8,10},{9,8},{11,9... | collective-permute-start | bytes 1572872 | tf_op jit(solution)/shard_map/ppermute | solution.py:756
  482.1 27.3 %collective-permute-start.75 = (bf16[128,2048]{1,0:T(8,128)(2,1)}, bf16[128,2048]{1,0:T(8,128)(2,1)}, u32[]{:S(2)}, u32[]{:S(2)}) collective-permute-start(bf16[128,2048]{1,0:T(8,128)(2,1)} %add_convert_fusion.7), channel_id=1, source_target_pairs={{0,16},{8,24},{16,0},{24,8},{1,17},{9,25},{17,1},{25,9},{2,18},{10... | collective-permute-start | bytes 1572872 | tf_op jit(solution)/shard_map/ppermute | solution.py:865
  514.0 21.1 %collective-permute-start.77 = (bf16[128,2048]{1,0:T(8,128)(2,1)}, bf16[128,2048]{1,0:T(8,128)(2,1)}, u32[]{:S(2)}, u32[]{:S(2)}) collective-permute-start(bf16[128,2048]{1,0:T(8,128)(2,1)} %get-tuple-element.773), channel_id=1, source_target_pairs={{0,1},{1,3},{3,5},{5,7},{7,6},{6,4},{4,2},{2,0},{8,9},{9,11},{11,1... | collective-permute-start | bytes 1572872 | tf_op jit(solution)/shard_map/ppermute | solution.py:756
  515.8 19.3 %collective-permute-start.78 = (bf16[128,2048]{1,0:T(8,128)(2,1)}, bf16[128,2048]{1,0:T(8,128)(2,1)}, u32[]{:S(2)}, u32[]{:S(2)}) collective-permute-start(bf16[128,2048]{1,0:T(8,128)(2,1)} %get-tuple-element.774), channel_id=1, source_target_pairs={{0,2},{1,0},{3,1},{5,3},{7,5},{6,7},{4,6},{2,4},{8,10},{9,8},{11,9... | collective-permute-start | bytes 1572872 | tf_op jit(solution)/shard_map/ppermute | solution.py:756
  525.1 28.4 %collective-permute-start.82 = (bf16[1,768,512]{2,1,0:T(8,128)(2,1)}, bf16[1,768,512]{2,1,0:T(8,128)(2,1)}, u32[]{:S(2)}, u32[]{:S(2)}) collective-permute-start(bf16[1,768,512]{2,1,0:T(8,128)(2,1)} %slice.263), channel_id=1, source_target_pairs={{0,16},{8,24},{16,0},{24,8},{1,17},{9,25},{17,1},{25,9},{2,18},{10... | collective-permute-start | bytes 2359304 | tf_op jit(solution)/shard_map/ppermute | solution.py:865
  536.7 20.3 %collective-permute-start.80 = (bf16[128,2048]{1,0:T(8,128)(2,1)S(1)}, bf16[128,2048]{1,0:T(8,128)(2,1)S(1)}, u32[]{:S(2)}, u32[]{:S(2)}) collective-permute-start(bf16[128,2048]{1,0:T(8,128)(2,1)S(1)} %get-tuple-element.785), channel_id=1, source_target_pairs={{0,1},{1,3},{3,5},{5,7},{7,6},{6,4},{4,2},{2,0},{8,9},{9,11},{11,1... | collective-permute-start | bytes 1572872 | tf_op jit(solution)/shard_map/ppermute | solution.py:756
  536.8 20.3 %collective-permute-start.81 = (bf16[128,2048]{1,0:T(8,128)(2,1)S(1)}, bf16[128,2048]{1,0:T(8,128)(2,1)S(1)}, u32[]{:S(2)}, u32[]{:S(2)}) collective-permute-start(bf16[128,2048]{1,0:T(8,128)(2,1)S(1)} %get-tuple-element.786), channel_id=1, source_target_pairs={{0,2},{1,0},{3,1},{5,3},{7,5},{6,7},{4,6},{2,4},{8,10},{9,8},{11,9... | collective-permute-start | bytes 1572872 | tf_op jit(solution)/shard_map/ppermute | solution.py:756
  (182 other events, 1881.4 us)
Sparse Core Ops, SparseCore 0:
  9.6 49.0 all-gather.3
  129.5 45.6 all-gather.5
  176.8 46.3 all-gather.7
  321.4 58.7 reduce-scatter.2
  382.7 58.3 reduce-scatter.4
